TPU v7x, 32 devices: a whole 2x2x4 slice. The times are simulated.
32 devices in a mesh: role: 4 (over y, core), seq: 2 (over x), mp: 4 (over z).
Axes of the slice: x: 2, y: 2, z: 4, core: 2. Of those that a mesh axis runs over, the one named last changes fastest.
Arguments:
- gen_heads: bfloat16 [128, 4096], P(None, 'seq'), may hold values from -6 to 6
- gen_resid: bfloat16 [128, 5120], P('seq', 'mp'), may hold values from -6 to 6
- gen_out_w: bfloat16 [4096, 5120], P('seq', 'mp'), may hold values from -0.09375 to 0.09375
- gen_time_w: bfloat16 [256, 5120], P(None, 'mp'), may hold values from -0.375 to 0.375
- noise: bfloat16 [128, 5120], P('seq', 'mp'), may hold values from -6 to 6
- steps: int32 [3], replicated, may hold values from 20 to 979
- teacher_qkv: bfloat16 [5120, 3, 4096], P('mp', None, 'seq'), may hold values from -0.078125 to 0.078125
- teacher_out: bfloat16 [4096, 5120], P('seq', 'mp'), may hold values from -0.09375 to 0.09375
- teacher_time: bfloat16 [256, 3, 5120], P(None, None, 'mp'), may hold values from -0.375 to 0.375
- teacher_norm: float32 [2, 4096], P(None, 'seq'), may hold values from 0.5 to 1.5
- critic_qkv: bfloat16 [5120, 3, 4096], P('mp', None, 'seq'), may hold values from -0.078125 to 0.078125
- critic_out: bfloat16 [4096, 5120], P('seq', 'mp'), may hold values from -0.09375 to 0.09375
- critic_time: bfloat16 [256, 3, 5120], P(None, None, 'mp'), may hold values from -0.375 to 0.375
- critic_norm: float32 [2, 4096], P(None, 'seq'), may hold values from 0.5 to 1.5
Outputs:
- latent: bfloat16 [128, 5120], P('seq', 'mp')
- weight_grad: bfloat16 [4096, 5120], P('seq', 'mp')
All inputs are finite; a program needn't handle non-finite values.
Results may differ from a plain program's by a relative error of at most 0.012.
Values may be sent and summed in bfloat16 or wider, within the bound.
No kernel may reach another device: no remote copies, remote signals or barrier semaphores. Data moves between devices by JAX's collectives and lax.ppermute only.
A program may use at most 128 MiB of HBM per device.

v0:
```python
import math

import jax
import jax.numpy as jnp
from jax import lax
from jax.experimental import pallas as pl
from jax.experimental.pallas import tpu as pltpu
from jax.sharding import PartitionSpec as P

D = 5120
HEAD_DIM = 128


def time_embed(step_value, width):
    half_width = width // 2
    positions = jnp.arange(half_width, dtype=jnp.float32)
    frequencies = jnp.exp(positions * (-math.log(10000.0) / half_width))
    angles = step_value.astype(jnp.float32) * frequencies
    return jnp.concatenate([jnp.cos(angles), jnp.sin(angles)]).astype(jnp.bfloat16)


def head_norm(values, gains):
    factor = lax.rsqrt(jnp.mean(values * values, axis=-1, keepdims=True) + 1e-06)
    return (values * factor * gains).astype(jnp.bfloat16)


def attend(query_norm, key_norm, value_rows):
    full_length, heads_here, head_width = query_norm.shape
    query_blocks = query_norm.reshape(
        full_length // full_length, full_length, heads_here, head_width
    )

    def one_block(query_block):
        logits = jnp.einsum(
            "qhd,khd->hqk", query_block, key_norm, preferred_element_type=jnp.float32
        ) * (1.0 / math.sqrt(head_width))
        expanded = jnp.exp(logits)
        probs = (expanded / jnp.sum(expanded, axis=2, keepdims=True)).astype(jnp.bfloat16)
        return jnp.einsum(
            "hqk,khd->qhd", probs, value_rows, preferred_element_type=jnp.float32
        ).astype(jnp.bfloat16)

    head_out = lax.map(one_block, query_blocks)
    return head_out.reshape(full_length, heads_here * head_width)


def pass_per_role(
    gen_heads,
    gen_resid,
    gen_out_w,
    gen_time_w,
    noise,
    steps,
    teacher_qkv,
    teacher_out,
    teacher_time,
    teacher_norm,
    critic_qkv,
    critic_out,
    critic_time,
    critic_norm,
):
    full_length = gen_heads.shape[0]
    head_cols = gen_heads.shape[1]
    embed_width = gen_time_w.shape[0]
    gen_gate = jnp.dot(
        time_embed(steps[0], embed_width)[None, :], gen_time_w, preferred_element_type=jnp.float32
    )[0]
    block = gen_heads
    gen_proj = lax.psum_scatter(
        jnp.dot(block, gen_out_w, preferred_element_type=jnp.float32),
        "seq",
        scatter_dimension=0,
        tiled=True,
    )
    latent = (gen_resid.astype(jnp.float32) + gen_gate * gen_proj).astype(jnp.bfloat16)
    role_index = lax.axis_index("role")
    level = steps[1 + role_index // 2]
    use_critic = role_index % 2 == 1
    w_qkv = jnp.where(use_critic, critic_qkv, teacher_qkv)
    w_out = jnp.where(use_critic, critic_out, teacher_out)
    w_time = jnp.where(use_critic, critic_time, teacher_time)
    w_norm = jnp.where(use_critic, critic_norm, teacher_norm)
    noise_level = level.astype(jnp.float32) / 1000.0
    noisy = (
        (1.0 - noise_level) * latent.astype(jnp.float32) + noise_level * noise.astype(jnp.float32)
    ).astype(jnp.bfloat16)
    modulation = jnp.einsum(
        "f,fkd->kd", time_embed(level, embed_width), w_time, preferred_element_type=jnp.float32
    )
    shift_vec = modulation[0]
    scale_vec = modulation[1]
    gate_vec = modulation[2]
    gathered = lax.all_gather(noisy, "seq", axis=0, tiled=True)
    partial_squares = jnp.sum(jnp.square(gathered.astype(jnp.float32)), axis=1)
    scaled = (gathered.astype(jnp.float32) * (1.0 + scale_vec)).astype(jnp.bfloat16)
    flat_w = w_qkv.reshape(w_qkv.shape[0], 3 * head_cols)
    projected = jnp.dot(scaled, flat_w, preferred_element_type=jnp.float32)
    shift_proj = jnp.dot(
        shift_vec.astype(jnp.bfloat16)[None, :], flat_w, preferred_element_type=jnp.float32
    )[0]
    projected, squares, shift_proj = lax.psum((projected, partial_squares, shift_proj), "mp")
    mixed = projected * lax.rsqrt(squares / D + 1e-06)[:, None] + shift_proj
    heads_here = head_cols // HEAD_DIM
    mixed = mixed.reshape(full_length, 3, heads_here, HEAD_DIM)
    gains = w_norm.reshape(2, heads_here, HEAD_DIM)
    query_norm = head_norm(mixed[:, 0], gains[0])
    key_norm = head_norm(mixed[:, 1], gains[1])
    value_rows = mixed[:, 2].astype(jnp.bfloat16)
    head_out = attend(query_norm, key_norm, value_rows)
    weight_sign = jnp.where(use_critic, 0.5, -0.5)
    block = head_out
    summed_rows = lax.psum_scatter(
        weight_sign * (gate_vec * jnp.dot(block, w_out, preferred_element_type=jnp.float32)),
        ("role", "seq"),
        scatter_dimension=0,
        tiled=True,
    )
    grad_rows = lax.all_gather(
        (gen_gate * summed_rows).astype(jnp.bfloat16), ("role", "seq"), axis=0, tiled=True
    )
    weight_grad = lax.dot_general(
        gen_heads, grad_rows, (((0,), (0,)), ((), ())), preferred_element_type=jnp.float32
    )
    return (latent, weight_grad.astype(jnp.bfloat16))

MIB = 1024 * 1024
EXTRA_ROWS = 16


def vmem_spec():
    return pl.BlockSpec(memory_space=pltpu.VMEM)


def smem_spec():
    return pl.BlockSpec(memory_space=pltpu.SMEM)


def params(mebibytes):
    return pltpu.CompilerParams(vmem_limit_bytes=mebibytes * MIB)


def dot32(a, b):
    return jnp.dot(a, b, preferred_element_type=jnp.float32)


def at_block(index, size):
    return pl.ds(pl.multiple_of(index * size, size), size)


def any_spec():
    return pl.BlockSpec(memory_space=pl.ANY)


def hbm_spec():
    return pl.BlockSpec(memory_space=pltpu.HBM)


def cost(flops, moved):
    return pl.CostEstimate(flops=flops, bytes_accessed=moved, transcendentals=0)


def pack_kernel(seq, product, gate, resid, noise, full, sent):
    length = full.shape[0]
    own = resid.shape[0]
    full[...] = product[...] * gate[0:1, :]
    at = at_block(seq[0], own)
    full[at, :] = full[at, :] + resid[...].astype(jnp.float32)
    sent[pl.ds(0, length), :] = full[...].astype(jnp.bfloat16)
    sent[pl.ds(length, own), :] = noise[...]


def pack_part(seq, product, gate, resid, noise):
    length, width = product.shape
    own = resid.shape[0]
    return pl.pallas_call(
        pack_kernel,
        in_specs=[smem_spec()] + [vmem_spec()] * 4,
        out_specs=[vmem_spec()] * 2,
        out_shape=[
            jax.ShapeDtypeStruct((length, width), jnp.float32),
            jax.ShapeDtypeStruct((length + own, width), jnp.bfloat16),
        ],
        compiler_params=params(8),
        name="pack_part",
    )(seq, product, gate, resid, noise)


def load_kernel(start, embed, time_a, time_b, planes_a, planes_b, weight_a, weight_b, mods, sems):
    cols = pl.ds(pl.multiple_of(start[0], weight_a.shape[2]), weight_a.shape[2])
    copies = []
    for index, (planes, weight) in enumerate(((planes_a, weight_a), (planes_b, weight_b))):
        for part in range(3):
            copies.append(
                pltpu.make_async_copy(planes.at[part, :, cols], weight.at[part], sems.at[3 * index + part])
            )
    for copy in copies:
        copy.start()
    for k in range(3):
        mods[0, k] = dot32(embed[...], time_a[k])
        mods[1, k] = dot32(embed[...], time_b[k])
    for copy in copies:
        copy.wait()


def load_part(start, embed, time_a, time_b, planes_a, planes_b, cols):
    parts, depth, _ = planes_a.shape
    width = time_a.shape[2]
    return pl.pallas_call(
        load_kernel,
        in_specs=[smem_spec()] + [vmem_spec()] * 3 + [hbm_spec()] * 2,
        out_specs=[vmem_spec()] * 3,
        out_shape=[jax.ShapeDtypeStruct((parts, depth, cols), jnp.bfloat16)] * 2
        + [jax.ShapeDtypeStruct((2, parts, 8, width), jnp.float32)],
        scratch_shapes=[pltpu.SemaphoreType.DMA((2 * parts,))],
        compiler_params=params(46),
        name="load_part",
    )(start, embed, time_a, time_b, planes_a, planes_b)


def join_kernel(full, arrived, joined):
    length = full.shape[0]
    own = arrived.shape[0] - length
    top = full[...] + arrived[pl.ds(0, length), :].astype(jnp.float32)
    joined[pl.ds(0, length), :] = top.astype(jnp.bfloat16)
    joined[pl.ds(length, own), :] = arrived[pl.ds(length, own), :]


def join_part(full, arrived):
    return pl.pallas_call(
        join_kernel,
        in_specs=[vmem_spec(), vmem_spec()],
        out_specs=vmem_spec(),
        out_shape=jax.ShapeDtypeStruct(arrived.shape, jnp.bfloat16),
        compiler_params=params(8),
        name="join_part",
    )(full, arrived)


def project(index, stride, mine, noisy, squares, mods, weight, kept, sent, result):
    tokens = noisy.shape[0]
    length = tokens // 2
    unit = squares.shape[1] // 2
    groups = weight.shape[2] // unit
    scale = mods[index, 1]
    shift = mods[index, 0]
    spread = noisy.astype(jnp.float32)
    top = spread[:length] * (1.0 + scale[1:2])
    low = spread[length:] * (1.0 + scale[2:3])
    extra = jnp.concatenate([shift[1:3], jnp.zeros((EXTRA_ROWS - 2, shift.shape[1]), jnp.float32)], axis=0)
    rows = jnp.concatenate([top, low, extra], axis=0).astype(jnp.bfloat16)
    row_id = lax.broadcasted_iota(jnp.int32, (EXTRA_ROWS, unit), 0)
    for part in range(3):
        result[...] = dot32(rows, weight[part])
        cols = pl.ds(part * unit, unit)
        for slot in range(groups):
            at = at_block(jnp.bitwise_xor(mine, slot), unit)
            goal = sent if slot & stride else kept
            place = slot // 2 if stride == 1 else slot % 2
            goal[place, pl.ds(0, tokens), cols] = result[pl.ds(0, tokens), at].astype(jnp.bfloat16)
            tail = jnp.where(row_id < 2, result[pl.ds(tokens, EXTRA_ROWS), at], 0.0)
            for level in range(2):
                tail = jnp.where(row_id == 2 + level, squares[0:1, level * length : (level + 1) * length], tail)
            goal[place, pl.ds(tokens, EXTRA_ROWS), cols] = tail.astype(jnp.bfloat16)


def qkv_kernel(seq, core, mine, levels, joined, swapped, noise, mods, weight_a, weight_b, latent, *refs):
    chunks, (values, noises, result) = refs[:4], refs[4:]
    length, cols = values.shape[0], joined.shape[1]
    own = latent.shape[0]
    tokens = 2 * length
    left, right = at_block(core[0], cols), at_block(1 - core[0], cols)
    values[:, left] = joined[pl.ds(0, length), :]
    values[:, right] = swapped[pl.ds(0, length), :]
    latent[...] = values[at_block(seq[0], own), :]
    noises[at_block(seq[0], own), :] = noise[...]
    theirs = at_block(1 - seq[0], own)
    noises[theirs, left] = joined[pl.ds(length, own), :]
    noises[theirs, right] = swapped[pl.ds(length, own), :]
    spread = values[...].astype(jnp.float32)
    noise_rows = noises[...].astype(jnp.float32)
    mixed = jnp.concatenate(
        [(1.0 - levels[level]) * spread + levels[level] * noise_rows for level in range(2)], axis=0
    ).astype(jnp.bfloat16)
    wide = mixed.astype(jnp.float32)
    sums = jnp.sum(wide * wide, axis=1, keepdims=True)
    sums = jnp.broadcast_to(sums, (tokens, length)).T[0:8]
    for index, weight in enumerate((weight_a, weight_b)):
        project(index, index + 1, mine[0], mixed, sums, mods, weight, *chunks[2 * index : 2 * index + 2], result)


def qkv_part(seq, core, mine, levels, joined, swapped, noise, mods, weight_a, weight_b):
    own, width = noise.shape
    length = joined.shape[0] - own
    tokens = 2 * length
    cols = weight_a.shape[2]
    return pl.pallas_call(
        qkv_kernel,
        in_specs=[smem_spec()] * 4 + [vmem_spec()] * 6,
        out_specs=[vmem_spec()] * 5,
        out_shape=[jax.ShapeDtypeStruct((own, width), jnp.bfloat16)]
        + [jax.ShapeDtypeStruct((cols // length // 2, tokens + EXTRA_ROWS, 3 * length), jnp.bfloat16)] * 4,
        scratch_shapes=[
            pltpu.VMEM((length, width), jnp.bfloat16),
            pltpu.VMEM((length, width), jnp.bfloat16),
            pltpu.VMEM((tokens + EXTRA_ROWS, cols), jnp.float32),
        ],
        compiler_params=params(20),
        name="qkv_part",
    )(seq, core, mine, levels, joined, swapped, noise, mods, weight_a, weight_b)


def attend_kernel(width, kept_a, other_a, kept_b, other_b, gains, out):
    _, _, length, unit = out.shape
    tokens = 2 * length
    for index, (kept, other) in enumerate(((kept_a, other_a), (kept_b, other_b))):
        mixed = kept[...] + other[...].astype(jnp.float32)
        extra = mixed[tokens:]
        for level in range(2):
            rows_at = slice(level * length, (level + 1) * length)
            squares = jnp.broadcast_to(extra[2 + level : 3 + level, :unit], (unit, unit)).T
            factor = lax.rsqrt(squares * (1.0 / width) + 1e-06)

            def pick(part):
                cols = slice(part * unit, (part + 1) * unit)
                return mixed[rows_at, cols] * factor + extra[level : level + 1, cols]

            def normed(part):
                rows = pick(part)
                mean = jnp.mean(rows * rows, axis=1, keepdims=True)
                return (rows * lax.rsqrt(mean + 1e-06) * gains[index, part : part + 1, :]).astype(jnp.bfloat16)

            query, key = normed(0), normed(1)
            value = pick(2).astype(jnp.bfloat16)
            logits = lax.dot_general(
                query, key, (((1,), (1,)), ((), ())), preferred_element_type=jnp.float32
            ) * (1.0 / math.sqrt(unit))
            expanded = jnp.exp(logits)
            probs = (expanded / jnp.sum(expanded, axis=1, keepdims=True)).astype(jnp.bfloat16)
            out[index, level] = dot32(probs, value).astype(jnp.bfloat16)


def attend_part(kept_a, other_a, kept_b, other_b, gains, width):
    unit = kept_a.shape[1] // 3
    length = (kept_a.shape[0] - EXTRA_ROWS) // 2
    return pl.pallas_call(
        lambda *refs: attend_kernel(width, *refs),
        in_specs=[vmem_spec()] * 5,
        out_specs=vmem_spec(),
        out_shape=jax.ShapeDtypeStruct((2, 2, length, unit), jnp.bfloat16),
        compiler_params=params(8),
        name="attend_part",
    )(kept_a, other_a, kept_b, other_b, gains)


def out_kernel(core, mine, *refs):
    heads = refs[0:4]
    weight_a, weight_b, mods, kept, sent, rows, total = refs[4:]
    _, _, length, unit = heads[0].shape
    for index, weight in enumerate((weight_a, weight_b)):
        for slot, head in enumerate(heads):
            at = at_block(jnp.bitwise_xor(mine[0], slot), unit)
            for level in range(2):
                rows[pl.ds(level * length, length), at] = head[index, level]
        result = dot32(rows[...], weight[...])
        gates = mods[index, 2]
        signed = gates[1:2] * result[:length] + gates[2:3] * result[length:]
        if index == 0:
            total[...] = -0.5 * signed
        else:
            total[...] = total[...] + 0.5 * signed
    cols = kept.shape[1]
    kept[...] = total[:, at_block(core[0], cols)]
    sent[...] = total[:, at_block(1 - core[0], cols)].astype(jnp.bfloat16)


def out_part(core, mine, heads, weight_a, weight_b, mods):
    length = heads[0].shape[2]
    depth, width = weight_a.shape
    return pl.pallas_call(
        out_kernel,
        in_specs=[smem_spec()] * 2 + [vmem_spec()] * 7,
        out_specs=[vmem_spec()] * 2,
        out_shape=[
            jax.ShapeDtypeStruct((length, width // 2), jnp.float32),
            jax.ShapeDtypeStruct((length, width // 2), jnp.bfloat16),
        ],
        scratch_shapes=[
            pltpu.VMEM((2 * length, depth), jnp.bfloat16),
            pltpu.VMEM((length, width), jnp.float32),
        ],
        compiler_params=params(16),
        name="out_part",
    )(core, mine, *heads, weight_a, weight_b, mods)


def grad_kernel(half, heads_t, rows, *refs):
    refs[-1][...] = dot32(heads_t[...], rows[...]).astype(jnp.bfloat16)


def grad_part(half, heads_t, rows, before, steps):
    depth, length = heads_t.shape
    cols = rows.shape[1]
    tile = depth // steps
    rest = [] if before is None else [before]
    grid_spec = pltpu.PrefetchScalarGridSpec(
        num_scalar_prefetch=1,
        grid=(steps,),
        in_specs=[
            pl.BlockSpec((tile, length), lambda n, w: (n, 0)),
            pl.BlockSpec((length, cols), lambda n, w: (0, 0)),
        ]
        + [any_spec()] * len(rest),
        out_specs=pl.BlockSpec((tile, cols), lambda n, w: (n, w[0])),
    )
    return pl.pallas_call(
        grad_kernel,
        grid_spec=grid_spec,
        out_shape=jax.ShapeDtypeStruct((depth, 2 * cols), jnp.bfloat16),
        input_output_aliases={3: 0} if rest else {},
        compiler_params=params(16),
        name="grad_part",
    )(half, heads_t, rows, *rest)


def exchange(array, axis, bit):
    return lax.ppermute(array, axis, [(i, i ^ bit) for i in range(lax.axis_size(axis))])


def take(array, begin, size, axis):
    return lax.dynamic_slice_in_dim(array, begin, size, axis=axis, allow_negative_indices=False)


def both(mine, theirs):
    return mine.astype(jnp.float32) + theirs.astype(jnp.float32)


def heads_per_role(
    gen_heads,
    gen_resid,
    gen_out_w,
    gen_time_w,
    noise,
    steps,
    teacher_qkv,
    teacher_out,
    teacher_time,
    teacher_norm,
    critic_qkv,
    critic_out,
    critic_time,
    critic_norm,
):
    length = gen_heads.shape[0]
    roles, groups = lax.axis_size("role"), lax.axis_size("mp")
    role, seq, mp = lax.axis_index("role"), lax.axis_index("seq"), lax.axis_index("mp")
    part_cols = gen_heads.shape[1] // roles
    freq = gen_time_w.shape[0]
    core = role % 2
    half_cols = gen_resid.shape[1] // 2
    unit = part_cols // groups

    embed = jax.vmap(lambda t: time_embed(t, freq))(steps)
    embed = jnp.concatenate([embed, jnp.zeros((5, freq), jnp.bfloat16)], axis=0)
    levels = steps[1:3].astype(jnp.float32) / 1000.0
    start = role * part_cols
    scalars = [seq, mp, core, 1 - core, core * half_cols, start, start + mp * unit]
    embed, *scalars = lax.optimization_barrier((embed, *scalars))
    seq_at, mine, core, other_core, start_at = [v.astype(jnp.int32).reshape(1) for v in scalars[:4] + scalars[5:6]]
    begin, start, gain_at = scalars[4:]
    weight, time_half, resid_half, noise_half = [
        take(w, begin, half_cols, 1) for w in (gen_out_w, gen_time_w, gen_resid, noise)
    ]
    gate = dot32(embed, time_half)
    full, sent = pack_part(seq_at, dot32(gen_heads, weight), gate, resid_half, noise_half)
    arrived = exchange(sent, "seq", 1)
    later, embed, _ = lax.optimization_barrier((start_at, embed, full))
    planes = [w.transpose(1, 0, 2) for w in (teacher_qkv, critic_qkv, teacher_time, critic_time)]
    weight_a, weight_b, mods = load_part(later, embed, planes[2], planes[3], planes[0], planes[1], part_cols)
    arrived, mods = lax.optimization_barrier((arrived, mods))
    joined = join_part(full, arrived)
    swapped = exchange(joined, "role", 1)

    latent, kept_a, sent_a, kept_b, sent_b = qkv_part(
        seq_at, core, mine, levels, joined, swapped, noise, mods, weight_a, weight_b
    )
    arrived_a, arrived_b = exchange(sent_a, "mp", 1), exchange(sent_b, "mp", 2)
    out_a, out_b = [take(w, start, part_cols, 0) for w in (teacher_out, critic_out)]
    gains = jnp.stack([teacher_norm, critic_norm])
    gains = take(gains, gain_at, unit, 2)
    arrived_a, arrived_b, out_a, out_b, gains = lax.optimization_barrier((arrived_a, arrived_b, out_a, out_b, gains))
    sum_a, sum_b = both(kept_a, arrived_a), both(kept_b, arrived_b)
    last_a = exchange(sum_a[1].astype(jnp.bfloat16), "mp", 2)
    last_b = exchange(sum_b[1].astype(jnp.bfloat16), "mp", 1)
    head = attend_part(sum_a[0], last_a, sum_b[0], last_b, gains, D)
    near, far = exchange(head, "mp", 1), exchange(head, "mp", 2)
    gathered = head, near, far, exchange(far, "mp", 1)

    kept, sent = out_part(core, mine, gathered, out_a, out_b, mods)
    total = both(kept, exchange(sent, "role", 1)).astype(jnp.bfloat16)
    along_x = exchange(total, "seq", 1)
    along_y = exchange(total, "role", 2)
    across = lax.ppermute(
        total, ("role", "seq"), [(i, i ^ (2 * lax.axis_size("seq") + 1)) for i in range(roles * lax.axis_size("seq"))]
    )
    total = both(total, along_x) + both(along_y, across)
    rows = (gate[0:1] * total).astype(jnp.bfloat16)
    heads_t = gen_heads.T
    theirs = exchange(rows, "role", 1)
    weight_grad = grad_part(core, heads_t, rows, None, 2)
    weight_grad = grad_part(other_core, heads_t, theirs, weight_grad, 2)
    return latent, weight_grad


def solution(mesh):
    in_specs = (
        P(None, "seq"),
        P("seq", "mp"),
        P("seq", "mp"),
        P(None, "mp"),
        P("seq", "mp"),
        P(),
        P("mp", None, "seq"),
        P("seq", "mp"),
        P(None, None, "mp"),
        P(None, "seq"),
        P("mp", None, "seq"),
        P("seq", "mp"),
        P(None, None, "mp"),
        P(None, "seq"),
    )
    out_specs = (P("seq", "mp"), P("seq", "mp"))
    roles, seqs, groups = mesh.shape["role"], mesh.shape["seq"], mesh.shape["mp"]

    def on_device(*arrays):
        heads_here = arrays[0].shape[1] // HEAD_DIM
        length = arrays[0].shape[0]
        fits = (roles, seqs, groups) == (4, 2, 4) and heads_here == roles * groups and length == HEAD_DIM
        return heads_per_role(*arrays) if fits else pass_per_role(*arrays)

    return jax.shard_map(
        on_device, mesh=mesh, in_specs=in_specs, out_specs=out_specs, check_vma=False
    )
```

profile of v0, /device:TPU:1, one launch (start us, length us, event | category | flops | bytes accessed | tf_op | source)
XLA Modules:
  0.0 88.6 jit_solution(7141864227392406398)
XLA Ops:
  0.6 0.0 copy-start
  0.6 0.0 copy-start.3
  0.7 0.8 convert_element_type.48
  1.5 0.1 fusion.13
  1.6 0.0 copy-start.4
  1.6 3.1 %fusion.2.product = f32[128,640]{1,0:T(8,128)S(1)} fusion(bf16[128,2048]{1,0:T(8,128)(2,1)} %param.14, bf16[2048,1280]{1,0:T(8,128)(2,1)} %param.16, s32[]{:T(128)S(6)} %mul.47), kind=kOutput, calls=%fused_computation.2 | convolution fusion | flops 335544320 | bytes 3473412 | tf_op jit(solution)/shard_map/dot_general | solution.py:144
  4.7 0.0 copy-done
  4.7 0.3 fusion.5.gate
  5.0 1.0 %constant_dynamic-slice_fusion.2 = (bf16[64,640]{1,0:T(8,128)(2,1)S(1)}, bf16[64,640]{1,0:T(8,128)(2,1)S(1)}) fusion(bf16[64,1280]{1,0:T(8,128)(2,1)} %noise.1, s32[]{:T(128)S(6)} %mul.47, bf16[64,1280]{1,0:T(8,128)(2,1)} %param.15), kind=kLoop, calls=%fused_computation.29 | loop fusion | bytes 327684 | tf_op jit(solution)/shard_map/dynamic_slice | solution.py:431
  6.0 0.1 pack_part.1
  6.1 2.1 %collective-permute-start = (bf16[192,640]{1,0:T(8,128)(2,1)S(1)}, bf16[192,640]{1,0:T(8,128)(2,1)S(1)}, u32[]{:S(2)}, u32[]{:S(2)}) collective-permute-start(bf16[192,640]{1,0:T(8,128)(2,1)S(1)} %get-tuple-element.37), channel_id=1, source_target_pairs={{0,4},{4,0},{1,5},{5,1},{2,6},{6,2},{3,7},{7,3},{8,12},{12,8},{9,1... | collective-permute-start | bytes 737288 | tf_op jit(solution)/shard_map/ppermute | solution.py:427
  8.2 0.0 copy-done.3
  8.2 0.0 copy-done.4
  8.2 0.0 copy-start.9
  8.2 5.6 %load_part.1 = (bf16[3,1280,512]{2,1,0:T(8,128)(2,1)S(1)}, bf16[3,1280,512]{2,1,0:T(8,128)(2,1)}, f32[2,3,8,1280]{3,2,1,0:T(8,128)S(1)}) custom-call(s32[1]{0:T(128)} %bitcast.4.start, bf16[8,256]{1,0:T(8,128)(2,1)S(1)} %fusion.11.embed, bf16[3,256,1280]{2,1,0:T(8,128)(2,1)S(1)} %bitcast.26, bf16[3,256,1280]{2,1,0:T(8,128)(2,1)S(1)} %bitcast.27, ...), custom_call_target="tpu_custom_call" | custom-call | tf_op jit(solution)/shard_map/load_part/pallas_call | solution.py:209
  13.9 0.0 copy-start.7
  13.9 0.0 copy-start.8
  13.9 0.0 collective-permute-done.arrived
  13.9 1.3 %collective-permute-start.1 = (bf16[192,640]{1,0:T(8,128)(2,1)S(1)}, bf16[192,640]{1,0:T(8,128)(2,1)S(1)}, u32[]{:S(2)}, u32[]{:S(2)}) collective-permute-start(bf16[192,640]{1,0:T(8,128)(2,1)S(1)} %join_part.1.joined), channel_id=1, source_target_pairs={{0,8},{8,0},{16,24},{24,16},{1,9},{9,1},{17,25},{25,17},{2,10},{10... | collective-permute-start | bytes 737288 | tf_op jit(solution)/shard_map/ppermute | solution.py:427
  15.2 0.0 copy-done.9
  15.3 0.1 convert_multiply_fusion.levels
  15.3 1.1 %collective-permute-done.1.swapped = bf16[192,640]{1,0:T(8,128)(2,1)S(1)} collective-permute-done((bf16[192,640]{1,0:T(8,128)(2,1)S(1)}, bf16[192,640]{1,0:T(8,128)(2,1)S(1)}, u32[]{:S(2)}, u32[]{:S(2)}) %collective-permute-start.1) | collective-permute-done | bytes 245792 | tf_op jit(solution)/shard_map/ppermute | solution.py:427
  16.4 0.0 copy-done.5
  16.4 2.1 %copy-done.2 = bf16[3,1280,512]{2,1,0:T(8,128)(2,1)S(1)} copy-done((bf16[3,1280,512]{2,1,0:T(8,128)(2,1)S(1)}, bf16[3,1280,512]{2,1,0:T(8,128)(2,1)}, u32[]{:S(2)}) %copy-start.2) | copy-done | bytes 3932184
  18.5 4.0 %qkv_part.1 = (bf16[64,1280]{1,0:T(8,128)(2,1)}, bf16[2,272,384]{2,1,0:T(8,128)(2,1)S(1)}, bf16[2,272,384]{2,1,0:T(8,128)(2,1)S(1)}, bf16[2,272,384]{2,1,0:T(8,128)(2,1)S(1)}, bf16[2,272,384]{2,1,0:T(8,128)(2,1)S(1)}) custom-call(s32[1]{0:T(128)} %bitcast.seq, s32[1]{0:T(128)} %bitcast.1.core.half, s32[1]{0:T(128)} %bitcast.2.mine, ...), custom_call_target="tpu_custom_call" | custom-call | tf_op jit(solution)/shard_map/qkv_part/pallas_call | solution.py:297
  22.5 1.6 %collective-permute-start.2 = (bf16[2,272,384]{2,1,0:T(8,128)(2,1)S(1)}, bf16[2,272,384]{2,1,0:T(8,128)(2,1)S(1)}, u32[]{:S(2)}, u32[]{:S(2)}) collective-permute-start(bf16[2,272,384]{2,1,0:T(8,128)(2,1)S(1)} %get-tuple-element.49), channel_id=1, source_target_pairs={{0,1},{1,0},{2,3},{3,2},{4,5},{5,4},{6,7},{7,6},{8,9},{9,8},{10,11... | collective-permute-start | bytes 1253384 | tf_op jit(solution)/shard_map/ppermute | solution.py:427
  24.0 2.3 %collective-permute-start.3 = (bf16[2,272,384]{2,1,0:T(8,128)(2,1)S(1)}, bf16[2,272,384]{2,1,0:T(8,128)(2,1)S(1)}, u32[]{:S(2)}, u32[]{:S(2)}) collective-permute-start(bf16[2,272,384]{2,1,0:T(8,128)(2,1)S(1)} %get-tuple-element.50), channel_id=1, source_target_pairs={{0,2},{1,3},{2,0},{3,1},{4,6},{5,7},{6,4},{7,5},{8,10},{9,11},{10,... | collective-permute-start | bytes 1253384 | tf_op jit(solution)/shard_map/ppermute | solution.py:427
  26.4 0.0 copy-done.7
  26.4 0.0 copy-done.8
  26.4 0.1 fusion.12.refs_4_
  26.4 2.3 %constant_dynamic-slice_fusion = (bf16[512,1280]{1,0:T(8,128)(2,1)S(1)}, bf16[512,1280]{1,0:T(8,128)(2,1)S(1)}) fusion(bf16[2048,1280]{1,0:T(8,128)(2,1)} %param.25, s32[]{:T(128)} %mul.48, bf16[2048,1280]{1,0:T(8,128)(2,1)} %param.21), kind=kLoop, calls=%fused_computation.27 | loop fusion | bytes 5242884 | tf_op jit(solution)/shard_map/dynamic_slice | solution.py:431
  28.8 13.6 %collective-permute-done.2 = bf16[2,272,384]{2,1,0:T(8,128)(2,1)S(1)} collective-permute-done((bf16[2,272,384]{2,1,0:T(8,128)(2,1)S(1)}, bf16[2,272,384]{2,1,0:T(8,128)(2,1)S(1)}, u32[]{:S(2)}, u32[]{:S(2)}) %collective-permute-start.2) | collective-permute-done | bytes 417824 | tf_op jit(solution)/shard_map/ppermute | solution.py:427
  42.4 0.0 collective-permute-done.3
  42.4 0.1 convert_add_fusion.1
  42.5 0.0 copy-start.6
  42.5 2.5 %collective-permute-start.4 = (bf16[272,384]{1,0:T(8,128)(2,1)S(1)}, bf16[272,384]{1,0:T(8,128)(2,1)S(1)}, u32[]{:S(2)}, u32[]{:S(2)}) collective-permute-start(bf16[272,384]{1,0:T(8,128)(2,1)S(1)} %fusion.7), channel_id=1, source_target_pairs={{0,2},{1,3},{2,0},{3,1},{4,6},{5,7},{6,4},{7,5},{8,10},{9,11},{10,... | collective-permute-start | bytes 626696 | tf_op jit(solution)/shard_map/ppermute | solution.py:427
  45.0 0.1 convert_add_fusion
  45.2 2.3 %collective-permute-start.5 = (bf16[272,384]{1,0:T(8,128)(2,1)S(1)}, bf16[272,384]{1,0:T(8,128)(2,1)S(1)}, u32[]{:S(2)}, u32[]{:S(2)}) collective-permute-start(bf16[272,384]{1,0:T(8,128)(2,1)S(1)} %fusion.8), channel_id=1, source_target_pairs={{0,1},{1,0},{2,3},{3,2},{4,5},{5,4},{6,7},{7,6},{8,9},{9,8},{10,11... | collective-permute-start | bytes 626696 | tf_op jit(solution)/shard_map/ppermute | solution.py:427
  47.4 0.8 collective-permute-done.4.refs_1_
  48.2 4.5 %collective-permute-done.5.refs_3_ = bf16[272,384]{1,0:T(8,128)(2,1)S(1)} collective-permute-done((bf16[272,384]{1,0:T(8,128)(2,1)S(1)}, bf16[272,384]{1,0:T(8,128)(2,1)S(1)}, u32[]{:S(2)}, u32[]{:S(2)}) %collective-permute-start.5) | collective-permute-done | bytes 208928 | tf_op jit(solution)/shard_map/ppermute | solution.py:427
  52.7 1.3 %attend_part.1.refs_0_ = bf16[2,2,128,128]{3,2,1,0:T(8,128)(2,1)S(1)} custom-call(f32[272,384]{1,0:T(8,128)S(1)} %slice_bitcast_fusion.1.refs_0_, bf16[272,384]{1,0:T(8,128)(2,1)S(1)} %collective-permute-done.4.refs_1_, f32[272,384]{1,0:T(8,128)S(1)} %slice_bitcast_fusion.refs_2_, bf16[272,384]{1,0:T(8,128)(2,1)S(1)} %collective-permute-done.5.refs_3_, ...), custom_call_target="tpu_custom_call" | custom-call | tf_op jit(solution)/shard_map/attend_part/pallas_call | solution.py:346
  54.0 3.3 %collective-permute-start.7 = (bf16[2,2,128,128]{3,2,1,0:T(8,128)(2,1)S(1)}, bf16[2,2,128,128]{3,2,1,0:T(8,128)(2,1)S(1)}, u32[]{:S(2)}, u32[]{:S(2)}) collective-permute-start(bf16[2,2,128,128]{3,2,1,0:T(8,128)(2,1)S(1)} %attend_part.1.refs_0_), channel_id=1, source_target_pairs={{0,2},{1,3},{2,0},{3,1},{4,6},{5,7},{6,4},{7,5},{8,10},{9,11},{10,... | collective-permute-start | bytes 393224 | tf_op jit(solution)/shard_map/ppermute | solution.py:427
  57.3 2.8 %collective-permute-start.6 = (bf16[2,2,128,128]{3,2,1,0:T(8,128)(2,1)S(1)}, bf16[2,2,128,128]{3,2,1,0:T(8,128)(2,1)S(1)}, u32[]{:S(2)}, u32[]{:S(2)}) collective-permute-start(bf16[2,2,128,128]{3,2,1,0:T(8,128)(2,1)S(1)} %attend_part.1.refs_0_), channel_id=1, source_target_pairs={{0,1},{1,0},{2,3},{3,2},{4,5},{5,4},{6,7},{7,6},{8,9},{9,8},{10,11... | collective-permute-start | bytes 393224 | tf_op jit(solution)/shard_map/ppermute | solution.py:427
  60.0 0.0 collective-permute-done.7.refs_2_
  60.1 2.8 %collective-permute-start.8 = (bf16[2,2,128,128]{3,2,1,0:T(8,128)(2,1)S(1)}, bf16[2,2,128,128]{3,2,1,0:T(8,128)(2,1)S(1)}, u32[]{:S(2)}, u32[]{:S(2)}) collective-permute-start(bf16[2,2,128,128]{3,2,1,0:T(8,128)(2,1)S(1)} %collective-permute-done.7.refs_2_), channel_id=1, source_target_pairs={{0,1},{1,0},{2,3},{3,2},{4,5},{5,4},{6,7},{7,6},{8,9},{9,8},{10,11... | collective-permute-start | bytes 393224 | tf_op jit(solution)/shard_map/ppermute | solution.py:427
  62.8 0.5 collective-permute-done.6.refs_1_
  63.4 3.3 %collective-permute-done.8.refs_3_ = bf16[2,2,128,128]{3,2,1,0:T(8,128)(2,1)S(1)} collective-permute-done((bf16[2,2,128,128]{3,2,1,0:T(8,128)(2,1)S(1)}, bf16[2,2,128,128]{3,2,1,0:T(8,128)(2,1)S(1)}, u32[]{:S(2)}, u32[]{:S(2)}) %collective-permute-start.8) | collective-permute-done | bytes 131104 | tf_op jit(solution)/shard_map/ppermute | solution.py:427
  66.6 1.0 %out_part.1 = (f32[128,640]{1,0:T(8,128)S(1)}, bf16[128,640]{1,0:T(8,128)(2,1)S(1)}) custom-call(s32[1]{0:T(128)} %bitcast.1.core.half, s32[1]{0:T(128)} %bitcast.2.mine, bf16[2,2,128,128]{3,2,1,0:T(8,128)(2,1)S(1)} %attend_part.1.refs_0_, bf16[2,2,128,128]{3,2,1,0:T(8,128)(2,1)S(1)} %collective-permute-done.6.refs_1_, ...), custom_call_target="tpu_custom_call" | custom-call | tf_op jit(solution)/shard_map/out_part/pallas_call | solution.py:380
  67.6 4.1 %collective-permute-start.9 = (bf16[128,640]{1,0:T(8,128)(2,1)S(1)}, bf16[128,640]{1,0:T(8,128)(2,1)S(1)}, u32[]{:S(2)}, u32[]{:S(2)}) collective-permute-start(bf16[128,640]{1,0:T(8,128)(2,1)S(1)} %get-tuple-element.59), channel_id=1, source_target_pairs={{0,8},{8,0},{16,24},{24,16},{1,9},{9,1},{17,25},{25,17},{2,10},{10... | collective-permute-start | bytes 491528 | tf_op jit(solution)/shard_map/ppermute | solution.py:427
  71.8 1.0 %collective-permute-done.9 = bf16[128,640]{1,0:T(8,128)(2,1)S(1)} collective-permute-done((bf16[128,640]{1,0:T(8,128)(2,1)S(1)}, bf16[128,640]{1,0:T(8,128)(2,1)S(1)}, u32[]{:S(2)}, u32[]{:S(2)}) %collective-permute-start.9) | collective-permute-done | bytes 163872 | tf_op jit(solution)/shard_map/ppermute | solution.py:427
  72.8 2.2 %collective-permute-start.12 = (bf16[128,640]{1,0:T(8,128)(2,1)S(1)}, bf16[128,640]{1,0:T(8,128)(2,1)S(1)}, u32[]{:S(2)}, u32[]{:S(2)}) collective-permute-start(bf16[128,640]{1,0:T(8,128)(2,1)S(1)} %add_convert_fusion), channel_id=1, source_target_pairs={{0,20},{4,16},{8,28},{12,24},{16,4},{20,0},{24,12},{28,8},{1,21},{... | collective-permute-start | bytes 491528 | tf_op jit(solution)/shard_map/ppermute | solution.py:503
  75.0 0.2 collective-permute-start.11
  75.2 0.3 collective-permute-start.10
  75.6 3.7 %collective-permute-done.12 = bf16[128,640]{1,0:T(8,128)(2,1)S(1)} collective-permute-done((bf16[128,640]{1,0:T(8,128)(2,1)S(1)}, bf16[128,640]{1,0:T(8,128)(2,1)S(1)}, u32[]{:S(2)}, u32[]{:S(2)}) %collective-permute-start.12) | collective-permute-done | bytes 163872 | tf_op jit(solution)/shard_map/ppermute | solution.py:503
  79.2 4.2 %collective-permute-done.11 = bf16[128,640]{1,0:T(8,128)(2,1)S(1)} collective-permute-done((bf16[128,640]{1,0:T(8,128)(2,1)S(1)}, bf16[128,640]{1,0:T(8,128)(2,1)S(1)}, u32[]{:S(2)}, u32[]{:S(2)}) %collective-permute-start.11) | collective-permute-done | bytes 163872 | tf_op jit(solution)/shard_map/ppermute | solution.py:427
  83.4 0.0 collective-permute-done.10
  83.4 0.1 multiply_convert_fusion.rows
  83.5 0.6 collective-permute-start.13
  84.2 0.0 copy-done.6
  84.2 0.3 copy.18
  84.5 2.1 %grad_part.2.refs_0_ = bf16[2048,1280]{1,0:T(8,128)(2,1)} custom-call(s32[1]{0:T(128)} %bitcast.1.core.half, bf16[2048,128]{1,0:T(8,128)(2,1)S(1)} %bitcast.24, bf16[128,640]{1,0:T(8,128)(2,1)S(1)} %multiply_convert_fusion.rows), custom_call_target="tpu_custom_call" | custom-call | tf_op jit(solution)/shard_map/grad_part/pallas_call | solution.py:416
  86.5 0.0 collective-permute-done.13.rows
  86.5 2.0 %grad_part.3 = bf16[2048,1280]{1,0:T(8,128)(2,1)} custom-call(s32[1]{0:T(128)} %bitcast.9.half, bf16[2048,128]{1,0:T(8,128)(2,1)S(1)} %bitcast.25, bf16[128,640]{1,0:T(8,128)(2,1)S(1)} %collective-permute-done.13.rows, bf16[2048,1280]{1,0:T(8,128)(2,1)} %grad_part.2.refs_0_), custom_call_target="tpu_custom_call", output_to_operand_aliasing={{}: (3, {})} | custom-call | tf_op jit(solution)/shard_map/grad_part/pallas_call | solution.py:416
  88.6 0.0 copy-done.1
  (12 shorter events, 0.2 us)
Async XLA Ops:
  0.6 4.1 %copy-start = (bf16[256,1280]{1,0:T(8,128)(2,1)S(1)}, bf16[256,1280]{1,0:T(8,128)(2,1)}, u32[]{:S(2)}) copy-start(bf16[256,1280]{1,0:T(8,128)(2,1)} %param.17) | copy-start | bytes 1966084
  0.6 7.6 %copy-start.3 = (bf16[256,3,1280]{2,0,1:T(8,128)(2,1)S(1)}, bf16[256,3,1280]{2,0,1:T(8,128)(2,1)}, u32[]{:S(2)}) copy-start(bf16[256,3,1280]{2,0,1:T(8,128)(2,1)} %param.22) | copy-start | bytes 5898244
  1.6 6.6 %copy-start.4 = (bf16[256,3,1280]{2,0,1:T(8,128)(2,1)S(1)}, bf16[256,3,1280]{2,0,1:T(8,128)(2,1)}, u32[]{:S(2)}) copy-start(bf16[256,3,1280]{2,0,1:T(8,128)(2,1)} %param.26) | copy-start | bytes 5898244
  6.1 7.8 %collective-permute-start = (bf16[192,640]{1,0:T(8,128)(2,1)S(1)}, bf16[192,640]{1,0:T(8,128)(2,1)S(1)}, u32[]{:S(2)}, u32[]{:S(2)}) collective-permute-start(bf16[192,640]{1,0:T(8,128)(2,1)S(1)} %get-tuple-element.37), channel_id=1, source_target_pairs={{0,4},{4,0},{1,5},{5,1},{2,6},{6,2},{3,7},{7,3},{8,12},{12,8},{9,1... | collective-permute-start | bytes 737288 | tf_op jit(solution)/shard_map/ppermute | solution.py:427
  8.2 7.0 %copy-start.9 = (s32[3]{0:T(128)S(1)}, s32[3]{0:T(128)}, u32[]{:S(2)}) copy-start(s32[3]{0:T(128)} %param.19) | copy-start | bytes 40
  8.2 8.2 %copy-start.5 = (bf16[64,1280]{1,0:T(8,128)(2,1)S(1)}, bf16[64,1280]{1,0:T(8,128)(2,1)}, u32[]{:S(2)}) copy-start(bf16[64,1280]{1,0:T(8,128)(2,1)} %noise.1) | copy-start | bytes 491524
  13.9 12.5 %copy-start.7 = (f32[2,2048]{1,0:T(2,128)S(1)}, f32[2,2048]{1,0:T(2,128)}, u32[]{:S(2)}) copy-start(f32[2,2048]{1,0:T(2,128)} %param.23) | copy-start | bytes 49156
  13.9 12.5 %copy-start.8 = (f32[2,2048]{1,0:T(2,128)S(1)}, f32[2,2048]{1,0:T(2,128)}, u32[]{:S(2)}) copy-start(f32[2,2048]{1,0:T(2,128)} %param.27) | copy-start | bytes 49156
  13.9 2.5 %collective-permute-start.1 = (bf16[192,640]{1,0:T(8,128)(2,1)S(1)}, bf16[192,640]{1,0:T(8,128)(2,1)S(1)}, u32[]{:S(2)}, u32[]{:S(2)}) collective-permute-start(bf16[192,640]{1,0:T(8,128)(2,1)S(1)} %join_part.1.joined), channel_id=1, source_target_pairs={{0,8},{8,0},{16,24},{24,16},{1,9},{9,1},{17,25},{25,17},{2,10},{10... | collective-permute-start | bytes 737288 | tf_op jit(solution)/shard_map/ppermute | solution.py:427
  16.4 2.1 %copy-start.2 = (bf16[3,1280,512]{2,1,0:T(8,128)(2,1)S(1)}, bf16[3,1280,512]{2,1,0:T(8,128)(2,1)}, u32[]{:S(2)}) copy-start(bf16[3,1280,512]{2,1,0:T(8,128)(2,1)} %get-tuple-element.45.weight_b) | copy-start | bytes 11796484
  22.5 19.9 %collective-permute-start.2 = (bf16[2,272,384]{2,1,0:T(8,128)(2,1)S(1)}, bf16[2,272,384]{2,1,0:T(8,128)(2,1)S(1)}, u32[]{:S(2)}, u32[]{:S(2)}) collective-permute-start(bf16[2,272,384]{2,1,0:T(8,128)(2,1)S(1)} %get-tuple-element.49), channel_id=1, source_target_pairs={{0,1},{1,0},{2,3},{3,2},{4,5},{5,4},{6,7},{7,6},{8,9},{9,8},{10,11... | collective-permute-start | bytes 1253384 | tf_op jit(solution)/shard_map/ppermute | solution.py:427
  24.0 18.3 %collective-permute-start.3 = (bf16[2,272,384]{2,1,0:T(8,128)(2,1)S(1)}, bf16[2,272,384]{2,1,0:T(8,128)(2,1)S(1)}, u32[]{:S(2)}, u32[]{:S(2)}) collective-permute-start(bf16[2,272,384]{2,1,0:T(8,128)(2,1)S(1)} %get-tuple-element.50), channel_id=1, source_target_pairs={{0,2},{1,3},{2,0},{3,1},{4,6},{5,7},{6,4},{7,5},{8,10},{9,11},{10,... | collective-permute-start | bytes 1253384 | tf_op jit(solution)/shard_map/ppermute | solution.py:427
  42.5 41.7 %copy-start.6 = (bf16[128,2048]{1,0:T(8,128)(2,1)S(1)}, bf16[128,2048]{1,0:T(8,128)(2,1)}, u32[]{:S(2)}) copy-start(bf16[128,2048]{1,0:T(8,128)(2,1)} %param.14) | copy-start | bytes 1572868
  42.5 5.7 %collective-permute-start.4 = (bf16[272,384]{1,0:T(8,128)(2,1)S(1)}, bf16[272,384]{1,0:T(8,128)(2,1)S(1)}, u32[]{:S(2)}, u32[]{:S(2)}) collective-permute-start(bf16[272,384]{1,0:T(8,128)(2,1)S(1)} %fusion.7), channel_id=1, source_target_pairs={{0,2},{1,3},{2,0},{3,1},{4,6},{5,7},{6,4},{7,5},{8,10},{9,11},{10,... | collective-permute-start | bytes 626696 | tf_op jit(solution)/shard_map/ppermute | solution.py:427
  45.2 7.6 %collective-permute-start.5 = (bf16[272,384]{1,0:T(8,128)(2,1)S(1)}, bf16[272,384]{1,0:T(8,128)(2,1)S(1)}, u32[]{:S(2)}, u32[]{:S(2)}) collective-permute-start(bf16[272,384]{1,0:T(8,128)(2,1)S(1)} %fusion.8), channel_id=1, source_target_pairs={{0,1},{1,0},{2,3},{3,2},{4,5},{5,4},{6,7},{7,6},{8,9},{9,8},{10,11... | collective-permute-start | bytes 626696 | tf_op jit(solution)/shard_map/ppermute | solution.py:427
  54.0 6.0 %collective-permute-start.7 = (bf16[2,2,128,128]{3,2,1,0:T(8,128)(2,1)S(1)}, bf16[2,2,128,128]{3,2,1,0:T(8,128)(2,1)S(1)}, u32[]{:S(2)}, u32[]{:S(2)}) collective-permute-start(bf16[2,2,128,128]{3,2,1,0:T(8,128)(2,1)S(1)} %attend_part.1.refs_0_), channel_id=1, source_target_pairs={{0,2},{1,3},{2,0},{3,1},{4,6},{5,7},{6,4},{7,5},{8,10},{9,11},{10,... | collective-permute-start | bytes 393224 | tf_op jit(solution)/shard_map/ppermute | solution.py:427
  57.3 6.1 %collective-permute-start.6 = (bf16[2,2,128,128]{3,2,1,0:T(8,128)(2,1)S(1)}, bf16[2,2,128,128]{3,2,1,0:T(8,128)(2,1)S(1)}, u32[]{:S(2)}, u32[]{:S(2)}) collective-permute-start(bf16[2,2,128,128]{3,2,1,0:T(8,128)(2,1)S(1)} %attend_part.1.refs_0_), channel_id=1, source_target_pairs={{0,1},{1,0},{2,3},{3,2},{4,5},{5,4},{6,7},{7,6},{8,9},{9,8},{10,11... | collective-permute-start | bytes 393224 | tf_op jit(solution)/shard_map/ppermute | solution.py:427
  60.1 6.6 %collective-permute-start.8 = (bf16[2,2,128,128]{3,2,1,0:T(8,128)(2,1)S(1)}, bf16[2,2,128,128]{3,2,1,0:T(8,128)(2,1)S(1)}, u32[]{:S(2)}, u32[]{:S(2)}) collective-permute-start(bf16[2,2,128,128]{3,2,1,0:T(8,128)(2,1)S(1)} %collective-permute-done.7.refs_2_), channel_id=1, source_target_pairs={{0,1},{1,0},{2,3},{3,2},{4,5},{5,4},{6,7},{7,6},{8,9},{9,8},{10,11... | collective-permute-start | bytes 393224 | tf_op jit(solution)/shard_map/ppermute | solution.py:427
  67.6 5.1 %collective-permute-start.9 = (bf16[128,640]{1,0:T(8,128)(2,1)S(1)}, bf16[128,640]{1,0:T(8,128)(2,1)S(1)}, u32[]{:S(2)}, u32[]{:S(2)}) collective-permute-start(bf16[128,640]{1,0:T(8,128)(2,1)S(1)} %get-tuple-element.59), channel_id=1, source_target_pairs={{0,8},{8,0},{16,24},{24,16},{1,9},{9,1},{17,25},{25,17},{2,10},{10... | collective-permute-start | bytes 491528 | tf_op jit(solution)/shard_map/ppermute | solution.py:427
  72.8 6.4 %collective-permute-start.12 = (bf16[128,640]{1,0:T(8,128)(2,1)S(1)}, bf16[128,640]{1,0:T(8,128)(2,1)S(1)}, u32[]{:S(2)}, u32[]{:S(2)}) collective-permute-start(bf16[128,640]{1,0:T(8,128)(2,1)S(1)} %add_convert_fusion), channel_id=1, source_target_pairs={{0,20},{4,16},{8,28},{12,24},{16,4},{20,0},{24,12},{28,8},{1,21},{... | collective-permute-start | bytes 491528 | tf_op jit(solution)/shard_map/ppermute | solution.py:503
  75.0 8.4 %collective-permute-start.11 = (bf16[128,640]{1,0:T(8,128)(2,1)S(1)}, bf16[128,640]{1,0:T(8,128)(2,1)S(1)}, u32[]{:S(2)}, u32[]{:S(2)}) collective-permute-start(bf16[128,640]{1,0:T(8,128)(2,1)S(1)} %add_convert_fusion), channel_id=1, source_target_pairs={{0,16},{8,24},{16,0},{24,8},{1,17},{9,25},{17,1},{25,9},{2,18},{10... | collective-permute-start | bytes 491528 | tf_op jit(solution)/shard_map/ppermute | solution.py:427
  75.2 8.2 %collective-permute-start.10 = (bf16[128,640]{1,0:T(8,128)(2,1)S(1)}, bf16[128,640]{1,0:T(8,128)(2,1)S(1)}, u32[]{:S(2)}, u32[]{:S(2)}) collective-permute-start(bf16[128,640]{1,0:T(8,128)(2,1)S(1)} %add_convert_fusion), channel_id=1, source_target_pairs={{0,4},{4,0},{1,5},{5,1},{2,6},{6,2},{3,7},{7,3},{8,12},{12,8},{9,1... | collective-permute-start | bytes 491528 | tf_op jit(solution)/shard_map/ppermute | solution.py:427
  83.5 3.0 %collective-permute-start.13 = (bf16[128,640]{1,0:T(8,128)(2,1)S(1)}, bf16[128,640]{1,0:T(8,128)(2,1)S(1)}, u32[]{:S(2)}, u32[]{:S(2)}) collective-permute-start(bf16[128,640]{1,0:T(8,128)(2,1)S(1)} %multiply_convert_fusion.rows), channel_id=1, source_target_pairs={{0,8},{8,0},{16,24},{24,16},{1,9},{9,1},{17,25},{25,17},{2,10},{10... | collective-permute-start | bytes 491528 | tf_op jit(solution)/shard_map/ppermute | solution.py:427
  86.5 2.0 %copy-start.1 = (bf16[256,1280]{1,0:T(8,128)(2,1)S(1)}, bf16[256,1280]{1,0:T(8,128)(2,1)}, u32[]{:S(2)}) copy-start(bf16[256,1280]{1,0:T(8,128)(2,1)} %param.17) | copy-start | bytes 1966084
where the time goes:
time: 88.8 us; the launch traced here: 88.6 us
  waiting for transfers between devices  32.7 us (37%)
  starting transfers between devices  28.3 us (32%)
  Pallas kernels  16.1 us (18%)
  local copies, waits for them, and re-layouts  5.92 us (7%)
  matrix products  3.34 us (4%)
  other arithmetic  1.4 us (2%)
    ppermute x13, waiting for transfers between devices, exchange(): lax.ppermute(array, axis, [(i, i ^ bit) for i in range(lax.axis_size(axis...  29 us
    ppermute x13, starting transfers between devices, exchange(): lax.ppermute(array, axis, [(i, i ^ bit) for i in range(lax.axis_size(axis...  26.1 us
    pallas_call x1, Pallas kernels, load_part(): pl.pallas_call(load_kernel, in_specs=[smem_spec()] + [vmem_spec()] * 3 +...  5.6 us
    pallas_call x2, Pallas kernels, grad_part(): pl.pallas_call(grad_kernel, grid_spec=grid_spec, out_shape=jax.ShapeDtype...  4.09 us
    pallas_call x1, Pallas kernels, qkv_part(): pl.pallas_call(qkv_kernel, in_specs=[smem_spec()] * 4 + [vmem_spec()] * 6...  3.98 us
    ppermute x1, waiting for transfers between devices, heads_per_role(): lax.ppermute(total, ('role', 'seq'), [(i, i ^ 2 * lax.axis_size('seq') +...  3.65 us
    dynamic_slice x2, local copies, waits for them, and re-layouts, take(): lax.dynamic_slice_in_dim(array, begin, size, axis=axis, allow_negative_in...  3.37 us
    dot_general x2, matrix products, dot32(): return jnp.dot(a, b, preferred_element_type=jnp.float32)  3.34 us
  transfers between devices with their start and end apart: 14, of which 9 were waited for; matrix products, arithmetic and copies ran while one was open for 3% of the time, Pallas kernels for 9%

commit v1 on v0

--- a/solution.py
+++ b/solution.py
@@ -213,7 +213,7 @@
         out_shape=[jax.ShapeDtypeStruct((parts, depth, cols), jnp.bfloat16)] * 2
         + [jax.ShapeDtypeStruct((2, parts, 8, width), jnp.float32)],
         scratch_shapes=[pltpu.SemaphoreType.DMA((2 * parts,))],
-        compiler_params=params(46),
+        compiler_params=params(40),
         name="load_part",
     )(start, embed, time_a, time_b, planes_a, planes_b)
 
@@ -394,6 +394,46 @@
     )(core, mine, *heads, weight_a, weight_b, mods)
 
 
+def spread_kernel(place, kept, arrived, own, *sends):
+    block = own.shape[0]
+    for hop, goal in enumerate((own, *sends)):
+        at = at_block(jnp.bitwise_xor(place[0], hop), block)
+        goal[...] = (kept[at, :] + arrived[at, :].astype(jnp.float32)).astype(goal.dtype)
+
+
+def spread_part(place, kept, arrived, count):
+    length, cols = kept.shape
+    shape = (length // count, cols)
+    return pl.pallas_call(
+        spread_kernel,
+        in_specs=[smem_spec()] + [vmem_spec()] * 2,
+        out_specs=[vmem_spec()] * count,
+        out_shape=[jax.ShapeDtypeStruct(shape, jnp.float32)]
+        + [jax.ShapeDtypeStruct(shape, jnp.bfloat16)] * (count - 1),
+        compiler_params=params(8),
+        name="spread_part",
+    )(place, kept, arrived)
+
+
+def merge_kernel(place, *refs):
+    blocks, rows = refs[:-1], refs[-1]
+    size = blocks[0].shape[0]
+    for hop, block in enumerate(blocks):
+        rows[at_block(jnp.bitwise_xor(place[0], hop), size), :] = block[...]
+
+
+def merge_part(place, blocks):
+    size, cols = blocks[0].shape
+    return pl.pallas_call(
+        merge_kernel,
+        in_specs=[smem_spec()] + [vmem_spec()] * len(blocks),
+        out_specs=vmem_spec(),
+        out_shape=jax.ShapeDtypeStruct((size * len(blocks), cols), jnp.bfloat16),
+        compiler_params=params(8),
+        name="merge_part",
+    )(place, *blocks)
+
+
 def grad_kernel(half, heads_t, rows, *refs):
     refs[-1][...] = dot32(heads_t[...], rows[...]).astype(jnp.bfloat16)
 
@@ -425,6 +465,13 @@
 
 def exchange(array, axis, bit):
     return lax.ppermute(array, axis, [(i, i ^ bit) for i in range(lax.axis_size(axis))])
+
+
+def chip_exchange(arrays):
+    seqs = lax.axis_size("seq")
+    everyone = range(lax.axis_size("role") * seqs)
+    bits = (1, 2 * seqs, 2 * seqs + 1)
+    return [lax.ppermute(x, ("role", "seq"), [(i, i ^ bit) for i in everyone]) for x, bit in zip(arrays, bits)]
 
 
 def take(array, begin, size, axis):
@@ -464,10 +511,12 @@
     embed = jnp.concatenate([embed, jnp.zeros((5, freq), jnp.bfloat16)], axis=0)
     levels = steps[1:3].astype(jnp.float32) / 1000.0
     start = role * part_cols
-    scalars = [seq, mp, core, 1 - core, core * half_cols, start, start + mp * unit]
+    scalars = [seq, mp, core, 1 - core, core * half_cols, start, start + mp * unit, role // 2 * 2 + seq]
     embed, *scalars = lax.optimization_barrier((embed, *scalars))
-    seq_at, mine, core, other_core, start_at = [v.astype(jnp.int32).reshape(1) for v in scalars[:4] + scalars[5:6]]
-    begin, start, gain_at = scalars[4:]
+    seq_at, mine, core, other_core, start_at, place = [
+        v.astype(jnp.int32).reshape(1) for v in scalars[:4] + scalars[5:6] + scalars[7:]
+    ]
+    begin, start, gain_at = scalars[4:7]
     weight, time_half, resid_half, noise_half = [
         take(w, begin, half_cols, 1) for w in (gen_out_w, gen_time_w, gen_resid, noise)
     ]
@@ -497,14 +546,10 @@
     gathered = head, near, far, exchange(far, "mp", 1)
 
     kept, sent = out_part(core, mine, gathered, out_a, out_b, mods)
-    total = both(kept, exchange(sent, "role", 1)).astype(jnp.bfloat16)
-    along_x = exchange(total, "seq", 1)
-    along_y = exchange(total, "role", 2)
-    across = lax.ppermute(
-        total, ("role", "seq"), [(i, i ^ (2 * lax.axis_size("seq") + 1)) for i in range(roles * lax.axis_size("seq"))]
-    )
-    total = both(total, along_x) + both(along_y, across)
-    rows = (gate[0:1] * total).astype(jnp.bfloat16)
+    own, *sends = spread_part(place, kept, exchange(sent, "role", 1), 4)
+    arrived = chip_exchange(sends)
+    rows = (gate[0:1] * (own + arrived[0].astype(jnp.float32) + both(*arrived[1:]))).astype(jnp.bfloat16)
+    rows = merge_part(place, [rows, *chip_exchange([rows] * 3)])
     heads_t = gen_heads.T
     theirs = exchange(rows, "role", 1)
     weight_grad = grad_part(core, heads_t, rows, None, 2)

time: 88.8 us -> 89.8 us (1.011)
  starting transfers between devices: 28.3 us -> 34.1 us
  local copies, waits for them, and re-layouts: 5.92 us -> 3.81 us
  Pallas kernels: 16.1 us -> 14 us
    ppermute x1 -> x6, starting transfers between devices: 2.22 us -> 5.43 us  [chip_exchange(): lax.ppermute(x, ('role', 'seq'), [(i, i ^ bit) for i in everyone])]
    ppermute x13 -> x11, starting transfers between devices: 26.1 us -> 28.7 us  [exchange(): lax.ppermute(array, axis, [(i, i ^ bit) for i in range(lax.axis_size(axis...]
    ppermute x13 -> x11, waiting for transfers between devices: 29 us -> 26.7 us  [exchange(): lax.ppermute(array, axis, [(i, i ^ bit) for i in range(lax.axis_size(axis...]
    unnamed x21 -> x19, local copies, waits for them, and re-layouts: 2.43 us -> 0.32 us
    pallas_call x1, Pallas kernels: 5.6 us -> 3.51 us  [load_part(): pl.pallas_call(load_kernel, in_specs=[smem_spec()] + [vmem_spec()] * 3 +...]
    ppermute x1 -> x6, waiting for transfers between devices: 3.65 us -> 5.47 us  [chip_exchange(): lax.ppermute(x, ('role', 'seq'), [(i, i ^ bit) for i in everyone])]
  transfers between devices with their start and end apart: 14 -> 17, of which waited for: 9 -> 14; matrix products, arithmetic and copies ran while one was open for 3% -> 3% of each run, Pallas kernels for 9% -> 6%
where the time goes in v1:
time: 89.8 us; the launch traced here: 89.6 us
  starting transfers between devices  34.1 us (38%)
  waiting for transfers between devices  32.2 us (36%)
  Pallas kernels  14 us (16%)
  local copies, waits for them, and re-layouts  3.81 us (4%)
  matrix products  3.34 us (4%)
  other arithmetic  1.29 us (1%)
    ppermute x11, starting transfers between devices, exchange(): lax.ppermute(array, axis, [(i, i ^ bit) for i in range(lax.axis_size(axis...  28.7 us
    ppermute x11, waiting for transfers between devices, exchange(): lax.ppermute(array, axis, [(i, i ^ bit) for i in range(lax.axis_size(axis...  26.7 us
    ppermute x6, waiting for transfers between devices, chip_exchange(): lax.ppermute(x, ('role', 'seq'), [(i, i ^ bit) for i in everyone])  5.47 us
    ppermute x6, starting transfers between devices, chip_exchange(): lax.ppermute(x, ('role', 'seq'), [(i, i ^ bit) for i in everyone])  5.43 us
    pallas_call x2, Pallas kernels, grad_part(): pl.pallas_call(grad_kernel, grid_spec=grid_spec, out_shape=jax.ShapeDtype...  4.09 us
    pallas_call x1, Pallas kernels, qkv_part(): pl.pallas_call(qkv_kernel, in_specs=[smem_spec()] * 4 + [vmem_spec()] * 6...  3.99 us
    pallas_call x1, Pallas kernels, load_part(): pl.pallas_call(load_kernel, in_specs=[smem_spec()] + [vmem_spec()] * 3 +...  3.51 us
    dynamic_slice x2, local copies, waits for them, and re-layouts, take(): lax.dynamic_slice_in_dim(array, begin, size, axis=axis, allow_negative_in...  3.37 us
  transfers between devices with their start and end apart: 17, of which 14 were waited for; matrix products, arithmetic and copies ran while one was open for 3% of the time, Pallas kernels for 6%

profile of v1, /device:TPU:1, one launch (start us, length us, event | category | flops | bytes accessed | tf_op | source)
XLA Modules:
  0.0 89.6 jit_solution(13361429531292098854)
XLA Ops:
  0.6 0.0 copy-start
  0.6 0.0 copy-start.2
  0.7 0.8 convert_element_type.39
  1.5 0.1 fusion.13
  1.6 0.0 copy-start.3
  1.6 3.1 %fusion.2.product = f32[128,640]{1,0:T(8,128)S(1)} fusion(bf16[128,2048]{1,0:T(8,128)(2,1)} %param.14, bf16[2048,1280]{1,0:T(8,128)(2,1)} %param.16, s32[]{:T(128)S(6)} %mul.50), kind=kOutput, calls=%fused_computation.2 | convolution fusion | flops 335544320 | bytes 3473412 | tf_op jit(solution)/shard_map/dot_general | solution.py:144
  4.7 0.0 copy-done
  4.7 0.3 fusion.5.gate
  5.0 1.0 %constant_dynamic-slice_fusion.2 = (bf16[64,640]{1,0:T(8,128)(2,1)S(1)}, bf16[64,640]{1,0:T(8,128)(2,1)S(1)}) fusion(bf16[64,1280]{1,0:T(8,128)(2,1)} %noise.1, s32[]{:T(128)S(6)} %mul.50, bf16[64,1280]{1,0:T(8,128)(2,1)} %param.15), kind=kLoop, calls=%fused_computation.28 | loop fusion | bytes 327684 | tf_op jit(solution)/shard_map/dynamic_slice | solution.py:478
  6.0 0.1 pack_part.1
  6.1 2.1 %collective-permute-start = (bf16[192,640]{1,0:T(8,128)(2,1)S(1)}, bf16[192,640]{1,0:T(8,128)(2,1)S(1)}, u32[]{:S(2)}, u32[]{:S(2)}) collective-permute-start(bf16[192,640]{1,0:T(8,128)(2,1)S(1)} %get-tuple-element.42), channel_id=1, source_target_pairs={{0,4},{4,0},{1,5},{5,1},{2,6},{6,2},{3,7},{7,3},{8,12},{12,8},{9,1... | collective-permute-start | bytes 737288 | tf_op jit(solution)/shard_map/ppermute | solution.py:467
  8.2 0.0 copy-done.2
  8.2 0.0 copy-done.3
  8.2 3.5 %load_part.1 = (bf16[3,1280,512]{2,1,0:T(8,128)(2,1)S(1)}, bf16[3,1280,512]{2,1,0:T(8,128)(2,1)S(1)}, f32[2,3,8,1280]{3,2,1,0:T(8,128)S(1)}) custom-call(s32[1]{0:T(128)} %bitcast.4.start, bf16[8,256]{1,0:T(8,128)(2,1)S(1)} %fusion.11.embed, bf16[3,256,1280]{2,1,0:T(8,128)(2,1)S(1)} %bitcast.27, bf16[3,256,1280]{2,1,0:T(8,128)(2,1)S(1)} %bitcast.28, ...), custom_call_target="tpu_custom_call" | custom-call | tf_op jit(solution)/shard_map/load_part/pallas_call | solution.py:209
  11.8 0.0 copy-start.6
  11.8 0.0 copy-start.7
  11.8 1.9 %collective-permute-done.arrived = bf16[192,640]{1,0:T(8,128)(2,1)S(1)} collective-permute-done((bf16[192,640]{1,0:T(8,128)(2,1)S(1)}, bf16[192,640]{1,0:T(8,128)(2,1)S(1)}, u32[]{:S(2)}, u32[]{:S(2)}) %collective-permute-start) | collective-permute-done | bytes 245792 | tf_op jit(solution)/shard_map/ppermute | solution.py:467
  13.8 1.5 %collective-permute-start.1 = (bf16[192,640]{1,0:T(8,128)(2,1)S(1)}, bf16[192,640]{1,0:T(8,128)(2,1)S(1)}, u32[]{:S(2)}, u32[]{:S(2)}) collective-permute-start(bf16[192,640]{1,0:T(8,128)(2,1)S(1)} %join_part.1.joined), channel_id=1, source_target_pairs={{0,8},{8,0},{16,24},{24,16},{1,9},{9,1},{17,25},{25,17},{2,10},{10... | collective-permute-start | bytes 737288 | tf_op jit(solution)/shard_map/ppermute | solution.py:467
  15.3 0.0 copy-done.8
  15.3 0.1 convert_multiply_fusion.levels
  15.3 1.1 %collective-permute-done.1.swapped = bf16[192,640]{1,0:T(8,128)(2,1)S(1)} collective-permute-done((bf16[192,640]{1,0:T(8,128)(2,1)S(1)}, bf16[192,640]{1,0:T(8,128)(2,1)S(1)}, u32[]{:S(2)}, u32[]{:S(2)}) %collective-permute-start.1) | collective-permute-done | bytes 245792 | tf_op jit(solution)/shard_map/ppermute | solution.py:467
  16.4 0.0 copy-done.4
  16.4 4.0 %qkv_part.1 = (bf16[64,1280]{1,0:T(8,128)(2,1)}, bf16[2,272,384]{2,1,0:T(8,128)(2,1)S(1)}, bf16[2,272,384]{2,1,0:T(8,128)(2,1)S(1)}, bf16[2,272,384]{2,1,0:T(8,128)(2,1)S(1)}, bf16[2,272,384]{2,1,0:T(8,128)(2,1)S(1)}) custom-call(s32[1]{0:T(128)} %bitcast.seq, s32[1]{0:T(128)} %bitcast.1.core.half, s32[1]{0:T(128)} %bitcast.2.mine, ...), custom_call_target="tpu_custom_call" | custom-call | tf_op jit(solution)/shard_map/qkv_part/pallas_call | solution.py:297
  20.4 1.6 %collective-permute-start.2 = (bf16[2,272,384]{2,1,0:T(8,128)(2,1)S(1)}, bf16[2,272,384]{2,1,0:T(8,128)(2,1)S(1)}, u32[]{:S(2)}, u32[]{:S(2)}) collective-permute-start(bf16[2,272,384]{2,1,0:T(8,128)(2,1)S(1)} %get-tuple-element.55), channel_id=1, source_target_pairs={{0,1},{1,0},{2,3},{3,2},{4,5},{5,4},{6,7},{7,6},{8,9},{9,8},{10,11... | collective-permute-start | bytes 1253384 | tf_op jit(solution)/shard_map/ppermute | solution.py:467
  21.9 2.3 %collective-permute-start.3 = (bf16[2,272,384]{2,1,0:T(8,128)(2,1)S(1)}, bf16[2,272,384]{2,1,0:T(8,128)(2,1)S(1)}, u32[]{:S(2)}, u32[]{:S(2)}) collective-permute-start(bf16[2,272,384]{2,1,0:T(8,128)(2,1)S(1)} %get-tuple-element.56), channel_id=1, source_target_pairs={{0,2},{1,3},{2,0},{3,1},{4,6},{5,7},{6,4},{7,5},{8,10},{9,11},{10,... | collective-permute-start | bytes 1253384 | tf_op jit(solution)/shard_map/ppermute | solution.py:467
  24.3 0.0 copy-done.6
  24.3 0.1 fusion.12.refs_4_
  24.3 2.3 %constant_dynamic-slice_fusion = (bf16[512,1280]{1,0:T(8,128)(2,1)S(1)}, bf16[512,1280]{1,0:T(8,128)(2,1)S(1)}) fusion(bf16[2048,1280]{1,0:T(8,128)(2,1)} %param.25, s32[]{:T(128)} %mul.51, bf16[2048,1280]{1,0:T(8,128)(2,1)} %param.21), kind=kLoop, calls=%fused_computation.26 | loop fusion | bytes 5242884 | tf_op jit(solution)/shard_map/dynamic_slice | solution.py:478
  26.7 13.6 %collective-permute-done.2 = bf16[2,272,384]{2,1,0:T(8,128)(2,1)S(1)} collective-permute-done((bf16[2,272,384]{2,1,0:T(8,128)(2,1)S(1)}, bf16[2,272,384]{2,1,0:T(8,128)(2,1)S(1)}, u32[]{:S(2)}, u32[]{:S(2)}) %collective-permute-start.2) | collective-permute-done | bytes 417824 | tf_op jit(solution)/shard_map/ppermute | solution.py:467
  40.3 0.0 collective-permute-done.3
  40.3 0.1 convert_add_fusion.1
  40.3 0.0 copy-start.5
  40.4 2.5 %collective-permute-start.4 = (bf16[272,384]{1,0:T(8,128)(2,1)S(1)}, bf16[272,384]{1,0:T(8,128)(2,1)S(1)}, u32[]{:S(2)}, u32[]{:S(2)}) collective-permute-start(bf16[272,384]{1,0:T(8,128)(2,1)S(1)} %fusion.7), channel_id=1, source_target_pairs={{0,2},{1,3},{2,0},{3,1},{4,6},{5,7},{6,4},{7,5},{8,10},{9,11},{10,... | collective-permute-start | bytes 626696 | tf_op jit(solution)/shard_map/ppermute | solution.py:467
  42.9 0.1 convert_add_fusion
  43.1 2.2 %collective-permute-start.5 = (bf16[272,384]{1,0:T(8,128)(2,1)S(1)}, bf16[272,384]{1,0:T(8,128)(2,1)S(1)}, u32[]{:S(2)}, u32[]{:S(2)}) collective-permute-start(bf16[272,384]{1,0:T(8,128)(2,1)S(1)} %fusion.8), channel_id=1, source_target_pairs={{0,1},{1,0},{2,3},{3,2},{4,5},{5,4},{6,7},{7,6},{8,9},{9,8},{10,11... | collective-permute-start | bytes 626696 | tf_op jit(solution)/shard_map/ppermute | solution.py:467
  45.3 0.8 collective-permute-done.4.refs_1_
  46.1 4.5 %collective-permute-done.5.refs_3_ = bf16[272,384]{1,0:T(8,128)(2,1)S(1)} collective-permute-done((bf16[272,384]{1,0:T(8,128)(2,1)S(1)}, bf16[272,384]{1,0:T(8,128)(2,1)S(1)}, u32[]{:S(2)}, u32[]{:S(2)}) %collective-permute-start.5) | collective-permute-done | bytes 208928 | tf_op jit(solution)/shard_map/ppermute | solution.py:467
  50.6 1.3 %attend_part.1.refs_0_ = bf16[2,2,128,128]{3,2,1,0:T(8,128)(2,1)S(1)} custom-call(f32[272,384]{1,0:T(8,128)S(1)} %slice_bitcast_fusion.1.refs_0_, bf16[272,384]{1,0:T(8,128)(2,1)S(1)} %collective-permute-done.4.refs_1_, f32[272,384]{1,0:T(8,128)S(1)} %slice_bitcast_fusion.refs_2_, bf16[272,384]{1,0:T(8,128)(2,1)S(1)} %collective-permute-done.5.refs_3_, ...), custom_call_target="tpu_custom_call" | custom-call | tf_op jit(solution)/shard_map/attend_part/pallas_call | solution.py:346
  51.9 3.3 %collective-permute-start.7 = (bf16[2,2,128,128]{3,2,1,0:T(8,128)(2,1)S(1)}, bf16[2,2,128,128]{3,2,1,0:T(8,128)(2,1)S(1)}, u32[]{:S(2)}, u32[]{:S(2)}) collective-permute-start(bf16[2,2,128,128]{3,2,1,0:T(8,128)(2,1)S(1)} %attend_part.1.refs_0_), channel_id=1, source_target_pairs={{0,2},{1,3},{2,0},{3,1},{4,6},{5,7},{6,4},{7,5},{8,10},{9,11},{10,... | collective-permute-start | bytes 393224 | tf_op jit(solution)/shard_map/ppermute | solution.py:467
  55.2 2.8 %collective-permute-start.6 = (bf16[2,2,128,128]{3,2,1,0:T(8,128)(2,1)S(1)}, bf16[2,2,128,128]{3,2,1,0:T(8,128)(2,1)S(1)}, u32[]{:S(2)}, u32[]{:S(2)}) collective-permute-start(bf16[2,2,128,128]{3,2,1,0:T(8,128)(2,1)S(1)} %attend_part.1.refs_0_), channel_id=1, source_target_pairs={{0,1},{1,0},{2,3},{3,2},{4,5},{5,4},{6,7},{7,6},{8,9},{9,8},{10,11... | collective-permute-start | bytes 393224 | tf_op jit(solution)/shard_map/ppermute | solution.py:467
  58.0 0.0 collective-permute-done.7.refs_2_
  58.0 2.8 %collective-permute-start.8 = (bf16[2,2,128,128]{3,2,1,0:T(8,128)(2,1)S(1)}, bf16[2,2,128,128]{3,2,1,0:T(8,128)(2,1)S(1)}, u32[]{:S(2)}, u32[]{:S(2)}) collective-permute-start(bf16[2,2,128,128]{3,2,1,0:T(8,128)(2,1)S(1)} %collective-permute-done.7.refs_2_), channel_id=1, source_target_pairs={{0,1},{1,0},{2,3},{3,2},{4,5},{5,4},{6,7},{7,6},{8,9},{9,8},{10,11... | collective-permute-start | bytes 393224 | tf_op jit(solution)/shard_map/ppermute | solution.py:467
  60.7 0.5 collective-permute-done.6.refs_1_
  61.3 3.3 %collective-permute-done.8.refs_3_ = bf16[2,2,128,128]{3,2,1,0:T(8,128)(2,1)S(1)} collective-permute-done((bf16[2,2,128,128]{3,2,1,0:T(8,128)(2,1)S(1)}, bf16[2,2,128,128]{3,2,1,0:T(8,128)(2,1)S(1)}, u32[]{:S(2)}, u32[]{:S(2)}) %collective-permute-start.8) | collective-permute-done | bytes 131104 | tf_op jit(solution)/shard_map/ppermute | solution.py:467
  64.5 1.0 %out_part.1 = (f32[128,640]{1,0:T(8,128)S(1)}, bf16[128,640]{1,0:T(8,128)(2,1)S(1)}) custom-call(s32[1]{0:T(128)} %bitcast.1.core.half, s32[1]{0:T(128)} %bitcast.2.mine, bf16[2,2,128,128]{3,2,1,0:T(8,128)(2,1)S(1)} %attend_part.1.refs_0_, bf16[2,2,128,128]{3,2,1,0:T(8,128)(2,1)S(1)} %collective-permute-done.6.refs_1_, ...), custom_call_target="tpu_custom_call" | custom-call | tf_op jit(solution)/shard_map/out_part/pallas_call | solution.py:380
  65.5 4.1 %collective-permute-start.9 = (bf16[128,640]{1,0:T(8,128)(2,1)S(1)}, bf16[128,640]{1,0:T(8,128)(2,1)S(1)}, u32[]{:S(2)}, u32[]{:S(2)}) collective-permute-start(bf16[128,640]{1,0:T(8,128)(2,1)S(1)} %get-tuple-element.65), channel_id=1, source_target_pairs={{0,8},{8,0},{16,24},{24,16},{1,9},{9,1},{17,25},{25,17},{2,10},{10... | collective-permute-start | bytes 491528 | tf_op jit(solution)/shard_map/ppermute | solution.py:467
  69.7 1.0 %collective-permute-done.9.arrived = bf16[128,640]{1,0:T(8,128)(2,1)S(1)} collective-permute-done((bf16[128,640]{1,0:T(8,128)(2,1)S(1)}, bf16[128,640]{1,0:T(8,128)(2,1)S(1)}, u32[]{:S(2)}, u32[]{:S(2)}) %collective-permute-start.9) | collective-permute-done | bytes 163872 | tf_op jit(solution)/shard_map/ppermute | solution.py:467
  70.7 2.2 %collective-permute-start.12 = (bf16[32,640]{1,0:T(8,128)(2,1)S(1)}, bf16[32,640]{1,0:T(8,128)(2,1)S(1)}, u32[]{:S(2)}, u32[]{:S(2)}) collective-permute-start(bf16[32,640]{1,0:T(8,128)(2,1)S(1)} %get-tuple-element.69), channel_id=1, source_target_pairs={{0,20},{4,16},{8,28},{12,24},{16,4},{20,0},{24,12},{28,8},{1,21},{... | collective-permute-start | bytes 122888 | tf_op jit(solution)/shard_map/ppermute | solution.py:474
  72.9 0.2 collective-permute-start.11
  73.1 0.3 collective-permute-start.10
  73.5 1.1 %collective-permute-done.12 = bf16[32,640]{1,0:T(8,128)(2,1)S(1)} collective-permute-done((bf16[32,640]{1,0:T(8,128)(2,1)S(1)}, bf16[32,640]{1,0:T(8,128)(2,1)S(1)}, u32[]{:S(2)}, u32[]{:S(2)}) %collective-permute-start.12) | collective-permute-done | bytes 40992 | tf_op jit(solution)/shard_map/ppermute | solution.py:474
  74.5 1.3 %collective-permute-done.11 = bf16[32,640]{1,0:T(8,128)(2,1)S(1)} collective-permute-done((bf16[32,640]{1,0:T(8,128)(2,1)S(1)}, bf16[32,640]{1,0:T(8,128)(2,1)S(1)}, u32[]{:S(2)}, u32[]{:S(2)}) %collective-permute-start.11) | collective-permute-done | bytes 40992 | tf_op jit(solution)/shard_map/ppermute | solution.py:474
  75.8 0.2 collective-permute-done.10
  76.0 0.9 %collective-permute-start.13 = (bf16[32,640]{1,0:T(8,128)(2,1)S(1)}, bf16[32,640]{1,0:T(8,128)(2,1)S(1)}, u32[]{:S(2)}, u32[]{:S(2)}) collective-permute-start(bf16[32,640]{1,0:T(8,128)(2,1)S(1)} %multiply_convert_fusion.refs_0_), channel_id=1, source_target_pairs={{0,4},{4,0},{8,12},{12,8},{16,20},{20,16},{24,28},{28,24},{1,5},{5... | collective-permute-start | bytes 122888 | tf_op jit(solution)/shard_map/ppermute | solution.py:474
  76.9 1.0 %collective-permute-start.14 = (bf16[32,640]{1,0:T(8,128)(2,1)S(1)}, bf16[32,640]{1,0:T(8,128)(2,1)S(1)}, u32[]{:S(2)}, u32[]{:S(2)}) collective-permute-start(bf16[32,640]{1,0:T(8,128)(2,1)S(1)} %multiply_convert_fusion.refs_0_), channel_id=1, source_target_pairs={{0,16},{4,20},{8,24},{12,28},{16,0},{20,4},{24,8},{28,12},{1,17},{... | collective-permute-start | bytes 122888 | tf_op jit(solution)/shard_map/ppermute | solution.py:474
  77.9 0.8 collective-permute-start.15
  78.7 0.2 collective-permute-done.13.refs_1_
  78.9 0.8 collective-permute-done.14.refs_2_
  79.8 1.9 %collective-permute-done.15.refs_3_ = bf16[32,640]{1,0:T(8,128)(2,1)S(1)} collective-permute-done((bf16[32,640]{1,0:T(8,128)(2,1)S(1)}, bf16[32,640]{1,0:T(8,128)(2,1)S(1)}, u32[]{:S(2)}, u32[]{:S(2)}) %collective-permute-start.15) | collective-permute-done | bytes 40992 | tf_op jit(solution)/shard_map/ppermute | solution.py:474
  81.7 3.6 %collective-permute-start.16 = (bf16[128,640]{1,0:T(8,128)(2,1)S(1)}, bf16[128,640]{1,0:T(8,128)(2,1)S(1)}, u32[]{:S(2)}, u32[]{:S(2)}) collective-permute-start(bf16[128,640]{1,0:T(8,128)(2,1)S(1)} %merge_part.1.rows), channel_id=1, source_target_pairs={{0,8},{8,0},{16,24},{24,16},{1,9},{9,1},{17,25},{25,17},{2,10},{10... | collective-permute-start | bytes 491528 | tf_op jit(solution)/shard_map/ppermute | solution.py:467
  85.2 0.3 copy.18
  85.5 2.1 %grad_part.2.refs_0_ = bf16[2048,1280]{1,0:T(8,128)(2,1)} custom-call(s32[1]{0:T(128)} %bitcast.1.core.half, bf16[2048,128]{1,0:T(8,128)(2,1)S(1)} %bitcast.25, bf16[128,640]{1,0:T(8,128)(2,1)S(1)} %merge_part.1.rows), custom_call_target="tpu_custom_call" | custom-call | tf_op jit(solution)/shard_map/grad_part/pallas_call | solution.py:456
  87.6 0.0 collective-permute-done.16.rows
  87.6 2.0 %grad_part.3 = bf16[2048,1280]{1,0:T(8,128)(2,1)} custom-call(s32[1]{0:T(128)} %bitcast.9.half, bf16[2048,128]{1,0:T(8,128)(2,1)S(1)} %bitcast.26, bf16[128,640]{1,0:T(8,128)(2,1)S(1)} %collective-permute-done.16.rows, bf16[2048,1280]{1,0:T(8,128)(2,1)} %grad_part.2.refs_0_), custom_call_target="tpu_custom_call", output_to_operand_aliasing={{}: (3, {})} | custom-call | tf_op jit(solution)/shard_map/grad_part/pallas_call | solution.py:456
  (17 shorter events, 0.3 us)
Async XLA Ops:
  0.6 4.1 %copy-start = (bf16[256,1280]{1,0:T(8,128)(2,1)S(1)}, bf16[256,1280]{1,0:T(8,128)(2,1)}, u32[]{:S(2)}) copy-start(bf16[256,1280]{1,0:T(8,128)(2,1)} %param.17) | copy-start | bytes 1966084
  0.6 7.6 %copy-start.2 = (bf16[256,3,1280]{2,0,1:T(8,128)(2,1)S(1)}, bf16[256,3,1280]{2,0,1:T(8,128)(2,1)}, u32[]{:S(2)}) copy-start(bf16[256,3,1280]{2,0,1:T(8,128)(2,1)} %param.22) | copy-start | bytes 5898244
  1.6 6.6 %copy-start.3 = (bf16[256,3,1280]{2,0,1:T(8,128)(2,1)S(1)}, bf16[256,3,1280]{2,0,1:T(8,128)(2,1)}, u32[]{:S(2)}) copy-start(bf16[256,3,1280]{2,0,1:T(8,128)(2,1)} %param.26) | copy-start | bytes 5898244
  6.1 7.6 %collective-permute-start = (bf16[192,640]{1,0:T(8,128)(2,1)S(1)}, bf16[192,640]{1,0:T(8,128)(2,1)S(1)}, u32[]{:S(2)}, u32[]{:S(2)}) collective-permute-start(bf16[192,640]{1,0:T(8,128)(2,1)S(1)} %get-tuple-element.42), channel_id=1, source_target_pairs={{0,4},{4,0},{1,5},{5,1},{2,6},{6,2},{3,7},{7,3},{8,12},{12,8},{9,1... | collective-permute-start | bytes 737288 | tf_op jit(solution)/shard_map/ppermute | solution.py:467
  8.2 7.0 %copy-start.8 = (s32[3]{0:T(128)S(1)}, s32[3]{0:T(128)}, u32[]{:S(2)}) copy-start(s32[3]{0:T(128)} %param.19) | copy-start | bytes 40
  8.2 8.2 %copy-start.4 = (bf16[64,1280]{1,0:T(8,128)(2,1)S(1)}, bf16[64,1280]{1,0:T(8,128)(2,1)}, u32[]{:S(2)}) copy-start(bf16[64,1280]{1,0:T(8,128)(2,1)} %noise.1) | copy-start | bytes 491524
  11.8 12.5 %copy-start.6 = (f32[2,2048]{1,0:T(2,128)S(1)}, f32[2,2048]{1,0:T(2,128)}, u32[]{:S(2)}) copy-start(f32[2,2048]{1,0:T(2,128)} %param.23) | copy-start | bytes 49156
  11.8 12.5 %copy-start.7 = (f32[2,2048]{1,0:T(2,128)S(1)}, f32[2,2048]{1,0:T(2,128)}, u32[]{:S(2)}) copy-start(f32[2,2048]{1,0:T(2,128)} %param.27) | copy-start | bytes 49156
  13.8 2.6 %collective-permute-start.1 = (bf16[192,640]{1,0:T(8,128)(2,1)S(1)}, bf16[192,640]{1,0:T(8,128)(2,1)S(1)}, u32[]{:S(2)}, u32[]{:S(2)}) collective-permute-start(bf16[192,640]{1,0:T(8,128)(2,1)S(1)} %join_part.1.joined), channel_id=1, source_target_pairs={{0,8},{8,0},{16,24},{24,16},{1,9},{9,1},{17,25},{25,17},{2,10},{10... | collective-permute-start | bytes 737288 | tf_op jit(solution)/shard_map/ppermute | solution.py:467
  20.4 19.9 %collective-permute-start.2 = (bf16[2,272,384]{2,1,0:T(8,128)(2,1)S(1)}, bf16[2,272,384]{2,1,0:T(8,128)(2,1)S(1)}, u32[]{:S(2)}, u32[]{:S(2)}) collective-permute-start(bf16[2,272,384]{2,1,0:T(8,128)(2,1)S(1)} %get-tuple-element.55), channel_id=1, source_target_pairs={{0,1},{1,0},{2,3},{3,2},{4,5},{5,4},{6,7},{7,6},{8,9},{9,8},{10,11... | collective-permute-start | bytes 1253384 | tf_op jit(solution)/shard_map/ppermute | solution.py:467
  21.9 18.3 %collective-permute-start.3 = (bf16[2,272,384]{2,1,0:T(8,128)(2,1)S(1)}, bf16[2,272,384]{2,1,0:T(8,128)(2,1)S(1)}, u32[]{:S(2)}, u32[]{:S(2)}) collective-permute-start(bf16[2,272,384]{2,1,0:T(8,128)(2,1)S(1)} %get-tuple-element.56), channel_id=1, source_target_pairs={{0,2},{1,3},{2,0},{3,1},{4,6},{5,7},{6,4},{7,5},{8,10},{9,11},{10,... | collective-permute-start | bytes 1253384 | tf_op jit(solution)/shard_map/ppermute | solution.py:467
  40.3 44.9 %copy-start.5 = (bf16[128,2048]{1,0:T(8,128)(2,1)S(1)}, bf16[128,2048]{1,0:T(8,128)(2,1)}, u32[]{:S(2)}) copy-start(bf16[128,2048]{1,0:T(8,128)(2,1)} %param.14) | copy-start | bytes 1572868
  40.4 5.7 %collective-permute-start.4 = (bf16[272,384]{1,0:T(8,128)(2,1)S(1)}, bf16[272,384]{1,0:T(8,128)(2,1)S(1)}, u32[]{:S(2)}, u32[]{:S(2)}) collective-permute-start(bf16[272,384]{1,0:T(8,128)(2,1)S(1)} %fusion.7), channel_id=1, source_target_pairs={{0,2},{1,3},{2,0},{3,1},{4,6},{5,7},{6,4},{7,5},{8,10},{9,11},{10,... | collective-permute-start | bytes 626696 | tf_op jit(solution)/shard_map/ppermute | solution.py:467
  43.1 7.6 %collective-permute-start.5 = (bf16[272,384]{1,0:T(8,128)(2,1)S(1)}, bf16[272,384]{1,0:T(8,128)(2,1)S(1)}, u32[]{:S(2)}, u32[]{:S(2)}) collective-permute-start(bf16[272,384]{1,0:T(8,128)(2,1)S(1)} %fusion.8), channel_id=1, source_target_pairs={{0,1},{1,0},{2,3},{3,2},{4,5},{5,4},{6,7},{7,6},{8,9},{9,8},{10,11... | collective-permute-start | bytes 626696 | tf_op jit(solution)/shard_map/ppermute | solution.py:467
  51.9 6.0 %collective-permute-start.7 = (bf16[2,2,128,128]{3,2,1,0:T(8,128)(2,1)S(1)}, bf16[2,2,128,128]{3,2,1,0:T(8,128)(2,1)S(1)}, u32[]{:S(2)}, u32[]{:S(2)}) collective-permute-start(bf16[2,2,128,128]{3,2,1,0:T(8,128)(2,1)S(1)} %attend_part.1.refs_0_), channel_id=1, source_target_pairs={{0,2},{1,3},{2,0},{3,1},{4,6},{5,7},{6,4},{7,5},{8,10},{9,11},{10,... | collective-permute-start | bytes 393224 | tf_op jit(solution)/shard_map/ppermute | solution.py:467
  55.2 6.1 %collective-permute-start.6 = (bf16[2,2,128,128]{3,2,1,0:T(8,128)(2,1)S(1)}, bf16[2,2,128,128]{3,2,1,0:T(8,128)(2,1)S(1)}, u32[]{:S(2)}, u32[]{:S(2)}) collective-permute-start(bf16[2,2,128,128]{3,2,1,0:T(8,128)(2,1)S(1)} %attend_part.1.refs_0_), channel_id=1, source_target_pairs={{0,1},{1,0},{2,3},{3,2},{4,5},{5,4},{6,7},{7,6},{8,9},{9,8},{10,11... | collective-permute-start | bytes 393224 | tf_op jit(solution)/shard_map/ppermute | solution.py:467
  58.0 6.6 %collective-permute-start.8 = (bf16[2,2,128,128]{3,2,1,0:T(8,128)(2,1)S(1)}, bf16[2,2,128,128]{3,2,1,0:T(8,128)(2,1)S(1)}, u32[]{:S(2)}, u32[]{:S(2)}) collective-permute-start(bf16[2,2,128,128]{3,2,1,0:T(8,128)(2,1)S(1)} %collective-permute-done.7.refs_2_), channel_id=1, source_target_pairs={{0,1},{1,0},{2,3},{3,2},{4,5},{5,4},{6,7},{7,6},{8,9},{9,8},{10,11... | collective-permute-start | bytes 393224 | tf_op jit(solution)/shard_map/ppermute | solution.py:467
  65.5 5.1 %collective-permute-start.9 = (bf16[128,640]{1,0:T(8,128)(2,1)S(1)}, bf16[128,640]{1,0:T(8,128)(2,1)S(1)}, u32[]{:S(2)}, u32[]{:S(2)}) collective-permute-start(bf16[128,640]{1,0:T(8,128)(2,1)S(1)} %get-tuple-element.65), channel_id=1, source_target_pairs={{0,8},{8,0},{16,24},{24,16},{1,9},{9,1},{17,25},{25,17},{2,10},{10... | collective-permute-start | bytes 491528 | tf_op jit(solution)/shard_map/ppermute | solution.py:467
  70.7 3.8 %collective-permute-start.12 = (bf16[32,640]{1,0:T(8,128)(2,1)S(1)}, bf16[32,640]{1,0:T(8,128)(2,1)S(1)}, u32[]{:S(2)}, u32[]{:S(2)}) collective-permute-start(bf16[32,640]{1,0:T(8,128)(2,1)S(1)} %get-tuple-element.69), channel_id=1, source_target_pairs={{0,20},{4,16},{8,28},{12,24},{16,4},{20,0},{24,12},{28,8},{1,21},{... | collective-permute-start | bytes 122888 | tf_op jit(solution)/shard_map/ppermute | solution.py:474
  72.9 2.9 %collective-permute-start.11 = (bf16[32,640]{1,0:T(8,128)(2,1)S(1)}, bf16[32,640]{1,0:T(8,128)(2,1)S(1)}, u32[]{:S(2)}, u32[]{:S(2)}) collective-permute-start(bf16[32,640]{1,0:T(8,128)(2,1)S(1)} %get-tuple-element.68), channel_id=1, source_target_pairs={{0,16},{4,20},{8,24},{12,28},{16,0},{20,4},{24,8},{28,12},{1,17},{... | collective-permute-start | bytes 122888 | tf_op jit(solution)/shard_map/ppermute | solution.py:474
  73.1 2.9 %collective-permute-start.10 = (bf16[32,640]{1,0:T(8,128)(2,1)S(1)}, bf16[32,640]{1,0:T(8,128)(2,1)S(1)}, u32[]{:S(2)}, u32[]{:S(2)}) collective-permute-start(bf16[32,640]{1,0:T(8,128)(2,1)S(1)} %get-tuple-element.67), channel_id=1, source_target_pairs={{0,4},{4,0},{8,12},{12,8},{16,20},{20,16},{24,28},{28,24},{1,5},{5... | collective-permute-start | bytes 122888 | tf_op jit(solution)/shard_map/ppermute | solution.py:474
  76.0 2.9 %collective-permute-start.13 = (bf16[32,640]{1,0:T(8,128)(2,1)S(1)}, bf16[32,640]{1,0:T(8,128)(2,1)S(1)}, u32[]{:S(2)}, u32[]{:S(2)}) collective-permute-start(bf16[32,640]{1,0:T(8,128)(2,1)S(1)} %multiply_convert_fusion.refs_0_), channel_id=1, source_target_pairs={{0,4},{4,0},{8,12},{12,8},{16,20},{20,16},{24,28},{28,24},{1,5},{5... | collective-permute-start | bytes 122888 | tf_op jit(solution)/shard_map/ppermute | solution.py:474
  76.9 2.9 %collective-permute-start.14 = (bf16[32,640]{1,0:T(8,128)(2,1)S(1)}, bf16[32,640]{1,0:T(8,128)(2,1)S(1)}, u32[]{:S(2)}, u32[]{:S(2)}) collective-permute-start(bf16[32,640]{1,0:T(8,128)(2,1)S(1)} %multiply_convert_fusion.refs_0_), channel_id=1, source_target_pairs={{0,16},{4,20},{8,24},{12,28},{16,0},{20,4},{24,8},{28,12},{1,17},{... | collective-permute-start | bytes 122888 | tf_op jit(solution)/shard_map/ppermute | solution.py:474
  77.9 3.8 %collective-permute-start.15 = (bf16[32,640]{1,0:T(8,128)(2,1)S(1)}, bf16[32,640]{1,0:T(8,128)(2,1)S(1)}, u32[]{:S(2)}, u32[]{:S(2)}) collective-permute-start(bf16[32,640]{1,0:T(8,128)(2,1)S(1)} %multiply_convert_fusion.refs_0_), channel_id=1, source_target_pairs={{0,20},{4,16},{8,28},{12,24},{16,4},{20,0},{24,12},{28,8},{1,21},{... | collective-permute-start | bytes 122888 | tf_op jit(solution)/shard_map/ppermute | solution.py:474
  81.7 5.9 %collective-permute-start.16 = (bf16[128,640]{1,0:T(8,128)(2,1)S(1)}, bf16[128,640]{1,0:T(8,128)(2,1)S(1)}, u32[]{:S(2)}, u32[]{:S(2)}) collective-permute-start(bf16[128,640]{1,0:T(8,128)(2,1)S(1)} %merge_part.1.rows), channel_id=1, source_target_pairs={{0,8},{8,0},{16,24},{24,16},{1,9},{9,1},{17,25},{25,17},{2,10},{10... | collective-permute-start | bytes 491528 | tf_op jit(solution)/shard_map/ppermute | solution.py:467
  87.6 2.0 %copy-start.1 = (bf16[256,1280]{1,0:T(8,128)(2,1)S(1)}, bf16[256,1280]{1,0:T(8,128)(2,1)}, u32[]{:S(2)}) copy-start(bf16[256,1280]{1,0:T(8,128)(2,1)} %param.17) | copy-start | bytes 1966084

commit v2 on v0

--- a/solution.py
+++ b/solution.py
@@ -213,7 +213,7 @@
         out_shape=[jax.ShapeDtypeStruct((parts, depth, cols), jnp.bfloat16)] * 2
         + [jax.ShapeDtypeStruct((2, parts, 8, width), jnp.float32)],
         scratch_shapes=[pltpu.SemaphoreType.DMA((2 * parts,))],
-        compiler_params=params(46),
+        compiler_params=params(40),
         name="load_part",
     )(start, embed, time_a, time_b, planes_a, planes_b)
 
@@ -286,7 +286,7 @@
     sums = jnp.sum(wide * wide, axis=1, keepdims=True)
     sums = jnp.broadcast_to(sums, (tokens, length)).T[0:8]
     for index, weight in enumerate((weight_a, weight_b)):
-        project(index, index + 1, mine[0], mixed, sums, mods, weight, *chunks[2 * index : 2 * index + 2], result)
+        project(index, 2 - index, mine[0], mixed, sums, mods, weight, *chunks[2 * index : 2 * index + 2], result)
 
 
 def qkv_part(seq, core, mine, levels, joined, swapped, noise, mods, weight_a, weight_b):
@@ -465,7 +465,7 @@
     levels = steps[1:3].astype(jnp.float32) / 1000.0
     start = role * part_cols
     scalars = [seq, mp, core, 1 - core, core * half_cols, start, start + mp * unit]
-    embed, *scalars = lax.optimization_barrier((embed, *scalars))
+    gen_heads, *scalars = lax.optimization_barrier((gen_heads, *scalars))
     seq_at, mine, core, other_core, start_at = [v.astype(jnp.int32).reshape(1) for v in scalars[:4] + scalars[5:6]]
     begin, start, gain_at = scalars[4:]
     weight, time_half, resid_half, noise_half = [
@@ -484,14 +484,16 @@
     latent, kept_a, sent_a, kept_b, sent_b = qkv_part(
         seq_at, core, mine, levels, joined, swapped, noise, mods, weight_a, weight_b
     )
-    arrived_a, arrived_b = exchange(sent_a, "mp", 1), exchange(sent_b, "mp", 2)
+    arrived_a, arrived_b = exchange(sent_a, "mp", 2), exchange(sent_b, "mp", 1)
     out_a, out_b = [take(w, start, part_cols, 0) for w in (teacher_out, critic_out)]
     gains = jnp.stack([teacher_norm, critic_norm])
     gains = take(gains, gain_at, unit, 2)
     arrived_a, arrived_b, out_a, out_b, gains = lax.optimization_barrier((arrived_a, arrived_b, out_a, out_b, gains))
-    sum_a, sum_b = both(kept_a, arrived_a), both(kept_b, arrived_b)
-    last_a = exchange(sum_a[1].astype(jnp.bfloat16), "mp", 2)
-    last_b = exchange(sum_b[1].astype(jnp.bfloat16), "mp", 1)
+    sum_b = both(kept_b, arrived_b)
+    send_b, arrived_a = lax.optimization_barrier((sum_b[1].astype(jnp.bfloat16), arrived_a))
+    last_b = exchange(send_b, "mp", 2)
+    sum_a = both(kept_a, arrived_a)
+    last_a = exchange(sum_a[1].astype(jnp.bfloat16), "mp", 1)
     head = attend_part(sum_a[0], last_a, sum_b[0], last_b, gains, D)
     near, far = exchange(head, "mp", 1), exchange(head, "mp", 2)
     gathered = head, near, far, exchange(far, "mp", 1)

time: 88.8 us -> 88.4 us (level)
  Pallas kernels: 16.1 us -> 13.9 us
  local copies, waits for them, and re-layouts: 5.92 us -> 3.82 us
  waiting for transfers between devices: 32.7 us -> 34.7 us
  starting transfers between devices: 28.3 us -> 29.9 us
    unnamed x21 -> x18, local copies, waits for them, and re-layouts: 2.43 us -> 0.06 us
    pallas_call x1, Pallas kernels: 5.6 us -> 3.5 us  [load_part(): pl.pallas_call(load_kernel, in_specs=[smem_spec()] + [vmem_spec()] * 3 +...]
    ppermute x13, waiting for transfers between devices: 29 us -> 31 us  [exchange(): lax.ppermute(array, axis, [(i, i ^ bit) for i in range(lax.axis_size(axis...]
    ppermute x13, starting transfers between devices: 26.1 us -> 27.7 us  [exchange(): lax.ppermute(array, axis, [(i, i ^ bit) for i in range(lax.axis_size(axis...]
  transfers between devices with their start and end apart: 14 -> 14, of which waited for: 9 -> 8; matrix products, arithmetic and copies ran while one was open for 3% -> 3% of each run, Pallas kernels for 9% -> 6%
where the time goes in v2:
time: 88.4 us; the launch traced here: 88.2 us
  waiting for transfers between devices  34.7 us (39%)
  starting transfers between devices  29.9 us (34%)
  Pallas kernels  13.9 us (16%)
  local copies, waits for them, and re-layouts  3.82 us (4%)
  matrix products  3.58 us (4%)
  other arithmetic  1.39 us (2%)
    ppermute x13, waiting for transfers between devices, exchange(): lax.ppermute(array, axis, [(i, i ^ bit) for i in range(lax.axis_size(axis...  31 us
    ppermute x13, starting transfers between devices, exchange(): lax.ppermute(array, axis, [(i, i ^ bit) for i in range(lax.axis_size(axis...  27.7 us
    pallas_call x2, Pallas kernels, grad_part(): pl.pallas_call(grad_kernel, grid_spec=grid_spec, out_shape=jax.ShapeDtype...  4.09 us
    pallas_call x1, Pallas kernels, qkv_part(): pl.pallas_call(qkv_kernel, in_specs=[smem_spec()] * 4 + [vmem_spec()] * 6...  3.98 us
    ppermute x1, waiting for transfers between devices, heads_per_role(): lax.ppermute(total, ('role', 'seq'), [(i, i ^ 2 * lax.axis_size('seq') +...  3.65 us
    dot_general x2, matrix products, dot32(): return jnp.dot(a, b, preferred_element_type=jnp.float32)  3.58 us
    pallas_call x1, Pallas kernels, load_part(): pl.pallas_call(load_kernel, in_specs=[smem_spec()] + [vmem_spec()] * 3 +...  3.5 us
    dynamic_slice x2, local copies, waits for them, and re-layouts, take(): lax.dynamic_slice_in_dim(array, begin, size, axis=axis, allow_negative_in...  3.38 us
  transfers between devices with their start and end apart: 14, of which 8 were waited for; matrix products, arithmetic and copies ran while one was open for 3% of the time, Pallas kernels for 6%

profile of v2, /device:TPU:1, one launch (start us, length us, event | category | flops | bytes accessed | tf_op | source)
XLA Modules:
  0.0 88.2 jit_solution(9689033111805206567)
XLA Ops:
  0.6 0.0 copy-start
  0.6 0.0 copy-start.2
  0.7 0.0 copy-start.3
  0.7 0.8 convert_element_type.49
  1.5 0.1 fusion.10
  1.6 3.3 %fusion.product = f32[128,640]{1,0:T(8,128)S(1)} fusion(bf16[128,2048]{1,0:T(8,128)(2,1)} %param.14, bf16[2048,1280]{1,0:T(8,128)(2,1)} %param.16, s32[]{:T(128)S(6)} %mul.42), kind=kOutput, calls=%fused_computation | convolution fusion | flops 335544320 | bytes 3473412 | tf_op jit(solution)/shard_map/dot_general | solution.py:144
  4.9 1.0 %constant_dynamic-slice_fusion.2 = (bf16[64,640]{1,0:T(8,128)(2,1)S(1)}, bf16[64,640]{1,0:T(8,128)(2,1)S(1)}) fusion(bf16[64,1280]{1,0:T(8,128)(2,1)} %noise.1, s32[]{:T(128)S(6)} %mul.42, bf16[64,1280]{1,0:T(8,128)(2,1)} %param.15), kind=kLoop, calls=%fused_computation.28 | loop fusion | bytes 327684 | tf_op jit(solution)/shard_map/dynamic_slice | solution.py:431
  6.0 0.0 copy-done
  6.0 0.3 fusion.2.gate
  6.3 0.1 pack_part.1
  6.4 2.1 %collective-permute-start = (bf16[192,640]{1,0:T(8,128)(2,1)S(1)}, bf16[192,640]{1,0:T(8,128)(2,1)S(1)}, u32[]{:S(2)}, u32[]{:S(2)}) collective-permute-start(bf16[192,640]{1,0:T(8,128)(2,1)S(1)} %get-tuple-element.39), channel_id=1, source_target_pairs={{0,4},{4,0},{1,5},{5,1},{2,6},{6,2},{3,7},{7,3},{8,12},{12,8},{9,1... | collective-permute-start | bytes 737288 | tf_op jit(solution)/shard_map/ppermute | solution.py:427
  8.5 0.0 copy-done.2
  8.5 0.0 copy-done.3
  8.5 0.0 copy-start.8
  8.5 0.0 copy-start.4
  8.5 3.5 %load_part.1 = (bf16[3,1280,512]{2,1,0:T(8,128)(2,1)S(1)}, bf16[3,1280,512]{2,1,0:T(8,128)(2,1)S(1)}, f32[2,3,8,1280]{3,2,1,0:T(8,128)S(1)}) custom-call(s32[1]{0:T(128)} %bitcast.3.start, bf16[8,256]{1,0:T(8,128)(2,1)S(1)} %fusion.8.embed, bf16[3,256,1280]{2,1,0:T(8,128)(2,1)S(1)} %bitcast.23, bf16[3,256,1280]{2,1,0:T(8,128)(2,1)S(1)} %bitcast.24, ...), custom_call_target="tpu_custom_call" | custom-call | tf_op jit(solution)/shard_map/load_part/pallas_call | solution.py:209
  12.0 0.0 copy-start.6
  12.0 0.0 copy-start.7
  12.1 1.9 %collective-permute-done.arrived = bf16[192,640]{1,0:T(8,128)(2,1)S(1)} collective-permute-done((bf16[192,640]{1,0:T(8,128)(2,1)S(1)}, bf16[192,640]{1,0:T(8,128)(2,1)S(1)}, u32[]{:S(2)}, u32[]{:S(2)}) %collective-permute-start) | collective-permute-done | bytes 245792 | tf_op jit(solution)/shard_map/ppermute | solution.py:427
  14.0 1.5 %collective-permute-start.1 = (bf16[192,640]{1,0:T(8,128)(2,1)S(1)}, bf16[192,640]{1,0:T(8,128)(2,1)S(1)}, u32[]{:S(2)}, u32[]{:S(2)}) collective-permute-start(bf16[192,640]{1,0:T(8,128)(2,1)S(1)} %join_part.1.joined), channel_id=1, source_target_pairs={{0,8},{8,0},{16,24},{24,16},{1,9},{9,1},{17,25},{25,17},{2,10},{10... | collective-permute-start | bytes 737288 | tf_op jit(solution)/shard_map/ppermute | solution.py:427
  15.5 0.0 copy-done.8
  15.5 0.1 convert_multiply_fusion.levels
  15.6 1.1 %collective-permute-done.1.swapped = bf16[192,640]{1,0:T(8,128)(2,1)S(1)} collective-permute-done((bf16[192,640]{1,0:T(8,128)(2,1)S(1)}, bf16[192,640]{1,0:T(8,128)(2,1)S(1)}, u32[]{:S(2)}, u32[]{:S(2)}) %collective-permute-start.1) | collective-permute-done | bytes 245792 | tf_op jit(solution)/shard_map/ppermute | solution.py:427
  16.6 0.0 copy-done.4
  16.6 4.0 %qkv_part.1 = (bf16[64,1280]{1,0:T(8,128)(2,1)}, bf16[2,272,384]{2,1,0:T(8,128)(2,1)S(1)}, bf16[2,272,384]{2,1,0:T(8,128)(2,1)S(1)}, bf16[2,272,384]{2,1,0:T(8,128)(2,1)S(1)}, bf16[2,272,384]{2,1,0:T(8,128)(2,1)S(1)}) custom-call(s32[1]{0:T(128)} %bitcast.seq, s32[1]{0:T(128)} %bitcast.1.core.half, s32[1]{0:T(128)} %bitcast.2.mine, ...), custom_call_target="tpu_custom_call" | custom-call | tf_op jit(solution)/shard_map/qkv_part/pallas_call | solution.py:297
  20.6 2.6 %collective-permute-start.2 = (bf16[2,272,384]{2,1,0:T(8,128)(2,1)S(1)}, bf16[2,272,384]{2,1,0:T(8,128)(2,1)S(1)}, u32[]{:S(2)}, u32[]{:S(2)}) collective-permute-start(bf16[2,272,384]{2,1,0:T(8,128)(2,1)S(1)} %get-tuple-element.52), channel_id=1, source_target_pairs={{0,2},{1,3},{2,0},{3,1},{4,6},{5,7},{6,4},{7,5},{8,10},{9,11},{10,... | collective-permute-start | bytes 1253384 | tf_op jit(solution)/shard_map/ppermute | solution.py:427
  23.2 1.3 %collective-permute-start.3 = (bf16[2,272,384]{2,1,0:T(8,128)(2,1)S(1)}, bf16[2,272,384]{2,1,0:T(8,128)(2,1)S(1)}, u32[]{:S(2)}, u32[]{:S(2)}) collective-permute-start(bf16[2,272,384]{2,1,0:T(8,128)(2,1)S(1)} %get-tuple-element.53), channel_id=1, source_target_pairs={{0,1},{1,0},{2,3},{3,2},{4,5},{5,4},{6,7},{7,6},{8,9},{9,8},{10,11... | collective-permute-start | bytes 1253384 | tf_op jit(solution)/shard_map/ppermute | solution.py:427
  24.5 0.0 copy-done.6
  24.5 0.0 copy-done.7
  24.5 0.1 fusion.9.refs_4_
  24.6 2.3 %constant_dynamic-slice_fusion = (bf16[512,1280]{1,0:T(8,128)(2,1)S(1)}, bf16[512,1280]{1,0:T(8,128)(2,1)S(1)}) fusion(bf16[2048,1280]{1,0:T(8,128)(2,1)} %param.25, s32[]{:T(128)} %mul.43, bf16[2048,1280]{1,0:T(8,128)(2,1)} %param.21), kind=kLoop, calls=%fused_computation.26 | loop fusion | bytes 5242884 | tf_op jit(solution)/shard_map/dynamic_slice | solution.py:431
  26.9 14.9 %collective-permute-done.2 = bf16[2,272,384]{2,1,0:T(8,128)(2,1)S(1)} collective-permute-done((bf16[2,272,384]{2,1,0:T(8,128)(2,1)S(1)}, bf16[2,272,384]{2,1,0:T(8,128)(2,1)S(1)}, u32[]{:S(2)}, u32[]{:S(2)}) %collective-permute-start.2) | collective-permute-done | bytes 417824 | tf_op jit(solution)/shard_map/ppermute | solution.py:427
  41.8 0.0 collective-permute-done.3
  41.8 0.1 convert_add_fusion.1
  41.9 0.0 copy-start.5
  41.9 0.1 convert_add_fusion
  42.1 1.3 %collective-permute-start.4 = (bf16[272,384]{1,0:T(8,128)(2,1)S(1)}, bf16[272,384]{1,0:T(8,128)(2,1)S(1)}, u32[]{:S(2)}, u32[]{:S(2)}) collective-permute-start(bf16[272,384]{1,0:T(8,128)(2,1)S(1)} %fusion.5), channel_id=1, source_target_pairs={{0,1},{1,0},{2,3},{3,2},{4,5},{5,4},{6,7},{7,6},{8,9},{9,8},{10,11... | collective-permute-start | bytes 626696 | tf_op jit(solution)/shard_map/ppermute | solution.py:427
  43.4 2.8 %collective-permute-start.5 = (bf16[272,384]{1,0:T(8,128)(2,1)S(1)}, bf16[272,384]{1,0:T(8,128)(2,1)S(1)}, u32[]{:S(2)}, u32[]{:S(2)}) collective-permute-start(bf16[272,384]{1,0:T(8,128)(2,1)S(1)} %fusion.4), channel_id=1, source_target_pairs={{0,2},{1,3},{2,0},{3,1},{4,6},{5,7},{6,4},{7,5},{8,10},{9,11},{10,... | collective-permute-start | bytes 626696 | tf_op jit(solution)/shard_map/ppermute | solution.py:427
  46.2 5.1 %collective-permute-done.4.refs_1_ = bf16[272,384]{1,0:T(8,128)(2,1)S(1)} collective-permute-done((bf16[272,384]{1,0:T(8,128)(2,1)S(1)}, bf16[272,384]{1,0:T(8,128)(2,1)S(1)}, u32[]{:S(2)}, u32[]{:S(2)}) %collective-permute-start.4) | collective-permute-done | bytes 208928 | tf_op jit(solution)/shard_map/ppermute | solution.py:427
  51.3 0.0 collective-permute-done.5.refs_3_
  51.3 1.3 %attend_part.1.refs_0_ = bf16[2,2,128,128]{3,2,1,0:T(8,128)(2,1)S(1)} custom-call(f32[272,384]{1,0:T(8,128)S(1)} %slice_bitcast_fusion.1.refs_0_, bf16[272,384]{1,0:T(8,128)(2,1)S(1)} %collective-permute-done.4.refs_1_, f32[272,384]{1,0:T(8,128)S(1)} %slice_bitcast_fusion.refs_2_, bf16[272,384]{1,0:T(8,128)(2,1)S(1)} %collective-permute-done.5.refs_3_, ...), custom_call_target="tpu_custom_call" | custom-call | tf_op jit(solution)/shard_map/attend_part/pallas_call | solution.py:346
  52.6 3.0 %collective-permute-start.7 = (bf16[2,2,128,128]{3,2,1,0:T(8,128)(2,1)S(1)}, bf16[2,2,128,128]{3,2,1,0:T(8,128)(2,1)S(1)}, u32[]{:S(2)}, u32[]{:S(2)}) collective-permute-start(bf16[2,2,128,128]{3,2,1,0:T(8,128)(2,1)S(1)} %attend_part.1.refs_0_), channel_id=1, source_target_pairs={{0,2},{1,3},{2,0},{3,1},{4,6},{5,7},{6,4},{7,5},{8,10},{9,11},{10,... | collective-permute-start | bytes 393224 | tf_op jit(solution)/shard_map/ppermute | solution.py:427
  55.7 3.6 %collective-permute-start.6 = (bf16[2,2,128,128]{3,2,1,0:T(8,128)(2,1)S(1)}, bf16[2,2,128,128]{3,2,1,0:T(8,128)(2,1)S(1)}, u32[]{:S(2)}, u32[]{:S(2)}) collective-permute-start(bf16[2,2,128,128]{3,2,1,0:T(8,128)(2,1)S(1)} %attend_part.1.refs_0_), channel_id=1, source_target_pairs={{0,1},{1,0},{2,3},{3,2},{4,5},{5,4},{6,7},{7,6},{8,9},{9,8},{10,11... | collective-permute-start | bytes 393224 | tf_op jit(solution)/shard_map/ppermute | solution.py:427
  59.3 0.0 collective-permute-done.7.refs_2_
  59.3 4.1 %collective-permute-start.8 = (bf16[2,2,128,128]{3,2,1,0:T(8,128)(2,1)S(1)}, bf16[2,2,128,128]{3,2,1,0:T(8,128)(2,1)S(1)}, u32[]{:S(2)}, u32[]{:S(2)}) collective-permute-start(bf16[2,2,128,128]{3,2,1,0:T(8,128)(2,1)S(1)} %collective-permute-done.7.refs_2_), channel_id=1, source_target_pairs={{0,1},{1,0},{2,3},{3,2},{4,5},{5,4},{6,7},{7,6},{8,9},{9,8},{10,11... | collective-permute-start | bytes 393224 | tf_op jit(solution)/shard_map/ppermute | solution.py:427
  63.4 0.0 collective-permute-done.6.refs_1_
  63.4 2.8 %collective-permute-done.8.refs_3_ = bf16[2,2,128,128]{3,2,1,0:T(8,128)(2,1)S(1)} collective-permute-done((bf16[2,2,128,128]{3,2,1,0:T(8,128)(2,1)S(1)}, bf16[2,2,128,128]{3,2,1,0:T(8,128)(2,1)S(1)}, u32[]{:S(2)}, u32[]{:S(2)}) %collective-permute-start.8) | collective-permute-done | bytes 131104 | tf_op jit(solution)/shard_map/ppermute | solution.py:427
  66.2 1.0 %out_part.1 = (f32[128,640]{1,0:T(8,128)S(1)}, bf16[128,640]{1,0:T(8,128)(2,1)S(1)}) custom-call(s32[1]{0:T(128)} %bitcast.1.core.half, s32[1]{0:T(128)} %bitcast.2.mine, bf16[2,2,128,128]{3,2,1,0:T(8,128)(2,1)S(1)} %attend_part.1.refs_0_, bf16[2,2,128,128]{3,2,1,0:T(8,128)(2,1)S(1)} %collective-permute-done.6.refs_1_, ...), custom_call_target="tpu_custom_call" | custom-call | tf_op jit(solution)/shard_map/out_part/pallas_call | solution.py:380
  67.2 4.2 %collective-permute-start.9 = (bf16[128,640]{1,0:T(8,128)(2,1)S(1)}, bf16[128,640]{1,0:T(8,128)(2,1)S(1)}, u32[]{:S(2)}, u32[]{:S(2)}) collective-permute-start(bf16[128,640]{1,0:T(8,128)(2,1)S(1)} %get-tuple-element.63), channel_id=1, source_target_pairs={{0,8},{8,0},{16,24},{24,16},{1,9},{9,1},{17,25},{25,17},{2,10},{10... | collective-permute-start | bytes 491528 | tf_op jit(solution)/shard_map/ppermute | solution.py:427
  71.4 1.0 %collective-permute-done.9 = bf16[128,640]{1,0:T(8,128)(2,1)S(1)} collective-permute-done((bf16[128,640]{1,0:T(8,128)(2,1)S(1)}, bf16[128,640]{1,0:T(8,128)(2,1)S(1)}, u32[]{:S(2)}, u32[]{:S(2)}) %collective-permute-start.9) | collective-permute-done | bytes 163872 | tf_op jit(solution)/shard_map/ppermute | solution.py:427
  72.4 2.2 %collective-permute-start.12 = (bf16[128,640]{1,0:T(8,128)(2,1)S(1)}, bf16[128,640]{1,0:T(8,128)(2,1)S(1)}, u32[]{:S(2)}, u32[]{:S(2)}) collective-permute-start(bf16[128,640]{1,0:T(8,128)(2,1)S(1)} %add_convert_fusion), channel_id=1, source_target_pairs={{0,20},{4,16},{8,28},{12,24},{16,4},{20,0},{24,12},{28,8},{1,21},{... | collective-permute-start | bytes 491528 | tf_op jit(solution)/shard_map/ppermute | solution.py:505
  74.7 0.2 collective-permute-start.11
  74.9 0.3 collective-permute-start.10
  75.2 3.7 %collective-permute-done.12 = bf16[128,640]{1,0:T(8,128)(2,1)S(1)} collective-permute-done((bf16[128,640]{1,0:T(8,128)(2,1)S(1)}, bf16[128,640]{1,0:T(8,128)(2,1)S(1)}, u32[]{:S(2)}, u32[]{:S(2)}) %collective-permute-start.12) | collective-permute-done | bytes 163872 | tf_op jit(solution)/shard_map/ppermute | solution.py:505
  78.8 4.2 %collective-permute-done.11 = bf16[128,640]{1,0:T(8,128)(2,1)S(1)} collective-permute-done((bf16[128,640]{1,0:T(8,128)(2,1)S(1)}, bf16[128,640]{1,0:T(8,128)(2,1)S(1)}, u32[]{:S(2)}, u32[]{:S(2)}) %collective-permute-start.11) | collective-permute-done | bytes 163872 | tf_op jit(solution)/shard_map/ppermute | solution.py:427
  83.0 0.0 collective-permute-done.10
  83.0 0.1 multiply_convert_fusion.rows
  83.1 0.7 collective-permute-start.13
  83.8 0.0 copy-done.5
  83.8 0.3 copy.17
  84.1 2.1 %grad_part.2.refs_0_ = bf16[2048,1280]{1,0:T(8,128)(2,1)} custom-call(s32[1]{0:T(128)} %bitcast.1.core.half, bf16[2048,128]{1,0:T(8,128)(2,1)S(1)} %bitcast.21, bf16[128,640]{1,0:T(8,128)(2,1)S(1)} %multiply_convert_fusion.rows), custom_call_target="tpu_custom_call" | custom-call | tf_op jit(solution)/shard_map/grad_part/pallas_call | solution.py:416
  86.1 0.0 collective-permute-done.13.rows
  86.1 2.0 %grad_part.3 = bf16[2048,1280]{1,0:T(8,128)(2,1)} custom-call(s32[1]{0:T(128)} %bitcast.8.half, bf16[2048,128]{1,0:T(8,128)(2,1)S(1)} %bitcast.22, bf16[128,640]{1,0:T(8,128)(2,1)S(1)} %collective-permute-done.13.rows, bf16[2048,1280]{1,0:T(8,128)(2,1)} %grad_part.2.refs_0_), custom_call_target="tpu_custom_call", output_to_operand_aliasing={{}: (3, {})} | custom-call | tf_op jit(solution)/shard_map/grad_part/pallas_call | solution.py:416
  88.2 0.0 copy-done.1
  (10 shorter events, 0.2 us)
Async XLA Ops:
  0.6 5.4 %copy-start = (bf16[256,1280]{1,0:T(8,128)(2,1)S(1)}, bf16[256,1280]{1,0:T(8,128)(2,1)}, u32[]{:S(2)}) copy-start(bf16[256,1280]{1,0:T(8,128)(2,1)} %param.17) | copy-start | bytes 1966084
  0.6 7.8 %copy-start.2 = (bf16[256,3,1280]{2,0,1:T(8,128)(2,1)S(1)}, bf16[256,3,1280]{2,0,1:T(8,128)(2,1)}, u32[]{:S(2)}) copy-start(bf16[256,3,1280]{2,0,1:T(8,128)(2,1)} %param.22) | copy-start | bytes 5898244
  0.7 7.8 %copy-start.3 = (bf16[256,3,1280]{2,0,1:T(8,128)(2,1)S(1)}, bf16[256,3,1280]{2,0,1:T(8,128)(2,1)}, u32[]{:S(2)}) copy-start(bf16[256,3,1280]{2,0,1:T(8,128)(2,1)} %param.26) | copy-start | bytes 5898244
  6.4 7.6 %collective-permute-start = (bf16[192,640]{1,0:T(8,128)(2,1)S(1)}, bf16[192,640]{1,0:T(8,128)(2,1)S(1)}, u32[]{:S(2)}, u32[]{:S(2)}) collective-permute-start(bf16[192,640]{1,0:T(8,128)(2,1)S(1)} %get-tuple-element.39), channel_id=1, source_target_pairs={{0,4},{4,0},{1,5},{5,1},{2,6},{6,2},{3,7},{7,3},{8,12},{12,8},{9,1... | collective-permute-start | bytes 737288 | tf_op jit(solution)/shard_map/ppermute | solution.py:427
  8.5 7.0 %copy-start.8 = (s32[3]{0:T(128)S(1)}, s32[3]{0:T(128)}, u32[]{:S(2)}) copy-start(s32[3]{0:T(128)} %param.19) | copy-start | bytes 40
  8.5 8.1 %copy-start.4 = (bf16[64,1280]{1,0:T(8,128)(2,1)S(1)}, bf16[64,1280]{1,0:T(8,128)(2,1)}, u32[]{:S(2)}) copy-start(bf16[64,1280]{1,0:T(8,128)(2,1)} %noise.1) | copy-start | bytes 491524
  12.0 12.5 %copy-start.6 = (f32[2,2048]{1,0:T(2,128)S(1)}, f32[2,2048]{1,0:T(2,128)}, u32[]{:S(2)}) copy-start(f32[2,2048]{1,0:T(2,128)} %param.23) | copy-start | bytes 49156
  12.0 12.4 %copy-start.7 = (f32[2,2048]{1,0:T(2,128)S(1)}, f32[2,2048]{1,0:T(2,128)}, u32[]{:S(2)}) copy-start(f32[2,2048]{1,0:T(2,128)} %param.27) | copy-start | bytes 49156
  14.0 2.6 %collective-permute-start.1 = (bf16[192,640]{1,0:T(8,128)(2,1)S(1)}, bf16[192,640]{1,0:T(8,128)(2,1)S(1)}, u32[]{:S(2)}, u32[]{:S(2)}) collective-permute-start(bf16[192,640]{1,0:T(8,128)(2,1)S(1)} %join_part.1.joined), channel_id=1, source_target_pairs={{0,8},{8,0},{16,24},{24,16},{1,9},{9,1},{17,25},{25,17},{2,10},{10... | collective-permute-start | bytes 737288 | tf_op jit(solution)/shard_map/ppermute | solution.py:427
  20.6 21.2 %collective-permute-start.2 = (bf16[2,272,384]{2,1,0:T(8,128)(2,1)S(1)}, bf16[2,272,384]{2,1,0:T(8,128)(2,1)S(1)}, u32[]{:S(2)}, u32[]{:S(2)}) collective-permute-start(bf16[2,272,384]{2,1,0:T(8,128)(2,1)S(1)} %get-tuple-element.52), channel_id=1, source_target_pairs={{0,2},{1,3},{2,0},{3,1},{4,6},{5,7},{6,4},{7,5},{8,10},{9,11},{10,... | collective-permute-start | bytes 1253384 | tf_op jit(solution)/shard_map/ppermute | solution.py:427
  23.2 18.6 %collective-permute-start.3 = (bf16[2,272,384]{2,1,0:T(8,128)(2,1)S(1)}, bf16[2,272,384]{2,1,0:T(8,128)(2,1)S(1)}, u32[]{:S(2)}, u32[]{:S(2)}) collective-permute-start(bf16[2,272,384]{2,1,0:T(8,128)(2,1)S(1)} %get-tuple-element.53), channel_id=1, source_target_pairs={{0,1},{1,0},{2,3},{3,2},{4,5},{5,4},{6,7},{7,6},{8,9},{9,8},{10,11... | collective-permute-start | bytes 1253384 | tf_op jit(solution)/shard_map/ppermute | solution.py:427
  41.9 41.9 %copy-start.5 = (bf16[128,2048]{1,0:T(8,128)(2,1)S(1)}, bf16[128,2048]{1,0:T(8,128)(2,1)}, u32[]{:S(2)}) copy-start(bf16[128,2048]{1,0:T(8,128)(2,1)} %param.14) | copy-start | bytes 1572868
  42.1 9.2 %collective-permute-start.4 = (bf16[272,384]{1,0:T(8,128)(2,1)S(1)}, bf16[272,384]{1,0:T(8,128)(2,1)S(1)}, u32[]{:S(2)}, u32[]{:S(2)}) collective-permute-start(bf16[272,384]{1,0:T(8,128)(2,1)S(1)} %fusion.5), channel_id=1, source_target_pairs={{0,1},{1,0},{2,3},{3,2},{4,5},{5,4},{6,7},{7,6},{8,9},{9,8},{10,11... | collective-permute-start | bytes 626696 | tf_op jit(solution)/shard_map/ppermute | solution.py:427
  43.4 7.9 %collective-permute-start.5 = (bf16[272,384]{1,0:T(8,128)(2,1)S(1)}, bf16[272,384]{1,0:T(8,128)(2,1)S(1)}, u32[]{:S(2)}, u32[]{:S(2)}) collective-permute-start(bf16[272,384]{1,0:T(8,128)(2,1)S(1)} %fusion.4), channel_id=1, source_target_pairs={{0,2},{1,3},{2,0},{3,1},{4,6},{5,7},{6,4},{7,5},{8,10},{9,11},{10,... | collective-permute-start | bytes 626696 | tf_op jit(solution)/shard_map/ppermute | solution.py:427
  52.6 6.7 %collective-permute-start.7 = (bf16[2,2,128,128]{3,2,1,0:T(8,128)(2,1)S(1)}, bf16[2,2,128,128]{3,2,1,0:T(8,128)(2,1)S(1)}, u32[]{:S(2)}, u32[]{:S(2)}) collective-permute-start(bf16[2,2,128,128]{3,2,1,0:T(8,128)(2,1)S(1)} %attend_part.1.refs_0_), channel_id=1, source_target_pairs={{0,2},{1,3},{2,0},{3,1},{4,6},{5,7},{6,4},{7,5},{8,10},{9,11},{10,... | collective-permute-start | bytes 393224 | tf_op jit(solution)/shard_map/ppermute | solution.py:427
  55.7 7.8 %collective-permute-start.6 = (bf16[2,2,128,128]{3,2,1,0:T(8,128)(2,1)S(1)}, bf16[2,2,128,128]{3,2,1,0:T(8,128)(2,1)S(1)}, u32[]{:S(2)}, u32[]{:S(2)}) collective-permute-start(bf16[2,2,128,128]{3,2,1,0:T(8,128)(2,1)S(1)} %attend_part.1.refs_0_), channel_id=1, source_target_pairs={{0,1},{1,0},{2,3},{3,2},{4,5},{5,4},{6,7},{7,6},{8,9},{9,8},{10,11... | collective-permute-start | bytes 393224 | tf_op jit(solution)/shard_map/ppermute | solution.py:427
  59.3 6.9 %collective-permute-start.8 = (bf16[2,2,128,128]{3,2,1,0:T(8,128)(2,1)S(1)}, bf16[2,2,128,128]{3,2,1,0:T(8,128)(2,1)S(1)}, u32[]{:S(2)}, u32[]{:S(2)}) collective-permute-start(bf16[2,2,128,128]{3,2,1,0:T(8,128)(2,1)S(1)} %collective-permute-done.7.refs_2_), channel_id=1, source_target_pairs={{0,1},{1,0},{2,3},{3,2},{4,5},{5,4},{6,7},{7,6},{8,9},{9,8},{10,11... | collective-permute-start | bytes 393224 | tf_op jit(solution)/shard_map/ppermute | solution.py:427
  67.2 5.2 %collective-permute-start.9 = (bf16[128,640]{1,0:T(8,128)(2,1)S(1)}, bf16[128,640]{1,0:T(8,128)(2,1)S(1)}, u32[]{:S(2)}, u32[]{:S(2)}) collective-permute-start(bf16[128,640]{1,0:T(8,128)(2,1)S(1)} %get-tuple-element.63), channel_id=1, source_target_pairs={{0,8},{8,0},{16,24},{24,16},{1,9},{9,1},{17,25},{25,17},{2,10},{10... | collective-permute-start | bytes 491528 | tf_op jit(solution)/shard_map/ppermute | solution.py:427
  72.4 6.4 %collective-permute-start.12 = (bf16[128,640]{1,0:T(8,128)(2,1)S(1)}, bf16[128,640]{1,0:T(8,128)(2,1)S(1)}, u32[]{:S(2)}, u32[]{:S(2)}) collective-permute-start(bf16[128,640]{1,0:T(8,128)(2,1)S(1)} %add_convert_fusion), channel_id=1, source_target_pairs={{0,20},{4,16},{8,28},{12,24},{16,4},{20,0},{24,12},{28,8},{1,21},{... | collective-permute-start | bytes 491528 | tf_op jit(solution)/shard_map/ppermute | solution.py:505
  74.7 8.4 %collective-permute-start.11 = (bf16[128,640]{1,0:T(8,128)(2,1)S(1)}, bf16[128,640]{1,0:T(8,128)(2,1)S(1)}, u32[]{:S(2)}, u32[]{:S(2)}) collective-permute-start(bf16[128,640]{1,0:T(8,128)(2,1)S(1)} %add_convert_fusion), channel_id=1, source_target_pairs={{0,16},{8,24},{16,0},{24,8},{1,17},{9,25},{17,1},{25,9},{2,18},{10... | collective-permute-start | bytes 491528 | tf_op jit(solution)/shard_map/ppermute | solution.py:427
  74.9 8.1 %collective-permute-start.10 = (bf16[128,640]{1,0:T(8,128)(2,1)S(1)}, bf16[128,640]{1,0:T(8,128)(2,1)S(1)}, u32[]{:S(2)}, u32[]{:S(2)}) collective-permute-start(bf16[128,640]{1,0:T(8,128)(2,1)S(1)} %add_convert_fusion), channel_id=1, source_target_pairs={{0,4},{4,0},{1,5},{5,1},{2,6},{6,2},{3,7},{7,3},{8,12},{12,8},{9,1... | collective-permute-start | bytes 491528 | tf_op jit(solution)/shard_map/ppermute | solution.py:427
  83.1 3.0 %collective-permute-start.13 = (bf16[128,640]{1,0:T(8,128)(2,1)S(1)}, bf16[128,640]{1,0:T(8,128)(2,1)S(1)}, u32[]{:S(2)}, u32[]{:S(2)}) collective-permute-start(bf16[128,640]{1,0:T(8,128)(2,1)S(1)} %multiply_convert_fusion.rows), channel_id=1, source_target_pairs={{0,8},{8,0},{16,24},{24,16},{1,9},{9,1},{17,25},{25,17},{2,10},{10... | collective-permute-start | bytes 491528 | tf_op jit(solution)/shard_map/ppermute | solution.py:427
  86.1 2.0 %copy-start.1 = (bf16[256,1280]{1,0:T(8,128)(2,1)S(1)}, bf16[256,1280]{1,0:T(8,128)(2,1)}, u32[]{:S(2)}) copy-start(bf16[256,1280]{1,0:T(8,128)(2,1)} %param.17) | copy-start | bytes 1966084

commit v3 on v0

--- a/solution.py
+++ b/solution.py
@@ -213,7 +213,7 @@
         out_shape=[jax.ShapeDtypeStruct((parts, depth, cols), jnp.bfloat16)] * 2
         + [jax.ShapeDtypeStruct((2, parts, 8, width), jnp.float32)],
         scratch_shapes=[pltpu.SemaphoreType.DMA((2 * parts,))],
-        compiler_params=params(46),
+        compiler_params=params(40),
         name="load_part",
     )(start, embed, time_a, time_b, planes_a, planes_b)
 
@@ -484,11 +484,12 @@
     latent, kept_a, sent_a, kept_b, sent_b = qkv_part(
         seq_at, core, mine, levels, joined, swapped, noise, mods, weight_a, weight_b
     )
-    arrived_a, arrived_b = exchange(sent_a, "mp", 1), exchange(sent_b, "mp", 2)
+    arrived_b = exchange(sent_b, "mp", 2)
+    arrived_a = exchange(sent_a, "mp", 1)
     out_a, out_b = [take(w, start, part_cols, 0) for w in (teacher_out, critic_out)]
     gains = jnp.stack([teacher_norm, critic_norm])
     gains = take(gains, gain_at, unit, 2)
-    arrived_a, arrived_b, out_a, out_b, gains = lax.optimization_barrier((arrived_a, arrived_b, out_a, out_b, gains))
+    arrived_b, arrived_a, out_a, out_b, gains = lax.optimization_barrier((arrived_b, arrived_a, out_a, out_b, gains))
     sum_a, sum_b = both(kept_a, arrived_a), both(kept_b, arrived_b)
     last_a = exchange(sum_a[1].astype(jnp.bfloat16), "mp", 2)
     last_b = exchange(sum_b[1].astype(jnp.bfloat16), "mp", 1)

time: 88.8 us -> 86.7 us (0.976)
  waiting for transfers between devices: 32.7 us -> 39.1 us
  starting transfers between devices: 28.3 us -> 24.1 us
  local copies, waits for them, and re-layouts: 5.92 us -> 3.81 us
  Pallas kernels: 16.1 us -> 14 us
    ppermute x13, waiting for transfers between devices: 29 us -> 35.4 us  [exchange(): lax.ppermute(array, axis, [(i, i ^ bit) for i in range(lax.axis_size(axis...]
    ppermute x13, starting transfers between devices: 26.1 us -> 22.4 us  [exchange(): lax.ppermute(array, axis, [(i, i ^ bit) for i in range(lax.axis_size(axis...]
    unnamed x21 -> x19, local copies, waits for them, and re-layouts: 2.43 us -> 0.32 us
    pallas_call x1, Pallas kernels: 5.6 us -> 3.51 us  [load_part(): pl.pallas_call(load_kernel, in_specs=[smem_spec()] + [vmem_spec()] * 3 +...]
  transfers between devices with their start and end apart: 14 -> 14, of which waited for: 9 -> 9; matrix products, arithmetic and copies ran while one was open for 3% -> 3% of each run, Pallas kernels for 9% -> 6%
where the time goes in v3:
time: 86.7 us; the launch traced here: 86.5 us
  waiting for transfers between devices  39.1 us (45%)
  starting transfers between devices  24.1 us (28%)
  Pallas kernels  14 us (16%)
  local copies, waits for them, and re-layouts  3.81 us (4%)
  matrix products  3.34 us (4%)
  other arithmetic  1.39 us (2%)
    ppermute x13, waiting for transfers between devices, exchange(): lax.ppermute(array, axis, [(i, i ^ bit) for i in range(lax.axis_size(axis...  35.4 us
    ppermute x13, starting transfers between devices, exchange(): lax.ppermute(array, axis, [(i, i ^ bit) for i in range(lax.axis_size(axis...  22.4 us
    pallas_call x2, Pallas kernels, grad_part(): pl.pallas_call(grad_kernel, grid_spec=grid_spec, out_shape=jax.ShapeDtype...  4.09 us
    pallas_call x1, Pallas kernels, qkv_part(): pl.pallas_call(qkv_kernel, in_specs=[smem_spec()] * 4 + [vmem_spec()] * 6...  3.98 us
    ppermute x1, waiting for transfers between devices, heads_per_role(): lax.ppermute(total, ('role', 'seq'), [(i, i ^ 2 * lax.axis_size('seq') +...  3.7 us
    pallas_call x1, Pallas kernels, load_part(): pl.pallas_call(load_kernel, in_specs=[smem_spec()] + [vmem_spec()] * 3 +...  3.51 us
    dynamic_slice x2, local copies, waits for them, and re-layouts, take(): lax.dynamic_slice_in_dim(array, begin, size, axis=axis, allow_negative_in...  3.37 us
    dot_general x2, matrix products, dot32(): return jnp.dot(a, b, preferred_element_type=jnp.float32)  3.34 us
  transfers between devices with their start and end apart: 14, of which 9 were waited for; matrix products, arithmetic and copies ran while one was open for 3% of the time, Pallas kernels for 6%

profile of v3, /device:TPU:1, one launch (start us, length us, event | category | flops | bytes accessed | tf_op | source)
XLA Modules:
  0.0 86.5 jit_solution(10976168259183382993)
XLA Ops:
  0.6 0.0 copy-start
  0.6 0.0 copy-start.2
  0.7 0.8 convert_element_type.48
  1.5 0.1 fusion.13
  1.6 0.0 copy-start.3
  1.6 3.1 %fusion.2.product = f32[128,640]{1,0:T(8,128)S(1)} fusion(bf16[128,2048]{1,0:T(8,128)(2,1)} %param.14, bf16[2048,1280]{1,0:T(8,128)(2,1)} %param.16, s32[]{:T(128)S(6)} %mul.47), kind=kOutput, calls=%fused_computation.2 | convolution fusion | flops 335544320 | bytes 3473412 | tf_op jit(solution)/shard_map/dot_general | solution.py:144
  4.7 0.0 copy-done
  4.7 0.3 fusion.5.gate
  5.0 1.0 %constant_dynamic-slice_fusion.2 = (bf16[64,640]{1,0:T(8,128)(2,1)S(1)}, bf16[64,640]{1,0:T(8,128)(2,1)S(1)}) fusion(bf16[64,1280]{1,0:T(8,128)(2,1)} %noise.1, s32[]{:T(128)S(6)} %mul.47, bf16[64,1280]{1,0:T(8,128)(2,1)} %param.15), kind=kLoop, calls=%fused_computation.29 | loop fusion | bytes 327684 | tf_op jit(solution)/shard_map/dynamic_slice | solution.py:431
  6.0 0.1 pack_part.1
  6.1 2.1 %collective-permute-start = (bf16[192,640]{1,0:T(8,128)(2,1)S(1)}, bf16[192,640]{1,0:T(8,128)(2,1)S(1)}, u32[]{:S(2)}, u32[]{:S(2)}) collective-permute-start(bf16[192,640]{1,0:T(8,128)(2,1)S(1)} %get-tuple-element.37), channel_id=1, source_target_pairs={{0,4},{4,0},{1,5},{5,1},{2,6},{6,2},{3,7},{7,3},{8,12},{12,8},{9,1... | collective-permute-start | bytes 737288 | tf_op jit(solution)/shard_map/ppermute | solution.py:427
  8.2 0.0 copy-done.2
  8.2 0.0 copy-done.3
  8.2 0.0 copy-start.8
  8.2 0.0 copy-start.4
  8.2 3.5 %load_part.1 = (bf16[3,1280,512]{2,1,0:T(8,128)(2,1)S(1)}, bf16[3,1280,512]{2,1,0:T(8,128)(2,1)S(1)}, f32[2,3,8,1280]{3,2,1,0:T(8,128)S(1)}) custom-call(s32[1]{0:T(128)} %bitcast.4.start, bf16[8,256]{1,0:T(8,128)(2,1)S(1)} %fusion.11.embed, bf16[3,256,1280]{2,1,0:T(8,128)(2,1)S(1)} %bitcast.26, bf16[3,256,1280]{2,1,0:T(8,128)(2,1)S(1)} %bitcast.27, ...), custom_call_target="tpu_custom_call" | custom-call | tf_op jit(solution)/shard_map/load_part/pallas_call | solution.py:209
  11.8 0.0 copy-start.6
  11.8 0.0 copy-start.7
  11.8 1.9 %collective-permute-done.arrived = bf16[192,640]{1,0:T(8,128)(2,1)S(1)} collective-permute-done((bf16[192,640]{1,0:T(8,128)(2,1)S(1)}, bf16[192,640]{1,0:T(8,128)(2,1)S(1)}, u32[]{:S(2)}, u32[]{:S(2)}) %collective-permute-start) | collective-permute-done | bytes 245792 | tf_op jit(solution)/shard_map/ppermute | solution.py:427
  13.8 1.5 %collective-permute-start.1 = (bf16[192,640]{1,0:T(8,128)(2,1)S(1)}, bf16[192,640]{1,0:T(8,128)(2,1)S(1)}, u32[]{:S(2)}, u32[]{:S(2)}) collective-permute-start(bf16[192,640]{1,0:T(8,128)(2,1)S(1)} %join_part.1.joined), channel_id=1, source_target_pairs={{0,8},{8,0},{16,24},{24,16},{1,9},{9,1},{17,25},{25,17},{2,10},{10... | collective-permute-start | bytes 737288 | tf_op jit(solution)/shard_map/ppermute | solution.py:427
  15.2 0.0 copy-done.8
  15.3 0.1 convert_multiply_fusion.levels
  15.3 1.1 %collective-permute-done.1.swapped = bf16[192,640]{1,0:T(8,128)(2,1)S(1)} collective-permute-done((bf16[192,640]{1,0:T(8,128)(2,1)S(1)}, bf16[192,640]{1,0:T(8,128)(2,1)S(1)}, u32[]{:S(2)}, u32[]{:S(2)}) %collective-permute-start.1) | collective-permute-done | bytes 245792 | tf_op jit(solution)/shard_map/ppermute | solution.py:427
  16.4 0.0 copy-done.4
  16.4 4.0 %qkv_part.1 = (bf16[64,1280]{1,0:T(8,128)(2,1)}, bf16[2,272,384]{2,1,0:T(8,128)(2,1)S(1)}, bf16[2,272,384]{2,1,0:T(8,128)(2,1)S(1)}, bf16[2,272,384]{2,1,0:T(8,128)(2,1)S(1)}, bf16[2,272,384]{2,1,0:T(8,128)(2,1)S(1)}) custom-call(s32[1]{0:T(128)} %bitcast.seq, s32[1]{0:T(128)} %bitcast.1.core.half, s32[1]{0:T(128)} %bitcast.2.mine, ...), custom_call_target="tpu_custom_call" | custom-call | tf_op jit(solution)/shard_map/qkv_part/pallas_call | solution.py:297
  20.4 2.6 %collective-permute-start.2 = (bf16[2,272,384]{2,1,0:T(8,128)(2,1)S(1)}, bf16[2,272,384]{2,1,0:T(8,128)(2,1)S(1)}, u32[]{:S(2)}, u32[]{:S(2)}) collective-permute-start(bf16[2,272,384]{2,1,0:T(8,128)(2,1)S(1)} %get-tuple-element.49), channel_id=1, source_target_pairs={{0,2},{1,3},{2,0},{3,1},{4,6},{5,7},{6,4},{7,5},{8,10},{9,11},{10,... | collective-permute-start | bytes 1253384 | tf_op jit(solution)/shard_map/ppermute | solution.py:427
  22.9 1.3 %collective-permute-start.3 = (bf16[2,272,384]{2,1,0:T(8,128)(2,1)S(1)}, bf16[2,272,384]{2,1,0:T(8,128)(2,1)S(1)}, u32[]{:S(2)}, u32[]{:S(2)}) collective-permute-start(bf16[2,272,384]{2,1,0:T(8,128)(2,1)S(1)} %get-tuple-element.50), channel_id=1, source_target_pairs={{0,1},{1,0},{2,3},{3,2},{4,5},{5,4},{6,7},{7,6},{8,9},{9,8},{10,11... | collective-permute-start | bytes 1253384 | tf_op jit(solution)/shard_map/ppermute | solution.py:427
  24.2 0.0 copy-done.6
  24.2 0.0 copy-done.7
  24.2 0.1 fusion.12.refs_4_
  24.3 2.3 %constant_dynamic-slice_fusion = (bf16[512,1280]{1,0:T(8,128)(2,1)S(1)}, bf16[512,1280]{1,0:T(8,128)(2,1)S(1)}) fusion(bf16[2048,1280]{1,0:T(8,128)(2,1)} %param.25, s32[]{:T(128)} %mul.48, bf16[2048,1280]{1,0:T(8,128)(2,1)} %param.21), kind=kLoop, calls=%fused_computation.27 | loop fusion | bytes 5242884 | tf_op jit(solution)/shard_map/dynamic_slice | solution.py:431
  26.7 14.9 %collective-permute-done.2 = bf16[2,272,384]{2,1,0:T(8,128)(2,1)S(1)} collective-permute-done((bf16[2,272,384]{2,1,0:T(8,128)(2,1)S(1)}, bf16[2,272,384]{2,1,0:T(8,128)(2,1)S(1)}, u32[]{:S(2)}, u32[]{:S(2)}) %collective-permute-start.2) | collective-permute-done | bytes 417824 | tf_op jit(solution)/shard_map/ppermute | solution.py:427
  41.5 0.0 collective-permute-done.3
  41.5 0.1 convert_add_fusion.1
  41.6 0.0 copy-start.5
  41.7 1.2 %collective-permute-start.4 = (bf16[272,384]{1,0:T(8,128)(2,1)S(1)}, bf16[272,384]{1,0:T(8,128)(2,1)S(1)}, u32[]{:S(2)}, u32[]{:S(2)}) collective-permute-start(bf16[272,384]{1,0:T(8,128)(2,1)S(1)} %fusion.7), channel_id=1, source_target_pairs={{0,2},{1,3},{2,0},{3,1},{4,6},{5,7},{6,4},{7,5},{8,10},{9,11},{10,... | collective-permute-start | bytes 626696 | tf_op jit(solution)/shard_map/ppermute | solution.py:427
  42.9 0.1 convert_add_fusion
  43.0 2.9 %collective-permute-start.5 = (bf16[272,384]{1,0:T(8,128)(2,1)S(1)}, bf16[272,384]{1,0:T(8,128)(2,1)S(1)}, u32[]{:S(2)}, u32[]{:S(2)}) collective-permute-start(bf16[272,384]{1,0:T(8,128)(2,1)S(1)} %fusion.8), channel_id=1, source_target_pairs={{0,1},{1,0},{2,3},{3,2},{4,5},{5,4},{6,7},{7,6},{8,9},{9,8},{10,11... | collective-permute-start | bytes 626696 | tf_op jit(solution)/shard_map/ppermute | solution.py:427
  46.0 6.8 %collective-permute-done.4.refs_1_ = bf16[272,384]{1,0:T(8,128)(2,1)S(1)} collective-permute-done((bf16[272,384]{1,0:T(8,128)(2,1)S(1)}, bf16[272,384]{1,0:T(8,128)(2,1)S(1)}, u32[]{:S(2)}, u32[]{:S(2)}) %collective-permute-start.4) | collective-permute-done | bytes 208928 | tf_op jit(solution)/shard_map/ppermute | solution.py:427
  52.8 0.0 collective-permute-done.5.refs_3_
  52.8 1.3 %attend_part.1.refs_0_ = bf16[2,2,128,128]{3,2,1,0:T(8,128)(2,1)S(1)} custom-call(f32[272,384]{1,0:T(8,128)S(1)} %slice_bitcast_fusion.1.refs_0_, bf16[272,384]{1,0:T(8,128)(2,1)S(1)} %collective-permute-done.4.refs_1_, f32[272,384]{1,0:T(8,128)S(1)} %slice_bitcast_fusion.refs_2_, bf16[272,384]{1,0:T(8,128)(2,1)S(1)} %collective-permute-done.5.refs_3_, ...), custom_call_target="tpu_custom_call" | custom-call | tf_op jit(solution)/shard_map/attend_part/pallas_call | solution.py:346
  54.1 2.0 %collective-permute-start.7 = (bf16[2,2,128,128]{3,2,1,0:T(8,128)(2,1)S(1)}, bf16[2,2,128,128]{3,2,1,0:T(8,128)(2,1)S(1)}, u32[]{:S(2)}, u32[]{:S(2)}) collective-permute-start(bf16[2,2,128,128]{3,2,1,0:T(8,128)(2,1)S(1)} %attend_part.1.refs_0_), channel_id=1, source_target_pairs={{0,2},{1,3},{2,0},{3,1},{4,6},{5,7},{6,4},{7,5},{8,10},{9,11},{10,... | collective-permute-start | bytes 393224 | tf_op jit(solution)/shard_map/ppermute | solution.py:427
  56.1 1.8 %collective-permute-start.6 = (bf16[2,2,128,128]{3,2,1,0:T(8,128)(2,1)S(1)}, bf16[2,2,128,128]{3,2,1,0:T(8,128)(2,1)S(1)}, u32[]{:S(2)}, u32[]{:S(2)}) collective-permute-start(bf16[2,2,128,128]{3,2,1,0:T(8,128)(2,1)S(1)} %attend_part.1.refs_0_), channel_id=1, source_target_pairs={{0,1},{1,0},{2,3},{3,2},{4,5},{5,4},{6,7},{7,6},{8,9},{9,8},{10,11... | collective-permute-start | bytes 393224 | tf_op jit(solution)/shard_map/ppermute | solution.py:427
  58.0 2.4 %collective-permute-done.7.refs_2_ = bf16[2,2,128,128]{3,2,1,0:T(8,128)(2,1)S(1)} collective-permute-done((bf16[2,2,128,128]{3,2,1,0:T(8,128)(2,1)S(1)}, bf16[2,2,128,128]{3,2,1,0:T(8,128)(2,1)S(1)}, u32[]{:S(2)}, u32[]{:S(2)}) %collective-permute-start.7) | collective-permute-done | bytes 131104 | tf_op jit(solution)/shard_map/ppermute | solution.py:427
  60.4 1.3 %collective-permute-start.8 = (bf16[2,2,128,128]{3,2,1,0:T(8,128)(2,1)S(1)}, bf16[2,2,128,128]{3,2,1,0:T(8,128)(2,1)S(1)}, u32[]{:S(2)}, u32[]{:S(2)}) collective-permute-start(bf16[2,2,128,128]{3,2,1,0:T(8,128)(2,1)S(1)} %collective-permute-done.7.refs_2_), channel_id=1, source_target_pairs={{0,1},{1,0},{2,3},{3,2},{4,5},{5,4},{6,7},{7,6},{8,9},{9,8},{10,11... | collective-permute-start | bytes 393224 | tf_op jit(solution)/shard_map/ppermute | solution.py:427
  61.7 0.0 collective-permute-done.6.refs_1_
  61.7 3.1 %collective-permute-done.8.refs_3_ = bf16[2,2,128,128]{3,2,1,0:T(8,128)(2,1)S(1)} collective-permute-done((bf16[2,2,128,128]{3,2,1,0:T(8,128)(2,1)S(1)}, bf16[2,2,128,128]{3,2,1,0:T(8,128)(2,1)S(1)}, u32[]{:S(2)}, u32[]{:S(2)}) %collective-permute-start.8) | collective-permute-done | bytes 131104 | tf_op jit(solution)/shard_map/ppermute | solution.py:427
  64.8 1.0 %out_part.1 = (f32[128,640]{1,0:T(8,128)S(1)}, bf16[128,640]{1,0:T(8,128)(2,1)S(1)}) custom-call(s32[1]{0:T(128)} %bitcast.1.core.half, s32[1]{0:T(128)} %bitcast.2.mine, bf16[2,2,128,128]{3,2,1,0:T(8,128)(2,1)S(1)} %attend_part.1.refs_0_, bf16[2,2,128,128]{3,2,1,0:T(8,128)(2,1)S(1)} %collective-permute-done.6.refs_1_, ...), custom_call_target="tpu_custom_call" | custom-call | tf_op jit(solution)/shard_map/out_part/pallas_call | solution.py:380
  65.8 4.0 %collective-permute-start.9 = (bf16[128,640]{1,0:T(8,128)(2,1)S(1)}, bf16[128,640]{1,0:T(8,128)(2,1)S(1)}, u32[]{:S(2)}, u32[]{:S(2)}) collective-permute-start(bf16[128,640]{1,0:T(8,128)(2,1)S(1)} %get-tuple-element.59), channel_id=1, source_target_pairs={{0,8},{8,0},{16,24},{24,16},{1,9},{9,1},{17,25},{25,17},{2,10},{10... | collective-permute-start | bytes 491528 | tf_op jit(solution)/shard_map/ppermute | solution.py:427
  69.8 1.0 %collective-permute-done.9 = bf16[128,640]{1,0:T(8,128)(2,1)S(1)} collective-permute-done((bf16[128,640]{1,0:T(8,128)(2,1)S(1)}, bf16[128,640]{1,0:T(8,128)(2,1)S(1)}, u32[]{:S(2)}, u32[]{:S(2)}) %collective-permute-start.9) | collective-permute-done | bytes 163872 | tf_op jit(solution)/shard_map/ppermute | solution.py:427
  70.9 1.7 %collective-permute-start.12 = (bf16[128,640]{1,0:T(8,128)(2,1)S(1)}, bf16[128,640]{1,0:T(8,128)(2,1)S(1)}, u32[]{:S(2)}, u32[]{:S(2)}) collective-permute-start(bf16[128,640]{1,0:T(8,128)(2,1)S(1)} %add_convert_fusion), channel_id=1, source_target_pairs={{0,20},{4,16},{8,28},{12,24},{16,4},{20,0},{24,12},{28,8},{1,21},{... | collective-permute-start | bytes 491528 | tf_op jit(solution)/shard_map/ppermute | solution.py:504
  72.6 0.2 collective-permute-start.11
  72.8 0.8 collective-permute-start.10
  73.6 3.7 %collective-permute-done.12 = bf16[128,640]{1,0:T(8,128)(2,1)S(1)} collective-permute-done((bf16[128,640]{1,0:T(8,128)(2,1)S(1)}, bf16[128,640]{1,0:T(8,128)(2,1)S(1)}, u32[]{:S(2)}, u32[]{:S(2)}) %collective-permute-start.12) | collective-permute-done | bytes 163872 | tf_op jit(solution)/shard_map/ppermute | solution.py:504
  77.3 4.2 %collective-permute-done.11 = bf16[128,640]{1,0:T(8,128)(2,1)S(1)} collective-permute-done((bf16[128,640]{1,0:T(8,128)(2,1)S(1)}, bf16[128,640]{1,0:T(8,128)(2,1)S(1)}, u32[]{:S(2)}, u32[]{:S(2)}) %collective-permute-start.11) | collective-permute-done | bytes 163872 | tf_op jit(solution)/shard_map/ppermute | solution.py:427
  81.5 0.0 collective-permute-done.10
  81.5 0.1 multiply_convert_fusion.rows
  81.6 0.6 collective-permute-start.13
  82.2 0.0 copy-done.5
  82.2 0.3 copy.18
  82.4 2.1 %grad_part.2.refs_0_ = bf16[2048,1280]{1,0:T(8,128)(2,1)} custom-call(s32[1]{0:T(128)} %bitcast.1.core.half, bf16[2048,128]{1,0:T(8,128)(2,1)S(1)} %bitcast.24, bf16[128,640]{1,0:T(8,128)(2,1)S(1)} %multiply_convert_fusion.rows), custom_call_target="tpu_custom_call" | custom-call | tf_op jit(solution)/shard_map/grad_part/pallas_call | solution.py:416
  84.5 0.0 collective-permute-done.13.rows
  84.5 2.0 %grad_part.3 = bf16[2048,1280]{1,0:T(8,128)(2,1)} custom-call(s32[1]{0:T(128)} %bitcast.9.half, bf16[2048,128]{1,0:T(8,128)(2,1)S(1)} %bitcast.25, bf16[128,640]{1,0:T(8,128)(2,1)S(1)} %collective-permute-done.13.rows, bf16[2048,1280]{1,0:T(8,128)(2,1)} %grad_part.2.refs_0_), custom_call_target="tpu_custom_call", output_to_operand_aliasing={{}: (3, {})} | custom-call | tf_op jit(solution)/shard_map/grad_part/pallas_call | solution.py:416
  86.5 0.0 copy-done.1
  (10 shorter events, 0.2 us)
Async XLA Ops:
  0.6 4.1 %copy-start = (bf16[256,1280]{1,0:T(8,128)(2,1)S(1)}, bf16[256,1280]{1,0:T(8,128)(2,1)}, u32[]{:S(2)}) copy-start(bf16[256,1280]{1,0:T(8,128)(2,1)} %param.17) | copy-start | bytes 1966084
  0.6 7.6 %copy-start.2 = (bf16[256,3,1280]{2,0,1:T(8,128)(2,1)S(1)}, bf16[256,3,1280]{2,0,1:T(8,128)(2,1)}, u32[]{:S(2)}) copy-start(bf16[256,3,1280]{2,0,1:T(8,128)(2,1)} %param.22) | copy-start | bytes 5898244
  1.6 6.6 %copy-start.3 = (bf16[256,3,1280]{2,0,1:T(8,128)(2,1)S(1)}, bf16[256,3,1280]{2,0,1:T(8,128)(2,1)}, u32[]{:S(2)}) copy-start(bf16[256,3,1280]{2,0,1:T(8,128)(2,1)} %param.26) | copy-start | bytes 5898244
  6.1 7.6 %collective-permute-start = (bf16[192,640]{1,0:T(8,128)(2,1)S(1)}, bf16[192,640]{1,0:T(8,128)(2,1)S(1)}, u32[]{:S(2)}, u32[]{:S(2)}) collective-permute-start(bf16[192,640]{1,0:T(8,128)(2,1)S(1)} %get-tuple-element.37), channel_id=1, source_target_pairs={{0,4},{4,0},{1,5},{5,1},{2,6},{6,2},{3,7},{7,3},{8,12},{12,8},{9,1... | collective-permute-start | bytes 737288 | tf_op jit(solution)/shard_map/ppermute | solution.py:427
  8.2 7.0 %copy-start.8 = (s32[3]{0:T(128)S(1)}, s32[3]{0:T(128)}, u32[]{:S(2)}) copy-start(s32[3]{0:T(128)} %param.19) | copy-start | bytes 40
  8.2 8.2 %copy-start.4 = (bf16[64,1280]{1,0:T(8,128)(2,1)S(1)}, bf16[64,1280]{1,0:T(8,128)(2,1)}, u32[]{:S(2)}) copy-start(bf16[64,1280]{1,0:T(8,128)(2,1)} %noise.1) | copy-start | bytes 491524
  11.8 12.5 %copy-start.6 = (f32[2,2048]{1,0:T(2,128)S(1)}, f32[2,2048]{1,0:T(2,128)}, u32[]{:S(2)}) copy-start(f32[2,2048]{1,0:T(2,128)} %param.23) | copy-start | bytes 49156
  11.8 12.5 %copy-start.7 = (f32[2,2048]{1,0:T(2,128)S(1)}, f32[2,2048]{1,0:T(2,128)}, u32[]{:S(2)}) copy-start(f32[2,2048]{1,0:T(2,128)} %param.27) | copy-start | bytes 49156
  13.8 2.6 %collective-permute-start.1 = (bf16[192,640]{1,0:T(8,128)(2,1)S(1)}, bf16[192,640]{1,0:T(8,128)(2,1)S(1)}, u32[]{:S(2)}, u32[]{:S(2)}) collective-permute-start(bf16[192,640]{1,0:T(8,128)(2,1)S(1)} %join_part.1.joined), channel_id=1, source_target_pairs={{0,8},{8,0},{16,24},{24,16},{1,9},{9,1},{17,25},{25,17},{2,10},{10... | collective-permute-start | bytes 737288 | tf_op jit(solution)/shard_map/ppermute | solution.py:427
  20.4 21.2 %collective-permute-start.2 = (bf16[2,272,384]{2,1,0:T(8,128)(2,1)S(1)}, bf16[2,272,384]{2,1,0:T(8,128)(2,1)S(1)}, u32[]{:S(2)}, u32[]{:S(2)}) collective-permute-start(bf16[2,272,384]{2,1,0:T(8,128)(2,1)S(1)} %get-tuple-element.49), channel_id=1, source_target_pairs={{0,2},{1,3},{2,0},{3,1},{4,6},{5,7},{6,4},{7,5},{8,10},{9,11},{10,... | collective-permute-start | bytes 1253384 | tf_op jit(solution)/shard_map/ppermute | solution.py:427
  22.9 18.6 %collective-permute-start.3 = (bf16[2,272,384]{2,1,0:T(8,128)(2,1)S(1)}, bf16[2,272,384]{2,1,0:T(8,128)(2,1)S(1)}, u32[]{:S(2)}, u32[]{:S(2)}) collective-permute-start(bf16[2,272,384]{2,1,0:T(8,128)(2,1)S(1)} %get-tuple-element.50), channel_id=1, source_target_pairs={{0,1},{1,0},{2,3},{3,2},{4,5},{5,4},{6,7},{7,6},{8,9},{9,8},{10,11... | collective-permute-start | bytes 1253384 | tf_op jit(solution)/shard_map/ppermute | solution.py:427
  41.6 40.5 %copy-start.5 = (bf16[128,2048]{1,0:T(8,128)(2,1)S(1)}, bf16[128,2048]{1,0:T(8,128)(2,1)}, u32[]{:S(2)}) copy-start(bf16[128,2048]{1,0:T(8,128)(2,1)} %param.14) | copy-start | bytes 1572868
  41.7 11.1 %collective-permute-start.4 = (bf16[272,384]{1,0:T(8,128)(2,1)S(1)}, bf16[272,384]{1,0:T(8,128)(2,1)S(1)}, u32[]{:S(2)}, u32[]{:S(2)}) collective-permute-start(bf16[272,384]{1,0:T(8,128)(2,1)S(1)} %fusion.7), channel_id=1, source_target_pairs={{0,2},{1,3},{2,0},{3,1},{4,6},{5,7},{6,4},{7,5},{8,10},{9,11},{10,... | collective-permute-start | bytes 626696 | tf_op jit(solution)/shard_map/ppermute | solution.py:427
  43.0 9.8 %collective-permute-start.5 = (bf16[272,384]{1,0:T(8,128)(2,1)S(1)}, bf16[272,384]{1,0:T(8,128)(2,1)S(1)}, u32[]{:S(2)}, u32[]{:S(2)}) collective-permute-start(bf16[272,384]{1,0:T(8,128)(2,1)S(1)} %fusion.8), channel_id=1, source_target_pairs={{0,1},{1,0},{2,3},{3,2},{4,5},{5,4},{6,7},{7,6},{8,9},{9,8},{10,11... | collective-permute-start | bytes 626696 | tf_op jit(solution)/shard_map/ppermute | solution.py:427
  54.1 6.3 %collective-permute-start.7 = (bf16[2,2,128,128]{3,2,1,0:T(8,128)(2,1)S(1)}, bf16[2,2,128,128]{3,2,1,0:T(8,128)(2,1)S(1)}, u32[]{:S(2)}, u32[]{:S(2)}) collective-permute-start(bf16[2,2,128,128]{3,2,1,0:T(8,128)(2,1)S(1)} %attend_part.1.refs_0_), channel_id=1, source_target_pairs={{0,2},{1,3},{2,0},{3,1},{4,6},{5,7},{6,4},{7,5},{8,10},{9,11},{10,... | collective-permute-start | bytes 393224 | tf_op jit(solution)/shard_map/ppermute | solution.py:427
  56.1 5.6 %collective-permute-start.6 = (bf16[2,2,128,128]{3,2,1,0:T(8,128)(2,1)S(1)}, bf16[2,2,128,128]{3,2,1,0:T(8,128)(2,1)S(1)}, u32[]{:S(2)}, u32[]{:S(2)}) collective-permute-start(bf16[2,2,128,128]{3,2,1,0:T(8,128)(2,1)S(1)} %attend_part.1.refs_0_), channel_id=1, source_target_pairs={{0,1},{1,0},{2,3},{3,2},{4,5},{5,4},{6,7},{7,6},{8,9},{9,8},{10,11... | collective-permute-start | bytes 393224 | tf_op jit(solution)/shard_map/ppermute | solution.py:427
  60.4 4.4 %collective-permute-start.8 = (bf16[2,2,128,128]{3,2,1,0:T(8,128)(2,1)S(1)}, bf16[2,2,128,128]{3,2,1,0:T(8,128)(2,1)S(1)}, u32[]{:S(2)}, u32[]{:S(2)}) collective-permute-start(bf16[2,2,128,128]{3,2,1,0:T(8,128)(2,1)S(1)} %collective-permute-done.7.refs_2_), channel_id=1, source_target_pairs={{0,1},{1,0},{2,3},{3,2},{4,5},{5,4},{6,7},{7,6},{8,9},{9,8},{10,11... | collective-permute-start | bytes 393224 | tf_op jit(solution)/shard_map/ppermute | solution.py:427
  65.8 5.1 %collective-permute-start.9 = (bf16[128,640]{1,0:T(8,128)(2,1)S(1)}, bf16[128,640]{1,0:T(8,128)(2,1)S(1)}, u32[]{:S(2)}, u32[]{:S(2)}) collective-permute-start(bf16[128,640]{1,0:T(8,128)(2,1)S(1)} %get-tuple-element.59), channel_id=1, source_target_pairs={{0,8},{8,0},{16,24},{24,16},{1,9},{9,1},{17,25},{25,17},{2,10},{10... | collective-permute-start | bytes 491528 | tf_op jit(solution)/shard_map/ppermute | solution.py:427
  70.9 6.4 %collective-permute-start.12 = (bf16[128,640]{1,0:T(8,128)(2,1)S(1)}, bf16[128,640]{1,0:T(8,128)(2,1)S(1)}, u32[]{:S(2)}, u32[]{:S(2)}) collective-permute-start(bf16[128,640]{1,0:T(8,128)(2,1)S(1)} %add_convert_fusion), channel_id=1, source_target_pairs={{0,20},{4,16},{8,28},{12,24},{16,4},{20,0},{24,12},{28,8},{1,21},{... | collective-permute-start | bytes 491528 | tf_op jit(solution)/shard_map/ppermute | solution.py:504
  72.6 8.9 %collective-permute-start.11 = (bf16[128,640]{1,0:T(8,128)(2,1)S(1)}, bf16[128,640]{1,0:T(8,128)(2,1)S(1)}, u32[]{:S(2)}, u32[]{:S(2)}) collective-permute-start(bf16[128,640]{1,0:T(8,128)(2,1)S(1)} %add_convert_fusion), channel_id=1, source_target_pairs={{0,16},{8,24},{16,0},{24,8},{1,17},{9,25},{17,1},{25,9},{2,18},{10... | collective-permute-start | bytes 491528 | tf_op jit(solution)/shard_map/ppermute | solution.py:427
  72.8 8.7 %collective-permute-start.10 = (bf16[128,640]{1,0:T(8,128)(2,1)S(1)}, bf16[128,640]{1,0:T(8,128)(2,1)S(1)}, u32[]{:S(2)}, u32[]{:S(2)}) collective-permute-start(bf16[128,640]{1,0:T(8,128)(2,1)S(1)} %add_convert_fusion), channel_id=1, source_target_pairs={{0,4},{4,0},{1,5},{5,1},{2,6},{6,2},{3,7},{7,3},{8,12},{12,8},{9,1... | collective-permute-start | bytes 491528 | tf_op jit(solution)/shard_map/ppermute | solution.py:427
  81.6 2.9 %collective-permute-start.13 = (bf16[128,640]{1,0:T(8,128)(2,1)S(1)}, bf16[128,640]{1,0:T(8,128)(2,1)S(1)}, u32[]{:S(2)}, u32[]{:S(2)}) collective-permute-start(bf16[128,640]{1,0:T(8,128)(2,1)S(1)} %multiply_convert_fusion.rows), channel_id=1, source_target_pairs={{0,8},{8,0},{16,24},{24,16},{1,9},{9,1},{17,25},{25,17},{2,10},{10... | collective-permute-start | bytes 491528 | tf_op jit(solution)/shard_map/ppermute | solution.py:427
  84.5 2.0 %copy-start.1 = (bf16[256,1280]{1,0:T(8,128)(2,1)S(1)}, bf16[256,1280]{1,0:T(8,128)(2,1)}, u32[]{:S(2)}) copy-start(bf16[256,1280]{1,0:T(8,128)(2,1)} %param.17) | copy-start | bytes 1966084

commit v4 on v3

--- a/solution.py
+++ b/solution.py
@@ -264,8 +264,8 @@
             goal[place, pl.ds(tokens, EXTRA_ROWS), cols] = tail.astype(jnp.bfloat16)
 
 
-def qkv_kernel(seq, core, mine, levels, joined, swapped, noise, mods, weight_a, weight_b, latent, *refs):
-    chunks, (values, noises, result) = refs[:4], refs[4:]
+def far_kernel(seq, core, mine, levels, joined, swapped, noise, mods, weight, latent, noisy, squares, *refs):
+    kept, sent, values, noises, result = refs
     length, cols = values.shape[0], joined.shape[1]
     own = latent.shape[0]
     tokens = 2 * length
@@ -285,29 +285,57 @@
     wide = mixed.astype(jnp.float32)
     sums = jnp.sum(wide * wide, axis=1, keepdims=True)
     sums = jnp.broadcast_to(sums, (tokens, length)).T[0:8]
-    for index, weight in enumerate((weight_a, weight_b)):
-        project(index, index + 1, mine[0], mixed, sums, mods, weight, *chunks[2 * index : 2 * index + 2], result)
-
-
-def qkv_part(seq, core, mine, levels, joined, swapped, noise, mods, weight_a, weight_b):
+    noisy[...] = mixed
+    squares[...] = sums
+    project(1, 2, mine[0], mixed, sums, mods, weight, kept, sent, result)
+
+
+def near_kernel(mine, noisy, squares, mods, weight, kept, sent, result):
+    project(0, 1, mine[0], noisy[...], squares[...], mods, weight, kept, sent, result)
+
+
+def chunk_shapes(tokens, cols):
+    unit = tokens // 2
+    return [jax.ShapeDtypeStruct((cols // unit // 2, tokens + EXTRA_ROWS, 3 * unit), jnp.bfloat16)] * 2
+
+
+def far_part(seq, core, mine, levels, joined, swapped, noise, mods, weight):
     own, width = noise.shape
     length = joined.shape[0] - own
     tokens = 2 * length
-    cols = weight_a.shape[2]
-    return pl.pallas_call(
-        qkv_kernel,
-        in_specs=[smem_spec()] * 4 + [vmem_spec()] * 6,
+    cols = weight.shape[2]
+    return pl.pallas_call(
+        far_kernel,
+        in_specs=[smem_spec()] * 4 + [vmem_spec()] * 5,
         out_specs=[vmem_spec()] * 5,
-        out_shape=[jax.ShapeDtypeStruct((own, width), jnp.bfloat16)]
-        + [jax.ShapeDtypeStruct((cols // length // 2, tokens + EXTRA_ROWS, 3 * length), jnp.bfloat16)] * 4,
+        out_shape=[
+            jax.ShapeDtypeStruct((own, width), jnp.bfloat16),
+            jax.ShapeDtypeStruct((tokens, width), jnp.bfloat16),
+            jax.ShapeDtypeStruct((8, tokens), jnp.float32),
+        ]
+        + chunk_shapes(tokens, cols),
         scratch_shapes=[
             pltpu.VMEM((length, width), jnp.bfloat16),
             pltpu.VMEM((length, width), jnp.bfloat16),
             pltpu.VMEM((tokens + EXTRA_ROWS, cols), jnp.float32),
         ],
         compiler_params=params(20),
-        name="qkv_part",
-    )(seq, core, mine, levels, joined, swapped, noise, mods, weight_a, weight_b)
+        name="far_part",
+    )(seq, core, mine, levels, joined, swapped, noise, mods, weight)
+
+
+def near_part(mine, noisy, squares, mods, weight):
+    tokens = noisy.shape[0]
+    cols = weight.shape[2]
+    return pl.pallas_call(
+        near_kernel,
+        in_specs=[smem_spec()] + [vmem_spec()] * 4,
+        out_specs=[vmem_spec()] * 2,
+        out_shape=chunk_shapes(tokens, cols),
+        scratch_shapes=[pltpu.VMEM((tokens + EXTRA_ROWS, cols), jnp.float32)],
+        compiler_params=params(20),
+        name="near_part",
+    )(mine, noisy, squares, mods, weight)
 
 
 def attend_kernel(width, kept_a, other_a, kept_b, other_b, gains, out):
@@ -481,10 +509,11 @@
     joined = join_part(full, arrived)
     swapped = exchange(joined, "role", 1)
 
-    latent, kept_a, sent_a, kept_b, sent_b = qkv_part(
-        seq_at, core, mine, levels, joined, swapped, noise, mods, weight_a, weight_b
+    latent, noisy, squares, kept_b, sent_b = far_part(
+        seq_at, core, mine, levels, joined, swapped, noise, mods, weight_b
     )
     arrived_b = exchange(sent_b, "mp", 2)
+    kept_a, sent_a = near_part(mine, noisy, squares, mods, weight_a)
     arrived_a = exchange(sent_a, "mp", 1)
     out_a, out_b = [take(w, start, part_cols, 0) for w in (teacher_out, critic_out)]
     gains = jnp.stack([teacher_norm, critic_norm])

time: 86.7 us -> 86.9 us (level)
  starting transfers between devices: 24.1 us -> 17.5 us
  waiting for transfers between devices: 39.1 us -> 45.7 us
    ppermute x13, starting transfers between devices: 22.4 us -> 15.2 us  [exchange(): lax.ppermute(array, axis, [(i, i ^ bit) for i in range(lax.axis_size(axis...]
    ppermute x13, waiting for transfers between devices: 35.4 us -> 42 us  [exchange(): lax.ppermute(array, axis, [(i, i ^ bit) for i in range(lax.axis_size(axis...]
    pallas_call x1 -> x2, Pallas kernels: 3.98 us -> 4.15 us  [the longest x1 2.69 us: far_part(): pl.pallas_call(far_kernel, in_specs=[smem_spec()] * 4 + [vmem_spec()] * 5...]
  transfers between devices with their start and end apart: 14 -> 14, of which waited for: 9 -> 10; matrix products, arithmetic and copies ran while one was open for 3% -> 3% of each run, Pallas kernels for 6% -> 8%
where the time goes in v4:
time: 86.9 us; the launch traced here: 86.7 us
  waiting for transfers between devices  45.7 us (53%)
  starting transfers between devices  17.5 us (20%)
  Pallas kernels  14.1 us (16%)
  local copies, waits for them, and re-layouts  3.81 us (4%)
  matrix products  3.34 us (4%)
  other arithmetic  1.4 us (2%)
    ppermute x13, waiting for transfers between devices, exchange(): lax.ppermute(array, axis, [(i, i ^ bit) for i in range(lax.axis_size(axis...  42 us
    ppermute x13, starting transfers between devices, exchange(): lax.ppermute(array, axis, [(i, i ^ bit) for i in range(lax.axis_size(axis...  15.2 us
    pallas_call x2, Pallas kernels, grad_part(): pl.pallas_call(grad_kernel, grid_spec=grid_spec, out_shape=jax.ShapeDtype...  4.1 us
    ppermute x1, waiting for transfers between devices, heads_per_role(): lax.ppermute(total, ('role', 'seq'), [(i, i ^ 2 * lax.axis_size('seq') +...  3.65 us
    pallas_call x1, Pallas kernels, load_part(): pl.pallas_call(load_kernel, in_specs=[smem_spec()] + [vmem_spec()] * 3 +...  3.51 us
    dynamic_slice x2, local copies, waits for them, and re-layouts, take(): lax.dynamic_slice_in_dim(array, begin, size, axis=axis, allow_negative_in...  3.37 us
    dot_general x2, matrix products, dot32(): return jnp.dot(a, b, preferred_element_type=jnp.float32)  3.34 us
    pallas_call x1, Pallas kernels, far_part(): pl.pallas_call(far_kernel, in_specs=[smem_spec()] * 4 + [vmem_spec()] * 5...  2.69 us
  transfers between devices with their start and end apart: 14, of which 10 were waited for; matrix products, arithmetic and copies ran while one was open for 3% of the time, Pallas kernels for 8%

profile of v4, /device:TPU:1, one launch (start us, length us, event | category | flops | bytes accessed | tf_op | source)
XLA Modules:
  0.0 86.7 jit_solution(14958218088538769780)
XLA Ops:
  0.6 0.0 copy-start
  0.6 0.0 copy-start.2
  0.7 0.8 convert_element_type.48
  1.5 0.1 fusion.13
  1.6 0.0 copy-start.3
  1.6 3.1 %fusion.2.product = f32[128,640]{1,0:T(8,128)S(1)} fusion(bf16[128,2048]{1,0:T(8,128)(2,1)} %param.14, bf16[2048,1280]{1,0:T(8,128)(2,1)} %param.16, s32[]{:T(128)S(6)} %mul.47), kind=kOutput, calls=%fused_computation.2 | convolution fusion | flops 335544320 | bytes 3473412 | tf_op jit(solution)/shard_map/dot_general | solution.py:144
  4.7 0.0 copy-done
  4.7 0.3 fusion.5.gate
  5.0 1.0 %constant_dynamic-slice_fusion.2 = (bf16[64,640]{1,0:T(8,128)(2,1)S(1)}, bf16[64,640]{1,0:T(8,128)(2,1)S(1)}) fusion(bf16[64,1280]{1,0:T(8,128)(2,1)} %noise.1, s32[]{:T(128)S(6)} %mul.47, bf16[64,1280]{1,0:T(8,128)(2,1)} %param.15), kind=kLoop, calls=%fused_computation.29 | loop fusion | bytes 327684 | tf_op jit(solution)/shard_map/dynamic_slice | solution.py:459
  6.0 0.1 pack_part.1
  6.1 2.1 %collective-permute-start = (bf16[192,640]{1,0:T(8,128)(2,1)S(1)}, bf16[192,640]{1,0:T(8,128)(2,1)S(1)}, u32[]{:S(2)}, u32[]{:S(2)}) collective-permute-start(bf16[192,640]{1,0:T(8,128)(2,1)S(1)} %get-tuple-element.39), channel_id=1, source_target_pairs={{0,4},{4,0},{1,5},{5,1},{2,6},{6,2},{3,7},{7,3},{8,12},{12,8},{9,1... | collective-permute-start | bytes 737288 | tf_op jit(solution)/shard_map/ppermute | solution.py:455
  8.2 0.0 copy-done.2
  8.2 0.0 copy-done.3
  8.2 0.0 copy-start.8
  8.2 0.0 copy-start.4
  8.2 3.5 %load_part.1 = (bf16[3,1280,512]{2,1,0:T(8,128)(2,1)S(1)}, bf16[3,1280,512]{2,1,0:T(8,128)(2,1)S(1)}, f32[2,3,8,1280]{3,2,1,0:T(8,128)S(1)}) custom-call(s32[1]{0:T(128)} %bitcast.4.start, bf16[8,256]{1,0:T(8,128)(2,1)S(1)} %fusion.11.embed, bf16[3,256,1280]{2,1,0:T(8,128)(2,1)S(1)} %bitcast.26, bf16[3,256,1280]{2,1,0:T(8,128)(2,1)S(1)} %bitcast.27, ...), custom_call_target="tpu_custom_call" | custom-call | tf_op jit(solution)/shard_map/load_part/pallas_call | solution.py:209
  11.8 2.0 %collective-permute-done.arrived = bf16[192,640]{1,0:T(8,128)(2,1)S(1)} collective-permute-done((bf16[192,640]{1,0:T(8,128)(2,1)S(1)}, bf16[192,640]{1,0:T(8,128)(2,1)S(1)}, u32[]{:S(2)}, u32[]{:S(2)}) %collective-permute-start) | collective-permute-done | bytes 245792 | tf_op jit(solution)/shard_map/ppermute | solution.py:455
  13.7 0.0 copy-start.6
  13.8 1.5 %collective-permute-start.1 = (bf16[192,640]{1,0:T(8,128)(2,1)S(1)}, bf16[192,640]{1,0:T(8,128)(2,1)S(1)}, u32[]{:S(2)}, u32[]{:S(2)}) collective-permute-start(bf16[192,640]{1,0:T(8,128)(2,1)S(1)} %join_part.1.joined), channel_id=1, source_target_pairs={{0,8},{8,0},{16,24},{24,16},{1,9},{9,1},{17,25},{25,17},{2,10},{10... | collective-permute-start | bytes 737288 | tf_op jit(solution)/shard_map/ppermute | solution.py:455
  15.3 0.0 copy-done.8
  15.3 0.1 convert_multiply_fusion.levels
  15.3 1.1 %collective-permute-done.1.swapped = bf16[192,640]{1,0:T(8,128)(2,1)S(1)} collective-permute-done((bf16[192,640]{1,0:T(8,128)(2,1)S(1)}, bf16[192,640]{1,0:T(8,128)(2,1)S(1)}, u32[]{:S(2)}, u32[]{:S(2)}) %collective-permute-start.1) | collective-permute-done | bytes 245792 | tf_op jit(solution)/shard_map/ppermute | solution.py:455
  16.4 0.0 copy-done.4
  16.4 2.7 %far_part.1 = (bf16[64,1280]{1,0:T(8,128)(2,1)}, bf16[256,1280]{1,0:T(8,128)(2,1)S(1)}, f32[8,256]{1,0:T(8,128)S(1)}, bf16[2,272,384]{2,1,0:T(8,128)(2,1)S(1)}, bf16[2,272,384]{2,1,0:T(8,128)(2,1)S(1)}) custom-call(s32[1]{0:T(128)} %bitcast.seq, s32[1]{0:T(128)} %bitcast.1.core.half, s32[1]{0:T(128)} %bitcast.2.mine, f32[2]{0:T(128)S(1)} %convert_multiply_fusion.levels, ...), custom_call_target="tpu_custom_call" | custom-call | tf_op jit(solution)/shard_map/far_part/pallas_call | solution.py:307
  19.1 2.6 %collective-permute-start.2 = (bf16[2,272,384]{2,1,0:T(8,128)(2,1)S(1)}, bf16[2,272,384]{2,1,0:T(8,128)(2,1)S(1)}, u32[]{:S(2)}, u32[]{:S(2)}) collective-permute-start(bf16[2,272,384]{2,1,0:T(8,128)(2,1)S(1)} %get-tuple-element.53), channel_id=1, source_target_pairs={{0,2},{1,3},{2,0},{3,1},{4,6},{5,7},{6,4},{7,5},{8,10},{9,11},{10,... | collective-permute-start | bytes 1253384 | tf_op jit(solution)/shard_map/ppermute | solution.py:455
  21.6 1.5 %near_part.1 = (bf16[2,272,384]{2,1,0:T(8,128)(2,1)S(1)}, bf16[2,272,384]{2,1,0:T(8,128)(2,1)S(1)}) custom-call(s32[1]{0:T(128)} %bitcast.2.mine, bf16[256,1280]{1,0:T(8,128)(2,1)S(1)} %get-tuple-element.49.noisy, f32[8,256]{1,0:T(8,128)S(1)} %get-tuple-element.50.squares, f32[2,3,8,1280]{3,2,1,0:T(8,128)S(1)} %get-tuple-element.45.mods.refs_6_, ...), custom_call_target="tpu_custom_call" | custom-call | tf_op jit(solution)/shard_map/near_part/pallas_call | solution.py:330
  23.1 1.4 %collective-permute-start.3 = (bf16[2,272,384]{2,1,0:T(8,128)(2,1)S(1)}, bf16[2,272,384]{2,1,0:T(8,128)(2,1)S(1)}, u32[]{:S(2)}, u32[]{:S(2)}) collective-permute-start(bf16[2,272,384]{2,1,0:T(8,128)(2,1)S(1)} %get-tuple-element.54), channel_id=1, source_target_pairs={{0,1},{1,0},{2,3},{3,2},{4,5},{5,4},{6,7},{7,6},{8,9},{9,8},{10,11... | collective-permute-start | bytes 1253384 | tf_op jit(solution)/shard_map/ppermute | solution.py:455
  24.5 0.0 copy-done.6
  24.5 0.0 copy-done.7
  24.5 0.1 fusion.12.refs_4_
  24.6 2.3 %constant_dynamic-slice_fusion = (bf16[512,1280]{1,0:T(8,128)(2,1)S(1)}, bf16[512,1280]{1,0:T(8,128)(2,1)S(1)}) fusion(bf16[2048,1280]{1,0:T(8,128)(2,1)} %param.25, s32[]{:T(128)} %mul.48, bf16[2048,1280]{1,0:T(8,128)(2,1)} %param.21), kind=kLoop, calls=%fused_computation.27 | loop fusion | bytes 5242884 | tf_op jit(solution)/shard_map/dynamic_slice | solution.py:459
  26.9 13.4 %collective-permute-done.2 = bf16[2,272,384]{2,1,0:T(8,128)(2,1)S(1)} collective-permute-done((bf16[2,272,384]{2,1,0:T(8,128)(2,1)S(1)}, bf16[2,272,384]{2,1,0:T(8,128)(2,1)S(1)}, u32[]{:S(2)}, u32[]{:S(2)}) %collective-permute-start.2) | collective-permute-done | bytes 417824 | tf_op jit(solution)/shard_map/ppermute | solution.py:455
  40.3 1.2 %collective-permute-done.3 = bf16[2,272,384]{2,1,0:T(8,128)(2,1)S(1)} collective-permute-done((bf16[2,272,384]{2,1,0:T(8,128)(2,1)S(1)}, bf16[2,272,384]{2,1,0:T(8,128)(2,1)S(1)}, u32[]{:S(2)}, u32[]{:S(2)}) %collective-permute-start.3) | collective-permute-done | bytes 417824 | tf_op jit(solution)/shard_map/ppermute | solution.py:455
  41.5 0.1 convert_add_fusion.1
  41.6 0.0 copy-start.5
  41.7 0.1 collective-permute-start.4
  41.8 0.1 convert_add_fusion
  41.9 2.9 %collective-permute-start.5 = (bf16[272,384]{1,0:T(8,128)(2,1)S(1)}, bf16[272,384]{1,0:T(8,128)(2,1)S(1)}, u32[]{:S(2)}, u32[]{:S(2)}) collective-permute-start(bf16[272,384]{1,0:T(8,128)(2,1)S(1)} %fusion.8), channel_id=1, source_target_pairs={{0,1},{1,0},{2,3},{3,2},{4,5},{5,4},{6,7},{7,6},{8,9},{9,8},{10,11... | collective-permute-start | bytes 626696 | tf_op jit(solution)/shard_map/ppermute | solution.py:455
  44.8 9.3 %collective-permute-done.4.refs_1_ = bf16[272,384]{1,0:T(8,128)(2,1)S(1)} collective-permute-done((bf16[272,384]{1,0:T(8,128)(2,1)S(1)}, bf16[272,384]{1,0:T(8,128)(2,1)S(1)}, u32[]{:S(2)}, u32[]{:S(2)}) %collective-permute-start.4) | collective-permute-done | bytes 208928 | tf_op jit(solution)/shard_map/ppermute | solution.py:455
  54.1 0.0 collective-permute-done.5.refs_3_
  54.1 1.3 %attend_part.1.refs_0_ = bf16[2,2,128,128]{3,2,1,0:T(8,128)(2,1)S(1)} custom-call(f32[272,384]{1,0:T(8,128)S(1)} %slice_bitcast_fusion.1.refs_0_, bf16[272,384]{1,0:T(8,128)(2,1)S(1)} %collective-permute-done.4.refs_1_, f32[272,384]{1,0:T(8,128)S(1)} %slice_bitcast_fusion.refs_2_, bf16[272,384]{1,0:T(8,128)(2,1)S(1)} %collective-permute-done.5.refs_3_, ...), custom_call_target="tpu_custom_call" | custom-call | tf_op jit(solution)/shard_map/attend_part/pallas_call | solution.py:374
  55.4 0.1 collective-permute-start.7
  55.4 1.3 %collective-permute-start.6 = (bf16[2,2,128,128]{3,2,1,0:T(8,128)(2,1)S(1)}, bf16[2,2,128,128]{3,2,1,0:T(8,128)(2,1)S(1)}, u32[]{:S(2)}, u32[]{:S(2)}) collective-permute-start(bf16[2,2,128,128]{3,2,1,0:T(8,128)(2,1)S(1)} %attend_part.1.refs_0_), channel_id=1, source_target_pairs={{0,1},{1,0},{2,3},{3,2},{4,5},{5,4},{6,7},{7,6},{8,9},{9,8},{10,11... | collective-permute-start | bytes 393224 | tf_op jit(solution)/shard_map/ppermute | solution.py:455
  56.7 6.0 %collective-permute-done.7.refs_2_ = bf16[2,2,128,128]{3,2,1,0:T(8,128)(2,1)S(1)} collective-permute-done((bf16[2,2,128,128]{3,2,1,0:T(8,128)(2,1)S(1)}, bf16[2,2,128,128]{3,2,1,0:T(8,128)(2,1)S(1)}, u32[]{:S(2)}, u32[]{:S(2)}) %collective-permute-start.7) | collective-permute-done | bytes 131104 | tf_op jit(solution)/shard_map/ppermute | solution.py:455
  62.7 0.0 collective-permute-start.8
  62.7 0.0 collective-permute-done.6.refs_1_
  62.7 3.8 %collective-permute-done.8.refs_3_ = bf16[2,2,128,128]{3,2,1,0:T(8,128)(2,1)S(1)} collective-permute-done((bf16[2,2,128,128]{3,2,1,0:T(8,128)(2,1)S(1)}, bf16[2,2,128,128]{3,2,1,0:T(8,128)(2,1)S(1)}, u32[]{:S(2)}, u32[]{:S(2)}) %collective-permute-start.8) | collective-permute-done | bytes 131104 | tf_op jit(solution)/shard_map/ppermute | solution.py:455
  66.6 1.0 %out_part.1 = (f32[128,640]{1,0:T(8,128)S(1)}, bf16[128,640]{1,0:T(8,128)(2,1)S(1)}) custom-call(s32[1]{0:T(128)} %bitcast.1.core.half, s32[1]{0:T(128)} %bitcast.2.mine, bf16[2,2,128,128]{3,2,1,0:T(8,128)(2,1)S(1)} %attend_part.1.refs_0_, bf16[2,2,128,128]{3,2,1,0:T(8,128)(2,1)S(1)} %collective-permute-done.6.refs_1_, ...), custom_call_target="tpu_custom_call" | custom-call | tf_op jit(solution)/shard_map/out_part/pallas_call | solution.py:408
  67.5 2.3 %collective-permute-start.9 = (bf16[128,640]{1,0:T(8,128)(2,1)S(1)}, bf16[128,640]{1,0:T(8,128)(2,1)S(1)}, u32[]{:S(2)}, u32[]{:S(2)}) collective-permute-start(bf16[128,640]{1,0:T(8,128)(2,1)S(1)} %get-tuple-element.63), channel_id=1, source_target_pairs={{0,8},{8,0},{16,24},{24,16},{1,9},{9,1},{17,25},{25,17},{2,10},{10... | collective-permute-start | bytes 491528 | tf_op jit(solution)/shard_map/ppermute | solution.py:455
  69.8 1.0 %collective-permute-done.9 = bf16[128,640]{1,0:T(8,128)(2,1)S(1)} collective-permute-done((bf16[128,640]{1,0:T(8,128)(2,1)S(1)}, bf16[128,640]{1,0:T(8,128)(2,1)S(1)}, u32[]{:S(2)}, u32[]{:S(2)}) %collective-permute-start.9) | collective-permute-done | bytes 163872 | tf_op jit(solution)/shard_map/ppermute | solution.py:455
  70.9 2.3 %collective-permute-start.12 = (bf16[128,640]{1,0:T(8,128)(2,1)S(1)}, bf16[128,640]{1,0:T(8,128)(2,1)S(1)}, u32[]{:S(2)}, u32[]{:S(2)}) collective-permute-start(bf16[128,640]{1,0:T(8,128)(2,1)S(1)} %add_convert_fusion), channel_id=1, source_target_pairs={{0,20},{4,16},{8,28},{12,24},{16,4},{20,0},{24,12},{28,8},{1,21},{... | collective-permute-start | bytes 491528 | tf_op jit(solution)/shard_map/ppermute | solution.py:533
  73.2 0.2 collective-permute-start.11
  73.4 0.2 collective-permute-start.10
  73.6 3.7 %collective-permute-done.12 = bf16[128,640]{1,0:T(8,128)(2,1)S(1)} collective-permute-done((bf16[128,640]{1,0:T(8,128)(2,1)S(1)}, bf16[128,640]{1,0:T(8,128)(2,1)S(1)}, u32[]{:S(2)}, u32[]{:S(2)}) %collective-permute-start.12) | collective-permute-done | bytes 163872 | tf_op jit(solution)/shard_map/ppermute | solution.py:533
  77.3 4.2 %collective-permute-done.11 = bf16[128,640]{1,0:T(8,128)(2,1)S(1)} collective-permute-done((bf16[128,640]{1,0:T(8,128)(2,1)S(1)}, bf16[128,640]{1,0:T(8,128)(2,1)S(1)}, u32[]{:S(2)}, u32[]{:S(2)}) %collective-permute-start.11) | collective-permute-done | bytes 163872 | tf_op jit(solution)/shard_map/ppermute | solution.py:455
  81.5 0.0 collective-permute-done.10
  81.5 0.1 multiply_convert_fusion.rows
  81.6 0.7 collective-permute-start.13
  82.3 0.0 copy-done.5
  82.3 0.3 copy.18
  82.6 2.1 %grad_part.2.refs_0_ = bf16[2048,1280]{1,0:T(8,128)(2,1)} custom-call(s32[1]{0:T(128)} %bitcast.1.core.half, bf16[2048,128]{1,0:T(8,128)(2,1)S(1)} %bitcast.24, bf16[128,640]{1,0:T(8,128)(2,1)S(1)} %multiply_convert_fusion.rows), custom_call_target="tpu_custom_call" | custom-call | tf_op jit(solution)/shard_map/grad_part/pallas_call | solution.py:444
  84.7 0.0 collective-permute-done.13.rows
  84.7 2.0 %grad_part.3 = bf16[2048,1280]{1,0:T(8,128)(2,1)} custom-call(s32[1]{0:T(128)} %bitcast.9.half, bf16[2048,128]{1,0:T(8,128)(2,1)S(1)} %bitcast.25, bf16[128,640]{1,0:T(8,128)(2,1)S(1)} %collective-permute-done.13.rows, bf16[2048,1280]{1,0:T(8,128)(2,1)} %grad_part.2.refs_0_), custom_call_target="tpu_custom_call", output_to_operand_aliasing={{}: (3, {})} | custom-call | tf_op jit(solution)/shard_map/grad_part/pallas_call | solution.py:444
  86.7 0.0 copy-done.1
  (11 shorter events, 0.2 us)
Async XLA Ops:
  0.6 4.1 %copy-start = (bf16[256,1280]{1,0:T(8,128)(2,1)S(1)}, bf16[256,1280]{1,0:T(8,128)(2,1)}, u32[]{:S(2)}) copy-start(bf16[256,1280]{1,0:T(8,128)(2,1)} %param.17) | copy-start | bytes 1966084
  0.6 7.6 %copy-start.2 = (bf16[256,3,1280]{2,0,1:T(8,128)(2,1)S(1)}, bf16[256,3,1280]{2,0,1:T(8,128)(2,1)}, u32[]{:S(2)}) copy-start(bf16[256,3,1280]{2,0,1:T(8,128)(2,1)} %param.22) | copy-start | bytes 5898244
  1.6 6.6 %copy-start.3 = (bf16[256,3,1280]{2,0,1:T(8,128)(2,1)S(1)}, bf16[256,3,1280]{2,0,1:T(8,128)(2,1)}, u32[]{:S(2)}) copy-start(bf16[256,3,1280]{2,0,1:T(8,128)(2,1)} %param.26) | copy-start | bytes 5898244
  6.1 7.6 %collective-permute-start = (bf16[192,640]{1,0:T(8,128)(2,1)S(1)}, bf16[192,640]{1,0:T(8,128)(2,1)S(1)}, u32[]{:S(2)}, u32[]{:S(2)}) collective-permute-start(bf16[192,640]{1,0:T(8,128)(2,1)S(1)} %get-tuple-element.39), channel_id=1, source_target_pairs={{0,4},{4,0},{1,5},{5,1},{2,6},{6,2},{3,7},{7,3},{8,12},{12,8},{9,1... | collective-permute-start | bytes 737288 | tf_op jit(solution)/shard_map/ppermute | solution.py:455
  8.2 7.0 %copy-start.8 = (s32[3]{0:T(128)S(1)}, s32[3]{0:T(128)}, u32[]{:S(2)}) copy-start(s32[3]{0:T(128)} %param.19) | copy-start | bytes 40
  8.2 8.2 %copy-start.4 = (bf16[64,1280]{1,0:T(8,128)(2,1)S(1)}, bf16[64,1280]{1,0:T(8,128)(2,1)}, u32[]{:S(2)}) copy-start(bf16[64,1280]{1,0:T(8,128)(2,1)} %noise.1) | copy-start | bytes 491524
  13.7 10.8 %copy-start.6 = (f32[2,2048]{1,0:T(2,128)S(1)}, f32[2,2048]{1,0:T(2,128)}, u32[]{:S(2)}) copy-start(f32[2,2048]{1,0:T(2,128)} %param.23) | copy-start | bytes 49156
  13.7 10.8 %copy-start.7 = (f32[2,2048]{1,0:T(2,128)S(1)}, f32[2,2048]{1,0:T(2,128)}, u32[]{:S(2)}) copy-start(f32[2,2048]{1,0:T(2,128)} %param.27) | copy-start | bytes 49156
  13.8 2.6 %collective-permute-start.1 = (bf16[192,640]{1,0:T(8,128)(2,1)S(1)}, bf16[192,640]{1,0:T(8,128)(2,1)S(1)}, u32[]{:S(2)}, u32[]{:S(2)}) collective-permute-start(bf16[192,640]{1,0:T(8,128)(2,1)S(1)} %join_part.1.joined), channel_id=1, source_target_pairs={{0,8},{8,0},{16,24},{24,16},{1,9},{9,1},{17,25},{25,17},{2,10},{10... | collective-permute-start | bytes 737288 | tf_op jit(solution)/shard_map/ppermute | solution.py:455
  19.1 21.2 %collective-permute-start.2 = (bf16[2,272,384]{2,1,0:T(8,128)(2,1)S(1)}, bf16[2,272,384]{2,1,0:T(8,128)(2,1)S(1)}, u32[]{:S(2)}, u32[]{:S(2)}) collective-permute-start(bf16[2,272,384]{2,1,0:T(8,128)(2,1)S(1)} %get-tuple-element.53), channel_id=1, source_target_pairs={{0,2},{1,3},{2,0},{3,1},{4,6},{5,7},{6,4},{7,5},{8,10},{9,11},{10,... | collective-permute-start | bytes 1253384 | tf_op jit(solution)/shard_map/ppermute | solution.py:455
  23.1 18.4 %collective-permute-start.3 = (bf16[2,272,384]{2,1,0:T(8,128)(2,1)S(1)}, bf16[2,272,384]{2,1,0:T(8,128)(2,1)S(1)}, u32[]{:S(2)}, u32[]{:S(2)}) collective-permute-start(bf16[2,272,384]{2,1,0:T(8,128)(2,1)S(1)} %get-tuple-element.54), channel_id=1, source_target_pairs={{0,1},{1,0},{2,3},{3,2},{4,5},{5,4},{6,7},{7,6},{8,9},{9,8},{10,11... | collective-permute-start | bytes 1253384 | tf_op jit(solution)/shard_map/ppermute | solution.py:455
  41.6 40.7 %copy-start.5 = (bf16[128,2048]{1,0:T(8,128)(2,1)S(1)}, bf16[128,2048]{1,0:T(8,128)(2,1)}, u32[]{:S(2)}) copy-start(bf16[128,2048]{1,0:T(8,128)(2,1)} %param.14) | copy-start | bytes 1572868
  41.7 12.4 %collective-permute-start.4 = (bf16[272,384]{1,0:T(8,128)(2,1)S(1)}, bf16[272,384]{1,0:T(8,128)(2,1)S(1)}, u32[]{:S(2)}, u32[]{:S(2)}) collective-permute-start(bf16[272,384]{1,0:T(8,128)(2,1)S(1)} %fusion.7), channel_id=1, source_target_pairs={{0,2},{1,3},{2,0},{3,1},{4,6},{5,7},{6,4},{7,5},{8,10},{9,11},{10,... | collective-permute-start | bytes 626696 | tf_op jit(solution)/shard_map/ppermute | solution.py:455
  41.9 12.2 %collective-permute-start.5 = (bf16[272,384]{1,0:T(8,128)(2,1)S(1)}, bf16[272,384]{1,0:T(8,128)(2,1)S(1)}, u32[]{:S(2)}, u32[]{:S(2)}) collective-permute-start(bf16[272,384]{1,0:T(8,128)(2,1)S(1)} %fusion.8), channel_id=1, source_target_pairs={{0,1},{1,0},{2,3},{3,2},{4,5},{5,4},{6,7},{7,6},{8,9},{9,8},{10,11... | collective-permute-start | bytes 626696 | tf_op jit(solution)/shard_map/ppermute | solution.py:455
  55.4 7.4 %collective-permute-start.7 = (bf16[2,2,128,128]{3,2,1,0:T(8,128)(2,1)S(1)}, bf16[2,2,128,128]{3,2,1,0:T(8,128)(2,1)S(1)}, u32[]{:S(2)}, u32[]{:S(2)}) collective-permute-start(bf16[2,2,128,128]{3,2,1,0:T(8,128)(2,1)S(1)} %attend_part.1.refs_0_), channel_id=1, source_target_pairs={{0,2},{1,3},{2,0},{3,1},{4,6},{5,7},{6,4},{7,5},{8,10},{9,11},{10,... | collective-permute-start | bytes 393224 | tf_op jit(solution)/shard_map/ppermute | solution.py:455
  55.4 7.3 %collective-permute-start.6 = (bf16[2,2,128,128]{3,2,1,0:T(8,128)(2,1)S(1)}, bf16[2,2,128,128]{3,2,1,0:T(8,128)(2,1)S(1)}, u32[]{:S(2)}, u32[]{:S(2)}) collective-permute-start(bf16[2,2,128,128]{3,2,1,0:T(8,128)(2,1)S(1)} %attend_part.1.refs_0_), channel_id=1, source_target_pairs={{0,1},{1,0},{2,3},{3,2},{4,5},{5,4},{6,7},{7,6},{8,9},{9,8},{10,11... | collective-permute-start | bytes 393224 | tf_op jit(solution)/shard_map/ppermute | solution.py:455
  62.7 3.8 %collective-permute-start.8 = (bf16[2,2,128,128]{3,2,1,0:T(8,128)(2,1)S(1)}, bf16[2,2,128,128]{3,2,1,0:T(8,128)(2,1)S(1)}, u32[]{:S(2)}, u32[]{:S(2)}) collective-permute-start(bf16[2,2,128,128]{3,2,1,0:T(8,128)(2,1)S(1)} %collective-permute-done.7.refs_2_), channel_id=1, source_target_pairs={{0,1},{1,0},{2,3},{3,2},{4,5},{5,4},{6,7},{7,6},{8,9},{9,8},{10,11... | collective-permute-start | bytes 393224 | tf_op jit(solution)/shard_map/ppermute | solution.py:455
  67.5 3.3 %collective-permute-start.9 = (bf16[128,640]{1,0:T(8,128)(2,1)S(1)}, bf16[128,640]{1,0:T(8,128)(2,1)S(1)}, u32[]{:S(2)}, u32[]{:S(2)}) collective-permute-start(bf16[128,640]{1,0:T(8,128)(2,1)S(1)} %get-tuple-element.63), channel_id=1, source_target_pairs={{0,8},{8,0},{16,24},{24,16},{1,9},{9,1},{17,25},{25,17},{2,10},{10... | collective-permute-start | bytes 491528 | tf_op jit(solution)/shard_map/ppermute | solution.py:455
  70.9 6.4 %collective-permute-start.12 = (bf16[128,640]{1,0:T(8,128)(2,1)S(1)}, bf16[128,640]{1,0:T(8,128)(2,1)S(1)}, u32[]{:S(2)}, u32[]{:S(2)}) collective-permute-start(bf16[128,640]{1,0:T(8,128)(2,1)S(1)} %add_convert_fusion), channel_id=1, source_target_pairs={{0,20},{4,16},{8,28},{12,24},{16,4},{20,0},{24,12},{28,8},{1,21},{... | collective-permute-start | bytes 491528 | tf_op jit(solution)/shard_map/ppermute | solution.py:533
  73.2 8.3 %collective-permute-start.11 = (bf16[128,640]{1,0:T(8,128)(2,1)S(1)}, bf16[128,640]{1,0:T(8,128)(2,1)S(1)}, u32[]{:S(2)}, u32[]{:S(2)}) collective-permute-start(bf16[128,640]{1,0:T(8,128)(2,1)S(1)} %add_convert_fusion), channel_id=1, source_target_pairs={{0,16},{8,24},{16,0},{24,8},{1,17},{9,25},{17,1},{25,9},{2,18},{10... | collective-permute-start | bytes 491528 | tf_op jit(solution)/shard_map/ppermute | solution.py:455
  73.4 8.1 %collective-permute-start.10 = (bf16[128,640]{1,0:T(8,128)(2,1)S(1)}, bf16[128,640]{1,0:T(8,128)(2,1)S(1)}, u32[]{:S(2)}, u32[]{:S(2)}) collective-permute-start(bf16[128,640]{1,0:T(8,128)(2,1)S(1)} %add_convert_fusion), channel_id=1, source_target_pairs={{0,4},{4,0},{1,5},{5,1},{2,6},{6,2},{3,7},{7,3},{8,12},{12,8},{9,1... | collective-permute-start | bytes 491528 | tf_op jit(solution)/shard_map/ppermute | solution.py:455
  81.6 3.1 %collective-permute-start.13 = (bf16[128,640]{1,0:T(8,128)(2,1)S(1)}, bf16[128,640]{1,0:T(8,128)(2,1)S(1)}, u32[]{:S(2)}, u32[]{:S(2)}) collective-permute-start(bf16[128,640]{1,0:T(8,128)(2,1)S(1)} %multiply_convert_fusion.rows), channel_id=1, source_target_pairs={{0,8},{8,0},{16,24},{24,16},{1,9},{9,1},{17,25},{25,17},{2,10},{10... | collective-permute-start | bytes 491528 | tf_op jit(solution)/shard_map/ppermute | solution.py:455
  84.7 2.0 %copy-start.1 = (bf16[256,1280]{1,0:T(8,128)(2,1)S(1)}, bf16[256,1280]{1,0:T(8,128)(2,1)}, u32[]{:S(2)}) copy-start(bf16[256,1280]{1,0:T(8,128)(2,1)} %param.17) | copy-start | bytes 1966084

commit v5 on v3

--- a/solution.py
+++ b/solution.py
@@ -253,15 +253,18 @@
     for part in range(3):
         result[...] = dot32(rows, weight[part])
         cols = pl.ds(part * unit, unit)
-        for slot in range(groups):
-            at = at_block(jnp.bitwise_xor(mine, slot), unit)
-            goal = sent if slot & stride else kept
-            place = slot // 2 if stride == 1 else slot % 2
-            goal[place, pl.ds(0, tokens), cols] = result[pl.ds(0, tokens), at].astype(jnp.bfloat16)
-            tail = jnp.where(row_id < 2, result[pl.ds(tokens, EXTRA_ROWS), at], 0.0)
-            for level in range(2):
-                tail = jnp.where(row_id == 2 + level, squares[0:1, level * length : (level + 1) * length], tail)
-            goal[place, pl.ds(tokens, EXTRA_ROWS), cols] = tail.astype(jnp.bfloat16)
+        for half, goal in enumerate((kept, sent)):
+            tail = jnp.zeros((EXTRA_ROWS, unit), jnp.float32)
+            for place in range(groups // 2):
+                slot = 2 * place + half if stride == 1 else 2 * half + place
+                at = at_block(jnp.bitwise_xor(mine, slot), unit)
+                goal[pl.ds(place * tokens, tokens), cols] = result[pl.ds(0, tokens), at].astype(jnp.bfloat16)
+                for level in range(2):
+                    row = 4 * place + level
+                    tail = jnp.where(row_id == row, result[pl.ds(tokens + level, 1), at], tail)
+                    sums = squares[0:1, level * length : (level + 1) * length]
+                    tail = jnp.where(row_id == row + 2, sums, tail)
+            goal[pl.ds(2 * tokens, EXTRA_ROWS), cols] = tail.astype(jnp.bfloat16)
 
 
 def qkv_kernel(seq, core, mine, levels, joined, swapped, noise, mods, weight_a, weight_b, latent, *refs):
@@ -299,7 +302,7 @@
         in_specs=[smem_spec()] * 4 + [vmem_spec()] * 6,
         out_specs=[vmem_spec()] * 5,
         out_shape=[jax.ShapeDtypeStruct((own, width), jnp.bfloat16)]
-        + [jax.ShapeDtypeStruct((cols // length // 2, tokens + EXTRA_ROWS, 3 * length), jnp.bfloat16)] * 4,
+        + [jax.ShapeDtypeStruct((cols // length // 2 * tokens + EXTRA_ROWS, 3 * length), jnp.bfloat16)] * 4,
         scratch_shapes=[
             pltpu.VMEM((length, width), jnp.bfloat16),
             pltpu.VMEM((length, width), jnp.bfloat16),
@@ -314,8 +317,9 @@
     _, _, length, unit = out.shape
     tokens = 2 * length
     for index, (kept, other) in enumerate(((kept_a, other_a), (kept_b, other_b))):
-        mixed = kept[...] + other[...].astype(jnp.float32)
-        extra = mixed[tokens:]
+        mixed = kept[pl.ds(0, tokens), :] + other[pl.ds(0, tokens), :].astype(jnp.float32)
+        theirs = other[pl.ds(tokens, EXTRA_ROWS), :].astype(jnp.float32)
+        extra = kept[pl.ds(2 * tokens, EXTRA_ROWS), :][0:4] + theirs[4:8]
         for level in range(2):
             rows_at = slice(level * length, (level + 1) * length)
             squares = jnp.broadcast_to(extra[2 + level : 3 + level, :unit], (unit, unit)).T
@@ -342,7 +346,7 @@
 
 def attend_part(kept_a, other_a, kept_b, other_b, gains, width):
     unit = kept_a.shape[1] // 3
-    length = (kept_a.shape[0] - EXTRA_ROWS) // 2
+    length = (kept_a.shape[0] - EXTRA_ROWS) // 4
     return pl.pallas_call(
         lambda *refs: attend_kernel(width, *refs),
         in_specs=[vmem_spec()] * 5,
@@ -491,9 +495,10 @@
     gains = take(gains, gain_at, unit, 2)
     arrived_b, arrived_a, out_a, out_b, gains = lax.optimization_barrier((arrived_b, arrived_a, out_a, out_b, gains))
     sum_a, sum_b = both(kept_a, arrived_a), both(kept_b, arrived_b)
-    last_a = exchange(sum_a[1].astype(jnp.bfloat16), "mp", 2)
-    last_b = exchange(sum_b[1].astype(jnp.bfloat16), "mp", 1)
-    head = attend_part(sum_a[0], last_a, sum_b[0], last_b, gains, D)
+    second = (sum_a.shape[0] - EXTRA_ROWS) // 2
+    last_a = exchange(sum_a[second:].astype(jnp.bfloat16), "mp", 2)
+    last_b = exchange(sum_b[second:].astype(jnp.bfloat16), "mp", 1)
+    head = attend_part(sum_a, last_a, sum_b, last_b, gains, D)
     near, far = exchange(head, "mp", 1), exchange(head, "mp", 2)
     gathered = head, near, far, exchange(far, "mp", 1)
 

time: 86.7 us -> 86.2 us (level)
  no operation moved by 1% of the time
where the time goes in v5:
time: 86.2 us; the launch traced here: 86 us
  waiting for transfers between devices  38.6 us (45%)
  starting transfers between devices  24.1 us (28%)
  Pallas kernels  14 us (16%)
  local copies, waits for them, and re-layouts  3.75 us (4%)
  matrix products  3.34 us (4%)
  other arithmetic  1.39 us (2%)
    ppermute x13, waiting for transfers between devices, exchange(): lax.ppermute(array, axis, [(i, i ^ bit) for i in range(lax.axis_size(axis...  34.9 us
    ppermute x13, starting transfers between devices, exchange(): lax.ppermute(array, axis, [(i, i ^ bit) for i in range(lax.axis_size(axis...  22.3 us
    pallas_call x2, Pallas kernels, grad_part(): pl.pallas_call(grad_kernel, grid_spec=grid_spec, out_shape=jax.ShapeDtype...  4.09 us
    pallas_call x1, Pallas kernels, qkv_part(): pl.pallas_call(qkv_kernel, in_specs=[smem_spec()] * 4 + [vmem_spec()] * 6...  3.99 us
    ppermute x1, waiting for transfers between devices, heads_per_role(): lax.ppermute(total, ('role', 'seq'), [(i, i ^ 2 * lax.axis_size('seq') +...  3.7 us
    pallas_call x1, Pallas kernels, load_part(): pl.pallas_call(load_kernel, in_specs=[smem_spec()] + [vmem_spec()] * 3 +...  3.51 us
    dynamic_slice x2, local copies, waits for them, and re-layouts, take(): lax.dynamic_slice_in_dim(array, begin, size, axis=axis, allow_negative_in...  3.37 us
    dot_general x2, matrix products, dot32(): return jnp.dot(a, b, preferred_element_type=jnp.float32)  3.34 us
  transfers between devices with their start and end apart: 14, of which 9 were waited for; matrix products, arithmetic and copies ran while one was open for 3% of the time, Pallas kernels for 6%

profile of v5, /device:TPU:1, one launch (start us, length us, event | category | flops | bytes accessed | tf_op | source)
XLA Modules:
  0.0 86.0 jit_solution(1017265816582457539)
XLA Ops:
  0.6 0.0 copy-start
  0.6 0.0 copy-start.2
  0.7 0.8 convert_element_type.42
  1.5 0.1 fusion.11
  1.6 0.0 copy-start.3
  1.6 3.1 %fusion.2.product = f32[128,640]{1,0:T(8,128)S(1)} fusion(bf16[128,2048]{1,0:T(8,128)(2,1)} %param.14, bf16[2048,1280]{1,0:T(8,128)(2,1)} %param.16, s32[]{:T(128)S(6)} %mul.47), kind=kOutput, calls=%fused_computation.2 | convolution fusion | flops 335544320 | bytes 3473412 | tf_op jit(solution)/shard_map/dot_general | solution.py:144
  4.7 0.0 copy-done
  4.7 0.3 fusion.5.gate
  5.0 1.0 %constant_dynamic-slice_fusion.2 = (bf16[64,640]{1,0:T(8,128)(2,1)S(1)}, bf16[64,640]{1,0:T(8,128)(2,1)S(1)}) fusion(bf16[64,1280]{1,0:T(8,128)(2,1)} %noise.1, s32[]{:T(128)S(6)} %mul.47, bf16[64,1280]{1,0:T(8,128)(2,1)} %param.15), kind=kLoop, calls=%fused_computation.25 | loop fusion | bytes 327684 | tf_op jit(solution)/shard_map/dynamic_slice | solution.py:435
  6.0 0.1 pack_part.1
  6.1 2.1 %collective-permute-start = (bf16[192,640]{1,0:T(8,128)(2,1)S(1)}, bf16[192,640]{1,0:T(8,128)(2,1)S(1)}, u32[]{:S(2)}, u32[]{:S(2)}) collective-permute-start(bf16[192,640]{1,0:T(8,128)(2,1)S(1)} %get-tuple-element.37), channel_id=1, source_target_pairs={{0,4},{4,0},{1,5},{5,1},{2,6},{6,2},{3,7},{7,3},{8,12},{12,8},{9,1... | collective-permute-start | bytes 737288 | tf_op jit(solution)/shard_map/ppermute | solution.py:431
  8.2 0.0 copy-done.2
  8.2 0.0 copy-done.3
  8.2 0.0 copy-start.8
  8.2 0.0 copy-start.4
  8.2 3.5 %load_part.1 = (bf16[3,1280,512]{2,1,0:T(8,128)(2,1)S(1)}, bf16[3,1280,512]{2,1,0:T(8,128)(2,1)S(1)}, f32[2,3,8,1280]{3,2,1,0:T(8,128)S(1)}) custom-call(s32[1]{0:T(128)} %bitcast.4.start, bf16[8,256]{1,0:T(8,128)(2,1)S(1)} %fusion.9.embed, bf16[3,256,1280]{2,1,0:T(8,128)(2,1)S(1)} %bitcast.18, bf16[3,256,1280]{2,1,0:T(8,128)(2,1)S(1)} %bitcast.19, ...), custom_call_target="tpu_custom_call" | custom-call | tf_op jit(solution)/shard_map/load_part/pallas_call | solution.py:209
  11.8 0.0 copy-start.6
  11.8 0.0 copy-start.7
  11.8 1.9 %collective-permute-done.arrived = bf16[192,640]{1,0:T(8,128)(2,1)S(1)} collective-permute-done((bf16[192,640]{1,0:T(8,128)(2,1)S(1)}, bf16[192,640]{1,0:T(8,128)(2,1)S(1)}, u32[]{:S(2)}, u32[]{:S(2)}) %collective-permute-start) | collective-permute-done | bytes 245792 | tf_op jit(solution)/shard_map/ppermute | solution.py:431
  13.8 1.5 %collective-permute-start.1 = (bf16[192,640]{1,0:T(8,128)(2,1)S(1)}, bf16[192,640]{1,0:T(8,128)(2,1)S(1)}, u32[]{:S(2)}, u32[]{:S(2)}) collective-permute-start(bf16[192,640]{1,0:T(8,128)(2,1)S(1)} %join_part.1.joined), channel_id=1, source_target_pairs={{0,8},{8,0},{16,24},{24,16},{1,9},{9,1},{17,25},{25,17},{2,10},{10... | collective-permute-start | bytes 737288 | tf_op jit(solution)/shard_map/ppermute | solution.py:431
  15.2 0.0 copy-done.8
  15.3 0.1 convert_multiply_fusion.levels
  15.3 1.1 %collective-permute-done.1.swapped = bf16[192,640]{1,0:T(8,128)(2,1)S(1)} collective-permute-done((bf16[192,640]{1,0:T(8,128)(2,1)S(1)}, bf16[192,640]{1,0:T(8,128)(2,1)S(1)}, u32[]{:S(2)}, u32[]{:S(2)}) %collective-permute-start.1) | collective-permute-done | bytes 245792 | tf_op jit(solution)/shard_map/ppermute | solution.py:431
  16.4 0.0 copy-done.4
  16.4 4.0 %qkv_part.1 = (bf16[64,1280]{1,0:T(8,128)(2,1)}, bf16[528,384]{1,0:T(8,128)(2,1)S(1)}, bf16[528,384]{1,0:T(8,128)(2,1)S(1)}, bf16[528,384]{1,0:T(8,128)(2,1)S(1)}, bf16[528,384]{1,0:T(8,128)(2,1)S(1)}) custom-call(s32[1]{0:T(128)} %bitcast.seq, s32[1]{0:T(128)} %bitcast.1.core.half, s32[1]{0:T(128)} %bitcast.2.mine, f32[2]{0:T(128)S(1)} %convert_multiply_fusion.levels, ...), custom_call_target="tpu_custom_call" | custom-call | tf_op jit(solution)/shard_map/qkv_part/pallas_call | solution.py:300
  20.4 2.6 %collective-permute-start.2 = (bf16[528,384]{1,0:T(8,128)(2,1)S(1)}, bf16[528,384]{1,0:T(8,128)(2,1)S(1)}, u32[]{:S(2)}, u32[]{:S(2)}) collective-permute-start(bf16[528,384]{1,0:T(8,128)(2,1)S(1)} %get-tuple-element.49), channel_id=1, source_target_pairs={{0,2},{1,3},{2,0},{3,1},{4,6},{5,7},{6,4},{7,5},{8,10},{9,11},{10,... | collective-permute-start | bytes 1216520 | tf_op jit(solution)/shard_map/ppermute | solution.py:431
  22.9 1.3 %collective-permute-start.3 = (bf16[528,384]{1,0:T(8,128)(2,1)S(1)}, bf16[528,384]{1,0:T(8,128)(2,1)S(1)}, u32[]{:S(2)}, u32[]{:S(2)}) collective-permute-start(bf16[528,384]{1,0:T(8,128)(2,1)S(1)} %get-tuple-element.50), channel_id=1, source_target_pairs={{0,1},{1,0},{2,3},{3,2},{4,5},{5,4},{6,7},{7,6},{8,9},{9,8},{10,11... | collective-permute-start | bytes 1216520 | tf_op jit(solution)/shard_map/ppermute | solution.py:431
  24.3 0.0 copy-done.6
  24.3 0.0 copy-done.7
  24.3 0.1 fusion.10.refs_4_
  24.3 2.3 %constant_dynamic-slice_fusion = (bf16[512,1280]{1,0:T(8,128)(2,1)S(1)}, bf16[512,1280]{1,0:T(8,128)(2,1)S(1)}) fusion(bf16[2048,1280]{1,0:T(8,128)(2,1)} %param.25, s32[]{:T(128)} %mul.48, bf16[2048,1280]{1,0:T(8,128)(2,1)} %param.21), kind=kLoop, calls=%fused_computation.23 | loop fusion | bytes 5242884 | tf_op jit(solution)/shard_map/dynamic_slice | solution.py:435
  26.7 14.4 %collective-permute-done.2 = bf16[528,384]{1,0:T(8,128)(2,1)S(1)} collective-permute-done((bf16[528,384]{1,0:T(8,128)(2,1)S(1)}, bf16[528,384]{1,0:T(8,128)(2,1)S(1)}, u32[]{:S(2)}, u32[]{:S(2)}) %collective-permute-start.2) | collective-permute-done | bytes 405536 | tf_op jit(solution)/shard_map/ppermute | solution.py:431
  41.0 0.0 collective-permute-done.3
  41.0 0.0 copy-start.5
  41.0 0.1 convert_add_fusion.1.refs_0_
  41.2 1.2 %collective-permute-start.4 = (bf16[272,384]{1,0:T(8,128)(2,1)S(1)}, bf16[272,384]{1,0:T(8,128)(2,1)S(1)}, u32[]{:S(2)}, u32[]{:S(2)}) collective-permute-start(bf16[272,384]{1,0:T(8,128)(2,1)S(1)} %slice.26), channel_id=1, source_target_pairs={{0,2},{1,3},{2,0},{3,1},{4,6},{5,7},{6,4},{7,5},{8,10},{9,11},{10,... | collective-permute-start | bytes 626696 | tf_op jit(solution)/shard_map/ppermute | solution.py:431
  42.4 0.1 convert_add_fusion.refs_2_
  42.5 2.9 %collective-permute-start.5 = (bf16[272,384]{1,0:T(8,128)(2,1)S(1)}, bf16[272,384]{1,0:T(8,128)(2,1)S(1)}, u32[]{:S(2)}, u32[]{:S(2)}) collective-permute-start(bf16[272,384]{1,0:T(8,128)(2,1)S(1)} %slice.25), channel_id=1, source_target_pairs={{0,1},{1,0},{2,3},{3,2},{4,5},{5,4},{6,7},{7,6},{8,9},{9,8},{10,11... | collective-permute-start | bytes 626696 | tf_op jit(solution)/shard_map/ppermute | solution.py:431
  45.4 6.8 %collective-permute-done.4.refs_1_ = bf16[272,384]{1,0:T(8,128)(2,1)S(1)} collective-permute-done((bf16[272,384]{1,0:T(8,128)(2,1)S(1)}, bf16[272,384]{1,0:T(8,128)(2,1)S(1)}, u32[]{:S(2)}, u32[]{:S(2)}) %collective-permute-start.4) | collective-permute-done | bytes 208928 | tf_op jit(solution)/shard_map/ppermute | solution.py:431
  52.3 0.0 collective-permute-done.5.refs_3_
  52.3 1.3 %attend_part.1.refs_0_ = bf16[2,2,128,128]{3,2,1,0:T(8,128)(2,1)S(1)} custom-call(f32[528,384]{1,0:T(8,128)S(1)} %convert_add_fusion.1.refs_0_, bf16[272,384]{1,0:T(8,128)(2,1)S(1)} %collective-permute-done.4.refs_1_, f32[528,384]{1,0:T(8,128)S(1)} %convert_add_fusion.refs_2_, bf16[272,384]{1,0:T(8,128)(2,1)S(1)} %collective-permute-done.5.refs_3_, ...), custom_call_target="tpu_custom_call" | custom-call | tf_op jit(solution)/shard_map/attend_part/pallas_call | solution.py:350
  53.5 2.0 %collective-permute-start.7 = (bf16[2,2,128,128]{3,2,1,0:T(8,128)(2,1)S(1)}, bf16[2,2,128,128]{3,2,1,0:T(8,128)(2,1)S(1)}, u32[]{:S(2)}, u32[]{:S(2)}) collective-permute-start(bf16[2,2,128,128]{3,2,1,0:T(8,128)(2,1)S(1)} %attend_part.1.refs_0_), channel_id=1, source_target_pairs={{0,2},{1,3},{2,0},{3,1},{4,6},{5,7},{6,4},{7,5},{8,10},{9,11},{10,... | collective-permute-start | bytes 393224 | tf_op jit(solution)/shard_map/ppermute | solution.py:431
  55.6 1.8 %collective-permute-start.6 = (bf16[2,2,128,128]{3,2,1,0:T(8,128)(2,1)S(1)}, bf16[2,2,128,128]{3,2,1,0:T(8,128)(2,1)S(1)}, u32[]{:S(2)}, u32[]{:S(2)}) collective-permute-start(bf16[2,2,128,128]{3,2,1,0:T(8,128)(2,1)S(1)} %attend_part.1.refs_0_), channel_id=1, source_target_pairs={{0,1},{1,0},{2,3},{3,2},{4,5},{5,4},{6,7},{7,6},{8,9},{9,8},{10,11... | collective-permute-start | bytes 393224 | tf_op jit(solution)/shard_map/ppermute | solution.py:431
  57.4 2.4 %collective-permute-done.7.refs_2_ = bf16[2,2,128,128]{3,2,1,0:T(8,128)(2,1)S(1)} collective-permute-done((bf16[2,2,128,128]{3,2,1,0:T(8,128)(2,1)S(1)}, bf16[2,2,128,128]{3,2,1,0:T(8,128)(2,1)S(1)}, u32[]{:S(2)}, u32[]{:S(2)}) %collective-permute-start.7) | collective-permute-done | bytes 131104 | tf_op jit(solution)/shard_map/ppermute | solution.py:431
  59.8 1.3 %collective-permute-start.8 = (bf16[2,2,128,128]{3,2,1,0:T(8,128)(2,1)S(1)}, bf16[2,2,128,128]{3,2,1,0:T(8,128)(2,1)S(1)}, u32[]{:S(2)}, u32[]{:S(2)}) collective-permute-start(bf16[2,2,128,128]{3,2,1,0:T(8,128)(2,1)S(1)} %collective-permute-done.7.refs_2_), channel_id=1, source_target_pairs={{0,1},{1,0},{2,3},{3,2},{4,5},{5,4},{6,7},{7,6},{8,9},{9,8},{10,11... | collective-permute-start | bytes 393224 | tf_op jit(solution)/shard_map/ppermute | solution.py:431
  61.2 0.0 collective-permute-done.6.refs_1_
  61.2 3.1 %collective-permute-done.8.refs_3_ = bf16[2,2,128,128]{3,2,1,0:T(8,128)(2,1)S(1)} collective-permute-done((bf16[2,2,128,128]{3,2,1,0:T(8,128)(2,1)S(1)}, bf16[2,2,128,128]{3,2,1,0:T(8,128)(2,1)S(1)}, u32[]{:S(2)}, u32[]{:S(2)}) %collective-permute-start.8) | collective-permute-done | bytes 131104 | tf_op jit(solution)/shard_map/ppermute | solution.py:431
  64.3 1.0 %out_part.1 = (f32[128,640]{1,0:T(8,128)S(1)}, bf16[128,640]{1,0:T(8,128)(2,1)S(1)}) custom-call(s32[1]{0:T(128)} %bitcast.1.core.half, s32[1]{0:T(128)} %bitcast.2.mine, bf16[2,2,128,128]{3,2,1,0:T(8,128)(2,1)S(1)} %attend_part.1.refs_0_, bf16[2,2,128,128]{3,2,1,0:T(8,128)(2,1)S(1)} %collective-permute-done.6.refs_1_, ...), custom_call_target="tpu_custom_call" | custom-call | tf_op jit(solution)/shard_map/out_part/pallas_call | solution.py:384
  65.2 4.0 %collective-permute-start.9 = (bf16[128,640]{1,0:T(8,128)(2,1)S(1)}, bf16[128,640]{1,0:T(8,128)(2,1)S(1)}, u32[]{:S(2)}, u32[]{:S(2)}) collective-permute-start(bf16[128,640]{1,0:T(8,128)(2,1)S(1)} %get-tuple-element.59), channel_id=1, source_target_pairs={{0,8},{8,0},{16,24},{24,16},{1,9},{9,1},{17,25},{25,17},{2,10},{10... | collective-permute-start | bytes 491528 | tf_op jit(solution)/shard_map/ppermute | solution.py:431
  69.3 1.0 %collective-permute-done.9 = bf16[128,640]{1,0:T(8,128)(2,1)S(1)} collective-permute-done((bf16[128,640]{1,0:T(8,128)(2,1)S(1)}, bf16[128,640]{1,0:T(8,128)(2,1)S(1)}, u32[]{:S(2)}, u32[]{:S(2)}) %collective-permute-start.9) | collective-permute-done | bytes 163872 | tf_op jit(solution)/shard_map/ppermute | solution.py:431
  70.3 1.7 %collective-permute-start.12 = (bf16[128,640]{1,0:T(8,128)(2,1)S(1)}, bf16[128,640]{1,0:T(8,128)(2,1)S(1)}, u32[]{:S(2)}, u32[]{:S(2)}) collective-permute-start(bf16[128,640]{1,0:T(8,128)(2,1)S(1)} %add_convert_fusion), channel_id=1, source_target_pairs={{0,20},{4,16},{8,28},{12,24},{16,4},{20,0},{24,12},{28,8},{1,21},{... | collective-permute-start | bytes 491528 | tf_op jit(solution)/shard_map/ppermute | solution.py:509
  72.1 0.2 collective-permute-start.11
  72.3 0.8 collective-permute-start.10
  73.1 3.7 %collective-permute-done.12 = bf16[128,640]{1,0:T(8,128)(2,1)S(1)} collective-permute-done((bf16[128,640]{1,0:T(8,128)(2,1)S(1)}, bf16[128,640]{1,0:T(8,128)(2,1)S(1)}, u32[]{:S(2)}, u32[]{:S(2)}) %collective-permute-start.12) | collective-permute-done | bytes 163872 | tf_op jit(solution)/shard_map/ppermute | solution.py:509
  76.8 4.2 %collective-permute-done.11 = bf16[128,640]{1,0:T(8,128)(2,1)S(1)} collective-permute-done((bf16[128,640]{1,0:T(8,128)(2,1)S(1)}, bf16[128,640]{1,0:T(8,128)(2,1)S(1)}, u32[]{:S(2)}, u32[]{:S(2)}) %collective-permute-start.11) | collective-permute-done | bytes 163872 | tf_op jit(solution)/shard_map/ppermute | solution.py:431
  80.9 0.0 collective-permute-done.10
  80.9 0.1 multiply_convert_fusion.rows
  81.1 0.6 collective-permute-start.13
  81.6 0.0 copy-done.5
  81.6 0.3 copy.18
  81.9 2.1 %grad_part.2.refs_0_ = bf16[2048,1280]{1,0:T(8,128)(2,1)} custom-call(s32[1]{0:T(128)} %bitcast.1.core.half, bf16[2048,128]{1,0:T(8,128)(2,1)S(1)} %bitcast.16, bf16[128,640]{1,0:T(8,128)(2,1)S(1)} %multiply_convert_fusion.rows), custom_call_target="tpu_custom_call" | custom-call | tf_op jit(solution)/shard_map/grad_part/pallas_call | solution.py:420
  83.9 0.0 collective-permute-done.13.rows
  84.0 2.0 %grad_part.3 = bf16[2048,1280]{1,0:T(8,128)(2,1)} custom-call(s32[1]{0:T(128)} %bitcast.9.half, bf16[2048,128]{1,0:T(8,128)(2,1)S(1)} %bitcast.17, bf16[128,640]{1,0:T(8,128)(2,1)S(1)} %collective-permute-done.13.rows, bf16[2048,1280]{1,0:T(8,128)(2,1)} %grad_part.2.refs_0_), custom_call_target="tpu_custom_call", output_to_operand_aliasing={{}: (3, {})} | custom-call | tf_op jit(solution)/shard_map/grad_part/pallas_call | solution.py:420
  86.0 0.0 copy-done.1
  (8 shorter events, 0.2 us)
Async XLA Ops:
  0.6 4.1 %copy-start = (bf16[256,1280]{1,0:T(8,128)(2,1)S(1)}, bf16[256,1280]{1,0:T(8,128)(2,1)}, u32[]{:S(2)}) copy-start(bf16[256,1280]{1,0:T(8,128)(2,1)} %param.17) | copy-start | bytes 1966084
  0.6 7.6 %copy-start.2 = (bf16[256,3,1280]{2,0,1:T(8,128)(2,1)S(1)}, bf16[256,3,1280]{2,0,1:T(8,128)(2,1)}, u32[]{:S(2)}) copy-start(bf16[256,3,1280]{2,0,1:T(8,128)(2,1)} %param.22) | copy-start | bytes 5898244
  1.6 6.6 %copy-start.3 = (bf16[256,3,1280]{2,0,1:T(8,128)(2,1)S(1)}, bf16[256,3,1280]{2,0,1:T(8,128)(2,1)}, u32[]{:S(2)}) copy-start(bf16[256,3,1280]{2,0,1:T(8,128)(2,1)} %param.26) | copy-start | bytes 5898244
  6.1 7.6 %collective-permute-start = (bf16[192,640]{1,0:T(8,128)(2,1)S(1)}, bf16[192,640]{1,0:T(8,128)(2,1)S(1)}, u32[]{:S(2)}, u32[]{:S(2)}) collective-permute-start(bf16[192,640]{1,0:T(8,128)(2,1)S(1)} %get-tuple-element.37), channel_id=1, source_target_pairs={{0,4},{4,0},{1,5},{5,1},{2,6},{6,2},{3,7},{7,3},{8,12},{12,8},{9,1... | collective-permute-start | bytes 737288 | tf_op jit(solution)/shard_map/ppermute | solution.py:431
  8.2 7.0 %copy-start.8 = (s32[3]{0:T(128)S(1)}, s32[3]{0:T(128)}, u32[]{:S(2)}) copy-start(s32[3]{0:T(128)} %param.19) | copy-start | bytes 40
  8.2 8.2 %copy-start.4 = (bf16[64,1280]{1,0:T(8,128)(2,1)S(1)}, bf16[64,1280]{1,0:T(8,128)(2,1)}, u32[]{:S(2)}) copy-start(bf16[64,1280]{1,0:T(8,128)(2,1)} %noise.1) | copy-start | bytes 491524
  11.8 12.5 %copy-start.6 = (f32[2,2048]{1,0:T(2,128)S(1)}, f32[2,2048]{1,0:T(2,128)}, u32[]{:S(2)}) copy-start(f32[2,2048]{1,0:T(2,128)} %param.23) | copy-start | bytes 49156
  11.8 12.5 %copy-start.7 = (f32[2,2048]{1,0:T(2,128)S(1)}, f32[2,2048]{1,0:T(2,128)}, u32[]{:S(2)}) copy-start(f32[2,2048]{1,0:T(2,128)} %param.27) | copy-start | bytes 49156
  13.8 2.6 %collective-permute-start.1 = (bf16[192,640]{1,0:T(8,128)(2,1)S(1)}, bf16[192,640]{1,0:T(8,128)(2,1)S(1)}, u32[]{:S(2)}, u32[]{:S(2)}) collective-permute-start(bf16[192,640]{1,0:T(8,128)(2,1)S(1)} %join_part.1.joined), channel_id=1, source_target_pairs={{0,8},{8,0},{16,24},{24,16},{1,9},{9,1},{17,25},{25,17},{2,10},{10... | collective-permute-start | bytes 737288 | tf_op jit(solution)/shard_map/ppermute | solution.py:431
  20.4 20.6 %collective-permute-start.2 = (bf16[528,384]{1,0:T(8,128)(2,1)S(1)}, bf16[528,384]{1,0:T(8,128)(2,1)S(1)}, u32[]{:S(2)}, u32[]{:S(2)}) collective-permute-start(bf16[528,384]{1,0:T(8,128)(2,1)S(1)} %get-tuple-element.49), channel_id=1, source_target_pairs={{0,2},{1,3},{2,0},{3,1},{4,6},{5,7},{6,4},{7,5},{8,10},{9,11},{10,... | collective-permute-start | bytes 1216520 | tf_op jit(solution)/shard_map/ppermute | solution.py:431
  22.9 18.1 %collective-permute-start.3 = (bf16[528,384]{1,0:T(8,128)(2,1)S(1)}, bf16[528,384]{1,0:T(8,128)(2,1)S(1)}, u32[]{:S(2)}, u32[]{:S(2)}) collective-permute-start(bf16[528,384]{1,0:T(8,128)(2,1)S(1)} %get-tuple-element.50), channel_id=1, source_target_pairs={{0,1},{1,0},{2,3},{3,2},{4,5},{5,4},{6,7},{7,6},{8,9},{9,8},{10,11... | collective-permute-start | bytes 1216520 | tf_op jit(solution)/shard_map/ppermute | solution.py:431
  41.0 40.6 %copy-start.5 = (bf16[128,2048]{1,0:T(8,128)(2,1)S(1)}, bf16[128,2048]{1,0:T(8,128)(2,1)}, u32[]{:S(2)}) copy-start(bf16[128,2048]{1,0:T(8,128)(2,1)} %param.14) | copy-start | bytes 1572868
  41.2 11.1 %collective-permute-start.4 = (bf16[272,384]{1,0:T(8,128)(2,1)S(1)}, bf16[272,384]{1,0:T(8,128)(2,1)S(1)}, u32[]{:S(2)}, u32[]{:S(2)}) collective-permute-start(bf16[272,384]{1,0:T(8,128)(2,1)S(1)} %slice.26), channel_id=1, source_target_pairs={{0,2},{1,3},{2,0},{3,1},{4,6},{5,7},{6,4},{7,5},{8,10},{9,11},{10,... | collective-permute-start | bytes 626696 | tf_op jit(solution)/shard_map/ppermute | solution.py:431
  42.5 9.8 %collective-permute-start.5 = (bf16[272,384]{1,0:T(8,128)(2,1)S(1)}, bf16[272,384]{1,0:T(8,128)(2,1)S(1)}, u32[]{:S(2)}, u32[]{:S(2)}) collective-permute-start(bf16[272,384]{1,0:T(8,128)(2,1)S(1)} %slice.25), channel_id=1, source_target_pairs={{0,1},{1,0},{2,3},{3,2},{4,5},{5,4},{6,7},{7,6},{8,9},{9,8},{10,11... | collective-permute-start | bytes 626696 | tf_op jit(solution)/shard_map/ppermute | solution.py:431
  53.5 6.3 %collective-permute-start.7 = (bf16[2,2,128,128]{3,2,1,0:T(8,128)(2,1)S(1)}, bf16[2,2,128,128]{3,2,1,0:T(8,128)(2,1)S(1)}, u32[]{:S(2)}, u32[]{:S(2)}) collective-permute-start(bf16[2,2,128,128]{3,2,1,0:T(8,128)(2,1)S(1)} %attend_part.1.refs_0_), channel_id=1, source_target_pairs={{0,2},{1,3},{2,0},{3,1},{4,6},{5,7},{6,4},{7,5},{8,10},{9,11},{10,... | collective-permute-start | bytes 393224 | tf_op jit(solution)/shard_map/ppermute | solution.py:431
  55.6 5.6 %collective-permute-start.6 = (bf16[2,2,128,128]{3,2,1,0:T(8,128)(2,1)S(1)}, bf16[2,2,128,128]{3,2,1,0:T(8,128)(2,1)S(1)}, u32[]{:S(2)}, u32[]{:S(2)}) collective-permute-start(bf16[2,2,128,128]{3,2,1,0:T(8,128)(2,1)S(1)} %attend_part.1.refs_0_), channel_id=1, source_target_pairs={{0,1},{1,0},{2,3},{3,2},{4,5},{5,4},{6,7},{7,6},{8,9},{9,8},{10,11... | collective-permute-start | bytes 393224 | tf_op jit(solution)/shard_map/ppermute | solution.py:431
  59.8 4.4 %collective-permute-start.8 = (bf16[2,2,128,128]{3,2,1,0:T(8,128)(2,1)S(1)}, bf16[2,2,128,128]{3,2,1,0:T(8,128)(2,1)S(1)}, u32[]{:S(2)}, u32[]{:S(2)}) collective-permute-start(bf16[2,2,128,128]{3,2,1,0:T(8,128)(2,1)S(1)} %collective-permute-done.7.refs_2_), channel_id=1, source_target_pairs={{0,1},{1,0},{2,3},{3,2},{4,5},{5,4},{6,7},{7,6},{8,9},{9,8},{10,11... | collective-permute-start | bytes 393224 | tf_op jit(solution)/shard_map/ppermute | solution.py:431
  65.2 5.1 %collective-permute-start.9 = (bf16[128,640]{1,0:T(8,128)(2,1)S(1)}, bf16[128,640]{1,0:T(8,128)(2,1)S(1)}, u32[]{:S(2)}, u32[]{:S(2)}) collective-permute-start(bf16[128,640]{1,0:T(8,128)(2,1)S(1)} %get-tuple-element.59), channel_id=1, source_target_pairs={{0,8},{8,0},{16,24},{24,16},{1,9},{9,1},{17,25},{25,17},{2,10},{10... | collective-permute-start | bytes 491528 | tf_op jit(solution)/shard_map/ppermute | solution.py:431
  70.3 6.4 %collective-permute-start.12 = (bf16[128,640]{1,0:T(8,128)(2,1)S(1)}, bf16[128,640]{1,0:T(8,128)(2,1)S(1)}, u32[]{:S(2)}, u32[]{:S(2)}) collective-permute-start(bf16[128,640]{1,0:T(8,128)(2,1)S(1)} %add_convert_fusion), channel_id=1, source_target_pairs={{0,20},{4,16},{8,28},{12,24},{16,4},{20,0},{24,12},{28,8},{1,21},{... | collective-permute-start | bytes 491528 | tf_op jit(solution)/shard_map/ppermute | solution.py:509
  72.1 8.8 %collective-permute-start.11 = (bf16[128,640]{1,0:T(8,128)(2,1)S(1)}, bf16[128,640]{1,0:T(8,128)(2,1)S(1)}, u32[]{:S(2)}, u32[]{:S(2)}) collective-permute-start(bf16[128,640]{1,0:T(8,128)(2,1)S(1)} %add_convert_fusion), channel_id=1, source_target_pairs={{0,16},{8,24},{16,0},{24,8},{1,17},{9,25},{17,1},{25,9},{2,18},{10... | collective-permute-start | bytes 491528 | tf_op jit(solution)/shard_map/ppermute | solution.py:431
  72.3 8.7 %collective-permute-start.10 = (bf16[128,640]{1,0:T(8,128)(2,1)S(1)}, bf16[128,640]{1,0:T(8,128)(2,1)S(1)}, u32[]{:S(2)}, u32[]{:S(2)}) collective-permute-start(bf16[128,640]{1,0:T(8,128)(2,1)S(1)} %add_convert_fusion), channel_id=1, source_target_pairs={{0,4},{4,0},{1,5},{5,1},{2,6},{6,2},{3,7},{7,3},{8,12},{12,8},{9,1... | collective-permute-start | bytes 491528 | tf_op jit(solution)/shard_map/ppermute | solution.py:431
  81.1 2.9 %collective-permute-start.13 = (bf16[128,640]{1,0:T(8,128)(2,1)S(1)}, bf16[128,640]{1,0:T(8,128)(2,1)S(1)}, u32[]{:S(2)}, u32[]{:S(2)}) collective-permute-start(bf16[128,640]{1,0:T(8,128)(2,1)S(1)} %multiply_convert_fusion.rows), channel_id=1, source_target_pairs={{0,8},{8,0},{16,24},{24,16},{1,9},{9,1},{17,25},{25,17},{2,10},{10... | collective-permute-start | bytes 491528 | tf_op jit(solution)/shard_map/ppermute | solution.py:431
  83.9 2.0 %copy-start.1 = (bf16[256,1280]{1,0:T(8,128)(2,1)S(1)}, bf16[256,1280]{1,0:T(8,128)(2,1)}, u32[]{:S(2)}) copy-start(bf16[256,1280]{1,0:T(8,128)(2,1)} %param.17) | copy-start | bytes 1966084

commit v6 on v5

--- a/solution.py
+++ b/solution.py
@@ -513,8 +513,8 @@
     rows = (gate[0:1] * total).astype(jnp.bfloat16)
     heads_t = gen_heads.T
     theirs = exchange(rows, "role", 1)
-    weight_grad = grad_part(core, heads_t, rows, None, 2)
-    weight_grad = grad_part(other_core, heads_t, theirs, weight_grad, 2)
+    weight_grad = grad_part(core, heads_t, rows, None, 1)
+    weight_grad = grad_part(other_core, heads_t, theirs, weight_grad, 1)
     return latent, weight_grad
 
 

time: 86.2 us -> 86.7 us (level)
  transfers between devices with their start and end apart: 14 -> 14, of which waited for: 9 -> 9; matrix products, arithmetic and copies ran while one was open for 3% -> 3% of each run, Pallas kernels for 6% -> 7%
where the time goes in v6:
time: 86.7 us; the launch traced here: 86.5 us
  waiting for transfers between devices  38.6 us (45%)
  starting transfers between devices  24.1 us (28%)
  Pallas kernels  14.5 us (17%)
  local copies, waits for them, and re-layouts  3.75 us (4%)
  matrix products  3.34 us (4%)
  other arithmetic  1.39 us (2%)
    ppermute x13, waiting for transfers between devices, exchange(): lax.ppermute(array, axis, [(i, i ^ bit) for i in range(lax.axis_size(axis...  34.9 us
    ppermute x13, starting transfers between devices, exchange(): lax.ppermute(array, axis, [(i, i ^ bit) for i in range(lax.axis_size(axis...  22.3 us
    pallas_call x2, Pallas kernels, grad_part(): pl.pallas_call(grad_kernel, grid_spec=grid_spec, out_shape=jax.ShapeDtype...  4.64 us
    pallas_call x1, Pallas kernels, qkv_part(): pl.pallas_call(qkv_kernel, in_specs=[smem_spec()] * 4 + [vmem_spec()] * 6...  3.99 us
    ppermute x1, waiting for transfers between devices, heads_per_role(): lax.ppermute(total, ('role', 'seq'), [(i, i ^ 2 * lax.axis_size('seq') +...  3.7 us
    pallas_call x1, Pallas kernels, load_part(): pl.pallas_call(load_kernel, in_specs=[smem_spec()] + [vmem_spec()] * 3 +...  3.51 us
    dynamic_slice x2, local copies, waits for them, and re-layouts, take(): lax.dynamic_slice_in_dim(array, begin, size, axis=axis, allow_negative_in...  3.37 us
    dot_general x2, matrix products, dot32(): return jnp.dot(a, b, preferred_element_type=jnp.float32)  3.34 us
  transfers between devices with their start and end apart: 14, of which 9 were waited for; matrix products, arithmetic and copies ran while one was open for 3% of the time, Pallas kernels for 7%

profile of v6, /device:TPU:1, one launch (start us, length us, event | category | flops | bytes accessed | tf_op | source)
XLA Modules:
  0.0 86.5 jit_solution(5419265751613592890)
XLA Ops:
  0.6 0.0 copy-start
  0.6 0.0 copy-start.2
  0.7 0.8 convert_element_type.42
  1.5 0.1 fusion.11
  1.6 0.0 copy-start.3
  1.6 3.1 %fusion.2.product = f32[128,640]{1,0:T(8,128)S(1)} fusion(bf16[128,2048]{1,0:T(8,128)(2,1)} %param.14, bf16[2048,1280]{1,0:T(8,128)(2,1)} %param.16, s32[]{:T(128)S(6)} %mul.47), kind=kOutput, calls=%fused_computation.2 | convolution fusion | flops 335544320 | bytes 3473412 | tf_op jit(solution)/shard_map/dot_general | solution.py:144
  4.7 0.0 copy-done
  4.7 0.3 fusion.5.gate
  5.0 1.0 %constant_dynamic-slice_fusion.2 = (bf16[64,640]{1,0:T(8,128)(2,1)S(1)}, bf16[64,640]{1,0:T(8,128)(2,1)S(1)}) fusion(bf16[64,1280]{1,0:T(8,128)(2,1)} %noise.1, s32[]{:T(128)S(6)} %mul.47, bf16[64,1280]{1,0:T(8,128)(2,1)} %param.15), kind=kLoop, calls=%fused_computation.25 | loop fusion | bytes 327684 | tf_op jit(solution)/shard_map/dynamic_slice | solution.py:435
  6.0 0.1 pack_part.1
  6.1 2.1 %collective-permute-start = (bf16[192,640]{1,0:T(8,128)(2,1)S(1)}, bf16[192,640]{1,0:T(8,128)(2,1)S(1)}, u32[]{:S(2)}, u32[]{:S(2)}) collective-permute-start(bf16[192,640]{1,0:T(8,128)(2,1)S(1)} %get-tuple-element.37), channel_id=1, source_target_pairs={{0,4},{4,0},{1,5},{5,1},{2,6},{6,2},{3,7},{7,3},{8,12},{12,8},{9,1... | collective-permute-start | bytes 737288 | tf_op jit(solution)/shard_map/ppermute | solution.py:431
  8.2 0.0 copy-done.2
  8.2 0.0 copy-done.3
  8.2 0.0 copy-start.8
  8.2 0.0 copy-start.4
  8.2 3.5 %load_part.1 = (bf16[3,1280,512]{2,1,0:T(8,128)(2,1)S(1)}, bf16[3,1280,512]{2,1,0:T(8,128)(2,1)S(1)}, f32[2,3,8,1280]{3,2,1,0:T(8,128)S(1)}) custom-call(s32[1]{0:T(128)} %bitcast.4.start, bf16[8,256]{1,0:T(8,128)(2,1)S(1)} %fusion.9.embed, bf16[3,256,1280]{2,1,0:T(8,128)(2,1)S(1)} %bitcast.18, bf16[3,256,1280]{2,1,0:T(8,128)(2,1)S(1)} %bitcast.19, ...), custom_call_target="tpu_custom_call" | custom-call | tf_op jit(solution)/shard_map/load_part/pallas_call | solution.py:209
  11.8 0.0 copy-start.6
  11.8 0.0 copy-start.7
  11.8 1.9 %collective-permute-done.arrived = bf16[192,640]{1,0:T(8,128)(2,1)S(1)} collective-permute-done((bf16[192,640]{1,0:T(8,128)(2,1)S(1)}, bf16[192,640]{1,0:T(8,128)(2,1)S(1)}, u32[]{:S(2)}, u32[]{:S(2)}) %collective-permute-start) | collective-permute-done | bytes 245792 | tf_op jit(solution)/shard_map/ppermute | solution.py:431
  13.8 1.5 %collective-permute-start.1 = (bf16[192,640]{1,0:T(8,128)(2,1)S(1)}, bf16[192,640]{1,0:T(8,128)(2,1)S(1)}, u32[]{:S(2)}, u32[]{:S(2)}) collective-permute-start(bf16[192,640]{1,0:T(8,128)(2,1)S(1)} %join_part.1.joined), channel_id=1, source_target_pairs={{0,8},{8,0},{16,24},{24,16},{1,9},{9,1},{17,25},{25,17},{2,10},{10... | collective-permute-start | bytes 737288 | tf_op jit(solution)/shard_map/ppermute | solution.py:431
  15.2 0.0 copy-done.8
  15.3 0.1 convert_multiply_fusion.levels
  15.3 1.1 %collective-permute-done.1.swapped = bf16[192,640]{1,0:T(8,128)(2,1)S(1)} collective-permute-done((bf16[192,640]{1,0:T(8,128)(2,1)S(1)}, bf16[192,640]{1,0:T(8,128)(2,1)S(1)}, u32[]{:S(2)}, u32[]{:S(2)}) %collective-permute-start.1) | collective-permute-done | bytes 245792 | tf_op jit(solution)/shard_map/ppermute | solution.py:431
  16.4 0.0 copy-done.4
  16.4 4.0 %qkv_part.1 = (bf16[64,1280]{1,0:T(8,128)(2,1)}, bf16[528,384]{1,0:T(8,128)(2,1)S(1)}, bf16[528,384]{1,0:T(8,128)(2,1)S(1)}, bf16[528,384]{1,0:T(8,128)(2,1)S(1)}, bf16[528,384]{1,0:T(8,128)(2,1)S(1)}) custom-call(s32[1]{0:T(128)} %bitcast.seq, s32[1]{0:T(128)} %bitcast.1.core.half, s32[1]{0:T(128)} %bitcast.2.mine, f32[2]{0:T(128)S(1)} %convert_multiply_fusion.levels, ...), custom_call_target="tpu_custom_call" | custom-call | tf_op jit(solution)/shard_map/qkv_part/pallas_call | solution.py:300
  20.4 2.6 %collective-permute-start.2 = (bf16[528,384]{1,0:T(8,128)(2,1)S(1)}, bf16[528,384]{1,0:T(8,128)(2,1)S(1)}, u32[]{:S(2)}, u32[]{:S(2)}) collective-permute-start(bf16[528,384]{1,0:T(8,128)(2,1)S(1)} %get-tuple-element.49), channel_id=1, source_target_pairs={{0,2},{1,3},{2,0},{3,1},{4,6},{5,7},{6,4},{7,5},{8,10},{9,11},{10,... | collective-permute-start | bytes 1216520 | tf_op jit(solution)/shard_map/ppermute | solution.py:431
  22.9 1.3 %collective-permute-start.3 = (bf16[528,384]{1,0:T(8,128)(2,1)S(1)}, bf16[528,384]{1,0:T(8,128)(2,1)S(1)}, u32[]{:S(2)}, u32[]{:S(2)}) collective-permute-start(bf16[528,384]{1,0:T(8,128)(2,1)S(1)} %get-tuple-element.50), channel_id=1, source_target_pairs={{0,1},{1,0},{2,3},{3,2},{4,5},{5,4},{6,7},{7,6},{8,9},{9,8},{10,11... | collective-permute-start | bytes 1216520 | tf_op jit(solution)/shard_map/ppermute | solution.py:431
  24.3 0.0 copy-done.6
  24.3 0.0 copy-done.7
  24.3 0.1 fusion.10.refs_4_
  24.3 2.3 %constant_dynamic-slice_fusion = (bf16[512,1280]{1,0:T(8,128)(2,1)S(1)}, bf16[512,1280]{1,0:T(8,128)(2,1)S(1)}) fusion(bf16[2048,1280]{1,0:T(8,128)(2,1)} %param.25, s32[]{:T(128)} %mul.48, bf16[2048,1280]{1,0:T(8,128)(2,1)} %param.21), kind=kLoop, calls=%fused_computation.23 | loop fusion | bytes 5242884 | tf_op jit(solution)/shard_map/dynamic_slice | solution.py:435
  26.7 14.4 %collective-permute-done.2 = bf16[528,384]{1,0:T(8,128)(2,1)S(1)} collective-permute-done((bf16[528,384]{1,0:T(8,128)(2,1)S(1)}, bf16[528,384]{1,0:T(8,128)(2,1)S(1)}, u32[]{:S(2)}, u32[]{:S(2)}) %collective-permute-start.2) | collective-permute-done | bytes 405536 | tf_op jit(solution)/shard_map/ppermute | solution.py:431
  41.0 0.0 collective-permute-done.3
  41.0 0.0 copy-start.5
  41.0 0.1 convert_add_fusion.1.refs_0_
  41.2 1.2 %collective-permute-start.4 = (bf16[272,384]{1,0:T(8,128)(2,1)S(1)}, bf16[272,384]{1,0:T(8,128)(2,1)S(1)}, u32[]{:S(2)}, u32[]{:S(2)}) collective-permute-start(bf16[272,384]{1,0:T(8,128)(2,1)S(1)} %slice.26), channel_id=1, source_target_pairs={{0,2},{1,3},{2,0},{3,1},{4,6},{5,7},{6,4},{7,5},{8,10},{9,11},{10,... | collective-permute-start | bytes 626696 | tf_op jit(solution)/shard_map/ppermute | solution.py:431
  42.4 0.1 convert_add_fusion.refs_2_
  42.5 2.9 %collective-permute-start.5 = (bf16[272,384]{1,0:T(8,128)(2,1)S(1)}, bf16[272,384]{1,0:T(8,128)(2,1)S(1)}, u32[]{:S(2)}, u32[]{:S(2)}) collective-permute-start(bf16[272,384]{1,0:T(8,128)(2,1)S(1)} %slice.25), channel_id=1, source_target_pairs={{0,1},{1,0},{2,3},{3,2},{4,5},{5,4},{6,7},{7,6},{8,9},{9,8},{10,11... | collective-permute-start | bytes 626696 | tf_op jit(solution)/shard_map/ppermute | solution.py:431
  45.4 6.8 %collective-permute-done.4.refs_1_ = bf16[272,384]{1,0:T(8,128)(2,1)S(1)} collective-permute-done((bf16[272,384]{1,0:T(8,128)(2,1)S(1)}, bf16[272,384]{1,0:T(8,128)(2,1)S(1)}, u32[]{:S(2)}, u32[]{:S(2)}) %collective-permute-start.4) | collective-permute-done | bytes 208928 | tf_op jit(solution)/shard_map/ppermute | solution.py:431
  52.3 0.0 collective-permute-done.5.refs_3_
  52.3 1.3 %attend_part.1.refs_0_ = bf16[2,2,128,128]{3,2,1,0:T(8,128)(2,1)S(1)} custom-call(f32[528,384]{1,0:T(8,128)S(1)} %convert_add_fusion.1.refs_0_, bf16[272,384]{1,0:T(8,128)(2,1)S(1)} %collective-permute-done.4.refs_1_, f32[528,384]{1,0:T(8,128)S(1)} %convert_add_fusion.refs_2_, bf16[272,384]{1,0:T(8,128)(2,1)S(1)} %collective-permute-done.5.refs_3_, ...), custom_call_target="tpu_custom_call" | custom-call | tf_op jit(solution)/shard_map/attend_part/pallas_call | solution.py:350
  53.5 2.0 %collective-permute-start.7 = (bf16[2,2,128,128]{3,2,1,0:T(8,128)(2,1)S(1)}, bf16[2,2,128,128]{3,2,1,0:T(8,128)(2,1)S(1)}, u32[]{:S(2)}, u32[]{:S(2)}) collective-permute-start(bf16[2,2,128,128]{3,2,1,0:T(8,128)(2,1)S(1)} %attend_part.1.refs_0_), channel_id=1, source_target_pairs={{0,2},{1,3},{2,0},{3,1},{4,6},{5,7},{6,4},{7,5},{8,10},{9,11},{10,... | collective-permute-start | bytes 393224 | tf_op jit(solution)/shard_map/ppermute | solution.py:431
  55.6 1.8 %collective-permute-start.6 = (bf16[2,2,128,128]{3,2,1,0:T(8,128)(2,1)S(1)}, bf16[2,2,128,128]{3,2,1,0:T(8,128)(2,1)S(1)}, u32[]{:S(2)}, u32[]{:S(2)}) collective-permute-start(bf16[2,2,128,128]{3,2,1,0:T(8,128)(2,1)S(1)} %attend_part.1.refs_0_), channel_id=1, source_target_pairs={{0,1},{1,0},{2,3},{3,2},{4,5},{5,4},{6,7},{7,6},{8,9},{9,8},{10,11... | collective-permute-start | bytes 393224 | tf_op jit(solution)/shard_map/ppermute | solution.py:431
  57.4 2.4 %collective-permute-done.7.refs_2_ = bf16[2,2,128,128]{3,2,1,0:T(8,128)(2,1)S(1)} collective-permute-done((bf16[2,2,128,128]{3,2,1,0:T(8,128)(2,1)S(1)}, bf16[2,2,128,128]{3,2,1,0:T(8,128)(2,1)S(1)}, u32[]{:S(2)}, u32[]{:S(2)}) %collective-permute-start.7) | collective-permute-done | bytes 131104 | tf_op jit(solution)/shard_map/ppermute | solution.py:431
  59.8 1.3 %collective-permute-start.8 = (bf16[2,2,128,128]{3,2,1,0:T(8,128)(2,1)S(1)}, bf16[2,2,128,128]{3,2,1,0:T(8,128)(2,1)S(1)}, u32[]{:S(2)}, u32[]{:S(2)}) collective-permute-start(bf16[2,2,128,128]{3,2,1,0:T(8,128)(2,1)S(1)} %collective-permute-done.7.refs_2_), channel_id=1, source_target_pairs={{0,1},{1,0},{2,3},{3,2},{4,5},{5,4},{6,7},{7,6},{8,9},{9,8},{10,11... | collective-permute-start | bytes 393224 | tf_op jit(solution)/shard_map/ppermute | solution.py:431
  61.2 0.0 collective-permute-done.6.refs_1_
  61.2 3.1 %collective-permute-done.8.refs_3_ = bf16[2,2,128,128]{3,2,1,0:T(8,128)(2,1)S(1)} collective-permute-done((bf16[2,2,128,128]{3,2,1,0:T(8,128)(2,1)S(1)}, bf16[2,2,128,128]{3,2,1,0:T(8,128)(2,1)S(1)}, u32[]{:S(2)}, u32[]{:S(2)}) %collective-permute-start.8) | collective-permute-done | bytes 131104 | tf_op jit(solution)/shard_map/ppermute | solution.py:431
  64.3 1.0 %out_part.1 = (f32[128,640]{1,0:T(8,128)S(1)}, bf16[128,640]{1,0:T(8,128)(2,1)S(1)}) custom-call(s32[1]{0:T(128)} %bitcast.1.core.half, s32[1]{0:T(128)} %bitcast.2.mine, bf16[2,2,128,128]{3,2,1,0:T(8,128)(2,1)S(1)} %attend_part.1.refs_0_, bf16[2,2,128,128]{3,2,1,0:T(8,128)(2,1)S(1)} %collective-permute-done.6.refs_1_, ...), custom_call_target="tpu_custom_call" | custom-call | tf_op jit(solution)/shard_map/out_part/pallas_call | solution.py:384
  65.2 4.0 %collective-permute-start.9 = (bf16[128,640]{1,0:T(8,128)(2,1)S(1)}, bf16[128,640]{1,0:T(8,128)(2,1)S(1)}, u32[]{:S(2)}, u32[]{:S(2)}) collective-permute-start(bf16[128,640]{1,0:T(8,128)(2,1)S(1)} %get-tuple-element.59), channel_id=1, source_target_pairs={{0,8},{8,0},{16,24},{24,16},{1,9},{9,1},{17,25},{25,17},{2,10},{10... | collective-permute-start | bytes 491528 | tf_op jit(solution)/shard_map/ppermute | solution.py:431
  69.3 1.0 %collective-permute-done.9 = bf16[128,640]{1,0:T(8,128)(2,1)S(1)} collective-permute-done((bf16[128,640]{1,0:T(8,128)(2,1)S(1)}, bf16[128,640]{1,0:T(8,128)(2,1)S(1)}, u32[]{:S(2)}, u32[]{:S(2)}) %collective-permute-start.9) | collective-permute-done | bytes 163872 | tf_op jit(solution)/shard_map/ppermute | solution.py:431
  70.3 1.7 %collective-permute-start.12 = (bf16[128,640]{1,0:T(8,128)(2,1)S(1)}, bf16[128,640]{1,0:T(8,128)(2,1)S(1)}, u32[]{:S(2)}, u32[]{:S(2)}) collective-permute-start(bf16[128,640]{1,0:T(8,128)(2,1)S(1)} %add_convert_fusion), channel_id=1, source_target_pairs={{0,20},{4,16},{8,28},{12,24},{16,4},{20,0},{24,12},{28,8},{1,21},{... | collective-permute-start | bytes 491528 | tf_op jit(solution)/shard_map/ppermute | solution.py:509
  72.1 0.2 collective-permute-start.11
  72.3 0.8 collective-permute-start.10
  73.1 3.7 %collective-permute-done.12 = bf16[128,640]{1,0:T(8,128)(2,1)S(1)} collective-permute-done((bf16[128,640]{1,0:T(8,128)(2,1)S(1)}, bf16[128,640]{1,0:T(8,128)(2,1)S(1)}, u32[]{:S(2)}, u32[]{:S(2)}) %collective-permute-start.12) | collective-permute-done | bytes 163872 | tf_op jit(solution)/shard_map/ppermute | solution.py:509
  76.8 4.2 %collective-permute-done.11 = bf16[128,640]{1,0:T(8,128)(2,1)S(1)} collective-permute-done((bf16[128,640]{1,0:T(8,128)(2,1)S(1)}, bf16[128,640]{1,0:T(8,128)(2,1)S(1)}, u32[]{:S(2)}, u32[]{:S(2)}) %collective-permute-start.11) | collective-permute-done | bytes 163872 | tf_op jit(solution)/shard_map/ppermute | solution.py:431
  80.9 0.0 collective-permute-done.10
  80.9 0.1 multiply_convert_fusion.rows
  81.1 0.6 collective-permute-start.13
  81.6 0.0 copy-done.5
  81.6 0.3 copy.18
  81.9 2.3 %grad_part.2.refs_0_ = bf16[2048,1280]{1,0:T(8,128)(2,1)} custom-call(s32[1]{0:T(128)} %bitcast.1.core.half, bf16[2048,128]{1,0:T(8,128)(2,1)S(1)} %bitcast.16, bf16[128,640]{1,0:T(8,128)(2,1)S(1)} %multiply_convert_fusion.rows), custom_call_target="tpu_custom_call" | custom-call | tf_op jit(solution)/shard_map/grad_part/pallas_call | solution.py:420
  84.2 0.0 collective-permute-done.13.rows
  84.2 2.3 %grad_part.3 = bf16[2048,1280]{1,0:T(8,128)(2,1)} custom-call(s32[1]{0:T(128)} %bitcast.9.half, bf16[2048,128]{1,0:T(8,128)(2,1)S(1)} %bitcast.17, bf16[128,640]{1,0:T(8,128)(2,1)S(1)} %collective-permute-done.13.rows, bf16[2048,1280]{1,0:T(8,128)(2,1)} %grad_part.2.refs_0_), custom_call_target="tpu_custom_call", output_to_operand_aliasing={{}: (3, {})} | custom-call | tf_op jit(solution)/shard_map/grad_part/pallas_call | solution.py:420
  86.5 0.0 copy-done.1
  (8 shorter events, 0.2 us)
Async XLA Ops:
  0.6 4.1 %copy-start = (bf16[256,1280]{1,0:T(8,128)(2,1)S(1)}, bf16[256,1280]{1,0:T(8,128)(2,1)}, u32[]{:S(2)}) copy-start(bf16[256,1280]{1,0:T(8,128)(2,1)} %param.17) | copy-start | bytes 1966084
  0.6 7.6 %copy-start.2 = (bf16[256,3,1280]{2,0,1:T(8,128)(2,1)S(1)}, bf16[256,3,1280]{2,0,1:T(8,128)(2,1)}, u32[]{:S(2)}) copy-start(bf16[256,3,1280]{2,0,1:T(8,128)(2,1)} %param.22) | copy-start | bytes 5898244
  1.6 6.6 %copy-start.3 = (bf16[256,3,1280]{2,0,1:T(8,128)(2,1)S(1)}, bf16[256,3,1280]{2,0,1:T(8,128)(2,1)}, u32[]{:S(2)}) copy-start(bf16[256,3,1280]{2,0,1:T(8,128)(2,1)} %param.26) | copy-start | bytes 5898244
  6.1 7.6 %collective-permute-start = (bf16[192,640]{1,0:T(8,128)(2,1)S(1)}, bf16[192,640]{1,0:T(8,128)(2,1)S(1)}, u32[]{:S(2)}, u32[]{:S(2)}) collective-permute-start(bf16[192,640]{1,0:T(8,128)(2,1)S(1)} %get-tuple-element.37), channel_id=1, source_target_pairs={{0,4},{4,0},{1,5},{5,1},{2,6},{6,2},{3,7},{7,3},{8,12},{12,8},{9,1... | collective-permute-start | bytes 737288 | tf_op jit(solution)/shard_map/ppermute | solution.py:431
  8.2 7.0 %copy-start.8 = (s32[3]{0:T(128)S(1)}, s32[3]{0:T(128)}, u32[]{:S(2)}) copy-start(s32[3]{0:T(128)} %param.19) | copy-start | bytes 40
  8.2 8.2 %copy-start.4 = (bf16[64,1280]{1,0:T(8,128)(2,1)S(1)}, bf16[64,1280]{1,0:T(8,128)(2,1)}, u32[]{:S(2)}) copy-start(bf16[64,1280]{1,0:T(8,128)(2,1)} %noise.1) | copy-start | bytes 491524
  11.8 12.5 %copy-start.6 = (f32[2,2048]{1,0:T(2,128)S(1)}, f32[2,2048]{1,0:T(2,128)}, u32[]{:S(2)}) copy-start(f32[2,2048]{1,0:T(2,128)} %param.23) | copy-start | bytes 49156
  11.8 12.5 %copy-start.7 = (f32[2,2048]{1,0:T(2,128)S(1)}, f32[2,2048]{1,0:T(2,128)}, u32[]{:S(2)}) copy-start(f32[2,2048]{1,0:T(2,128)} %param.27) | copy-start | bytes 49156
  13.8 2.6 %collective-permute-start.1 = (bf16[192,640]{1,0:T(8,128)(2,1)S(1)}, bf16[192,640]{1,0:T(8,128)(2,1)S(1)}, u32[]{:S(2)}, u32[]{:S(2)}) collective-permute-start(bf16[192,640]{1,0:T(8,128)(2,1)S(1)} %join_part.1.joined), channel_id=1, source_target_pairs={{0,8},{8,0},{16,24},{24,16},{1,9},{9,1},{17,25},{25,17},{2,10},{10... | collective-permute-start | bytes 737288 | tf_op jit(solution)/shard_map/ppermute | solution.py:431
  20.4 20.6 %collective-permute-start.2 = (bf16[528,384]{1,0:T(8,128)(2,1)S(1)}, bf16[528,384]{1,0:T(8,128)(2,1)S(1)}, u32[]{:S(2)}, u32[]{:S(2)}) collective-permute-start(bf16[528,384]{1,0:T(8,128)(2,1)S(1)} %get-tuple-element.49), channel_id=1, source_target_pairs={{0,2},{1,3},{2,0},{3,1},{4,6},{5,7},{6,4},{7,5},{8,10},{9,11},{10,... | collective-permute-start | bytes 1216520 | tf_op jit(solution)/shard_map/ppermute | solution.py:431
  22.9 18.1 %collective-permute-start.3 = (bf16[528,384]{1,0:T(8,128)(2,1)S(1)}, bf16[528,384]{1,0:T(8,128)(2,1)S(1)}, u32[]{:S(2)}, u32[]{:S(2)}) collective-permute-start(bf16[528,384]{1,0:T(8,128)(2,1)S(1)} %get-tuple-element.50), channel_id=1, source_target_pairs={{0,1},{1,0},{2,3},{3,2},{4,5},{5,4},{6,7},{7,6},{8,9},{9,8},{10,11... | collective-permute-start | bytes 1216520 | tf_op jit(solution)/shard_map/ppermute | solution.py:431
  41.0 40.6 %copy-start.5 = (bf16[128,2048]{1,0:T(8,128)(2,1)S(1)}, bf16[128,2048]{1,0:T(8,128)(2,1)}, u32[]{:S(2)}) copy-start(bf16[128,2048]{1,0:T(8,128)(2,1)} %param.14) | copy-start | bytes 1572868
  41.2 11.1 %collective-permute-start.4 = (bf16[272,384]{1,0:T(8,128)(2,1)S(1)}, bf16[272,384]{1,0:T(8,128)(2,1)S(1)}, u32[]{:S(2)}, u32[]{:S(2)}) collective-permute-start(bf16[272,384]{1,0:T(8,128)(2,1)S(1)} %slice.26), channel_id=1, source_target_pairs={{0,2},{1,3},{2,0},{3,1},{4,6},{5,7},{6,4},{7,5},{8,10},{9,11},{10,... | collective-permute-start | bytes 626696 | tf_op jit(solution)/shard_map/ppermute | solution.py:431
  42.5 9.8 %collective-permute-start.5 = (bf16[272,384]{1,0:T(8,128)(2,1)S(1)}, bf16[272,384]{1,0:T(8,128)(2,1)S(1)}, u32[]{:S(2)}, u32[]{:S(2)}) collective-permute-start(bf16[272,384]{1,0:T(8,128)(2,1)S(1)} %slice.25), channel_id=1, source_target_pairs={{0,1},{1,0},{2,3},{3,2},{4,5},{5,4},{6,7},{7,6},{8,9},{9,8},{10,11... | collective-permute-start | bytes 626696 | tf_op jit(solution)/shard_map/ppermute | solution.py:431
  53.5 6.3 %collective-permute-start.7 = (bf16[2,2,128,128]{3,2,1,0:T(8,128)(2,1)S(1)}, bf16[2,2,128,128]{3,2,1,0:T(8,128)(2,1)S(1)}, u32[]{:S(2)}, u32[]{:S(2)}) collective-permute-start(bf16[2,2,128,128]{3,2,1,0:T(8,128)(2,1)S(1)} %attend_part.1.refs_0_), channel_id=1, source_target_pairs={{0,2},{1,3},{2,0},{3,1},{4,6},{5,7},{6,4},{7,5},{8,10},{9,11},{10,... | collective-permute-start | bytes 393224 | tf_op jit(solution)/shard_map/ppermute | solution.py:431
  55.6 5.6 %collective-permute-start.6 = (bf16[2,2,128,128]{3,2,1,0:T(8,128)(2,1)S(1)}, bf16[2,2,128,128]{3,2,1,0:T(8,128)(2,1)S(1)}, u32[]{:S(2)}, u32[]{:S(2)}) collective-permute-start(bf16[2,2,128,128]{3,2,1,0:T(8,128)(2,1)S(1)} %attend_part.1.refs_0_), channel_id=1, source_target_pairs={{0,1},{1,0},{2,3},{3,2},{4,5},{5,4},{6,7},{7,6},{8,9},{9,8},{10,11... | collective-permute-start | bytes 393224 | tf_op jit(solution)/shard_map/ppermute | solution.py:431
  59.8 4.4 %collective-permute-start.8 = (bf16[2,2,128,128]{3,2,1,0:T(8,128)(2,1)S(1)}, bf16[2,2,128,128]{3,2,1,0:T(8,128)(2,1)S(1)}, u32[]{:S(2)}, u32[]{:S(2)}) collective-permute-start(bf16[2,2,128,128]{3,2,1,0:T(8,128)(2,1)S(1)} %collective-permute-done.7.refs_2_), channel_id=1, source_target_pairs={{0,1},{1,0},{2,3},{3,2},{4,5},{5,4},{6,7},{7,6},{8,9},{9,8},{10,11... | collective-permute-start | bytes 393224 | tf_op jit(solution)/shard_map/ppermute | solution.py:431
  65.2 5.1 %collective-permute-start.9 = (bf16[128,640]{1,0:T(8,128)(2,1)S(1)}, bf16[128,640]{1,0:T(8,128)(2,1)S(1)}, u32[]{:S(2)}, u32[]{:S(2)}) collective-permute-start(bf16[128,640]{1,0:T(8,128)(2,1)S(1)} %get-tuple-element.59), channel_id=1, source_target_pairs={{0,8},{8,0},{16,24},{24,16},{1,9},{9,1},{17,25},{25,17},{2,10},{10... | collective-permute-start | bytes 491528 | tf_op jit(solution)/shard_map/ppermute | solution.py:431
  70.3 6.4 %collective-permute-start.12 = (bf16[128,640]{1,0:T(8,128)(2,1)S(1)}, bf16[128,640]{1,0:T(8,128)(2,1)S(1)}, u32[]{:S(2)}, u32[]{:S(2)}) collective-permute-start(bf16[128,640]{1,0:T(8,128)(2,1)S(1)} %add_convert_fusion), channel_id=1, source_target_pairs={{0,20},{4,16},{8,28},{12,24},{16,4},{20,0},{24,12},{28,8},{1,21},{... | collective-permute-start | bytes 491528 | tf_op jit(solution)/shard_map/ppermute | solution.py:509
  72.1 8.8 %collective-permute-start.11 = (bf16[128,640]{1,0:T(8,128)(2,1)S(1)}, bf16[128,640]{1,0:T(8,128)(2,1)S(1)}, u32[]{:S(2)}, u32[]{:S(2)}) collective-permute-start(bf16[128,640]{1,0:T(8,128)(2,1)S(1)} %add_convert_fusion), channel_id=1, source_target_pairs={{0,16},{8,24},{16,0},{24,8},{1,17},{9,25},{17,1},{25,9},{2,18},{10... | collective-permute-start | bytes 491528 | tf_op jit(solution)/shard_map/ppermute | solution.py:431
  72.3 8.7 %collective-permute-start.10 = (bf16[128,640]{1,0:T(8,128)(2,1)S(1)}, bf16[128,640]{1,0:T(8,128)(2,1)S(1)}, u32[]{:S(2)}, u32[]{:S(2)}) collective-permute-start(bf16[128,640]{1,0:T(8,128)(2,1)S(1)} %add_convert_fusion), channel_id=1, source_target_pairs={{0,4},{4,0},{1,5},{5,1},{2,6},{6,2},{3,7},{7,3},{8,12},{12,8},{9,1... | collective-permute-start | bytes 491528 | tf_op jit(solution)/shard_map/ppermute | solution.py:431
  81.1 3.2 %collective-permute-start.13 = (bf16[128,640]{1,0:T(8,128)(2,1)S(1)}, bf16[128,640]{1,0:T(8,128)(2,1)S(1)}, u32[]{:S(2)}, u32[]{:S(2)}) collective-permute-start(bf16[128,640]{1,0:T(8,128)(2,1)S(1)} %multiply_convert_fusion.rows), channel_id=1, source_target_pairs={{0,8},{8,0},{16,24},{24,16},{1,9},{9,1},{17,25},{25,17},{2,10},{10... | collective-permute-start | bytes 491528 | tf_op jit(solution)/shard_map/ppermute | solution.py:431
  84.2 2.3 %copy-start.1 = (bf16[256,1280]{1,0:T(8,128)(2,1)S(1)}, bf16[256,1280]{1,0:T(8,128)(2,1)}, u32[]{:S(2)}) copy-start(bf16[256,1280]{1,0:T(8,128)(2,1)} %param.17) | copy-start | bytes 1966084

commit v7 on v5

--- a/solution.py
+++ b/solution.py
@@ -514,7 +514,7 @@
     heads_t = gen_heads.T
     theirs = exchange(rows, "role", 1)
     weight_grad = grad_part(core, heads_t, rows, None, 2)
-    weight_grad = grad_part(other_core, heads_t, theirs, weight_grad, 2)
+    weight_grad = grad_part(other_core, heads_t, theirs, weight_grad, 4)
     return latent, weight_grad
 
 

time: 86.2 us -> 86.8 us (level)
  no operation moved by 1% of the time
where the time goes in v7:
time: 86.8 us; the launch traced here: 86.6 us
  waiting for transfers between devices  38.6 us (44%)
  starting transfers between devices  24.1 us (28%)
  Pallas kernels  14.6 us (17%)
  local copies, waits for them, and re-layouts  3.75 us (4%)
  matrix products  3.34 us (4%)
  other arithmetic  1.39 us (2%)
    ppermute x13, waiting for transfers between devices, exchange(): lax.ppermute(array, axis, [(i, i ^ bit) for i in range(lax.axis_size(axis...  34.9 us
    ppermute x13, starting transfers between devices, exchange(): lax.ppermute(array, axis, [(i, i ^ bit) for i in range(lax.axis_size(axis...  22.3 us
    pallas_call x2, Pallas kernels, grad_part(): pl.pallas_call(grad_kernel, grid_spec=grid_spec, out_shape=jax.ShapeDtype...  4.68 us
    pallas_call x1, Pallas kernels, qkv_part(): pl.pallas_call(qkv_kernel, in_specs=[smem_spec()] * 4 + [vmem_spec()] * 6...  3.99 us
    ppermute x1, waiting for transfers between devices, heads_per_role(): lax.ppermute(total, ('role', 'seq'), [(i, i ^ 2 * lax.axis_size('seq') +...  3.7 us
    pallas_call x1, Pallas kernels, load_part(): pl.pallas_call(load_kernel, in_specs=[smem_spec()] + [vmem_spec()] * 3 +...  3.51 us
    dynamic_slice x2, local copies, waits for them, and re-layouts, take(): lax.dynamic_slice_in_dim(array, begin, size, axis=axis, allow_negative_in...  3.37 us
    dot_general x2, matrix products, dot32(): return jnp.dot(a, b, preferred_element_type=jnp.float32)  3.34 us
  transfers between devices with their start and end apart: 14, of which 9 were waited for; matrix products, arithmetic and copies ran while one was open for 3% of the time, Pallas kernels for 6%

profile of v7, /device:TPU:1, one launch (start us, length us, event | category | flops | bytes accessed | tf_op | source)
XLA Modules:
  0.0 86.6 jit_solution(9908536965982775237)
XLA Ops:
  0.6 0.0 copy-start
  0.6 0.0 copy-start.2
  0.7 0.8 convert_element_type.42
  1.5 0.1 fusion.11
  1.6 0.0 copy-start.3
  1.6 3.1 %fusion.2.product = f32[128,640]{1,0:T(8,128)S(1)} fusion(bf16[128,2048]{1,0:T(8,128)(2,1)} %param.14, bf16[2048,1280]{1,0:T(8,128)(2,1)} %param.16, s32[]{:T(128)S(6)} %mul.47), kind=kOutput, calls=%fused_computation.2 | convolution fusion | flops 335544320 | bytes 3473412 | tf_op jit(solution)/shard_map/dot_general | solution.py:144
  4.7 0.0 copy-done
  4.7 0.3 fusion.5.gate
  5.0 1.0 %constant_dynamic-slice_fusion.2 = (bf16[64,640]{1,0:T(8,128)(2,1)S(1)}, bf16[64,640]{1,0:T(8,128)(2,1)S(1)}) fusion(bf16[64,1280]{1,0:T(8,128)(2,1)} %noise.1, s32[]{:T(128)S(6)} %mul.47, bf16[64,1280]{1,0:T(8,128)(2,1)} %param.15), kind=kLoop, calls=%fused_computation.25 | loop fusion | bytes 327684 | tf_op jit(solution)/shard_map/dynamic_slice | solution.py:435
  6.0 0.1 pack_part.1
  6.1 2.1 %collective-permute-start = (bf16[192,640]{1,0:T(8,128)(2,1)S(1)}, bf16[192,640]{1,0:T(8,128)(2,1)S(1)}, u32[]{:S(2)}, u32[]{:S(2)}) collective-permute-start(bf16[192,640]{1,0:T(8,128)(2,1)S(1)} %get-tuple-element.37), channel_id=1, source_target_pairs={{0,4},{4,0},{1,5},{5,1},{2,6},{6,2},{3,7},{7,3},{8,12},{12,8},{9,1... | collective-permute-start | bytes 737288 | tf_op jit(solution)/shard_map/ppermute | solution.py:431
  8.2 0.0 copy-done.2
  8.2 0.0 copy-done.3
  8.2 0.0 copy-start.8
  8.2 0.0 copy-start.4
  8.2 3.5 %load_part.1 = (bf16[3,1280,512]{2,1,0:T(8,128)(2,1)S(1)}, bf16[3,1280,512]{2,1,0:T(8,128)(2,1)S(1)}, f32[2,3,8,1280]{3,2,1,0:T(8,128)S(1)}) custom-call(s32[1]{0:T(128)} %bitcast.4.start, bf16[8,256]{1,0:T(8,128)(2,1)S(1)} %fusion.9.embed, bf16[3,256,1280]{2,1,0:T(8,128)(2,1)S(1)} %bitcast.18, bf16[3,256,1280]{2,1,0:T(8,128)(2,1)S(1)} %bitcast.19, ...), custom_call_target="tpu_custom_call" | custom-call | tf_op jit(solution)/shard_map/load_part/pallas_call | solution.py:209
  11.8 0.0 copy-start.6
  11.8 0.0 copy-start.7
  11.8 1.9 %collective-permute-done.arrived = bf16[192,640]{1,0:T(8,128)(2,1)S(1)} collective-permute-done((bf16[192,640]{1,0:T(8,128)(2,1)S(1)}, bf16[192,640]{1,0:T(8,128)(2,1)S(1)}, u32[]{:S(2)}, u32[]{:S(2)}) %collective-permute-start) | collective-permute-done | bytes 245792 | tf_op jit(solution)/shard_map/ppermute | solution.py:431
  13.8 1.5 %collective-permute-start.1 = (bf16[192,640]{1,0:T(8,128)(2,1)S(1)}, bf16[192,640]{1,0:T(8,128)(2,1)S(1)}, u32[]{:S(2)}, u32[]{:S(2)}) collective-permute-start(bf16[192,640]{1,0:T(8,128)(2,1)S(1)} %join_part.1.joined), channel_id=1, source_target_pairs={{0,8},{8,0},{16,24},{24,16},{1,9},{9,1},{17,25},{25,17},{2,10},{10... | collective-permute-start | bytes 737288 | tf_op jit(solution)/shard_map/ppermute | solution.py:431
  15.2 0.0 copy-done.8
  15.3 0.1 convert_multiply_fusion.levels
  15.3 1.1 %collective-permute-done.1.swapped = bf16[192,640]{1,0:T(8,128)(2,1)S(1)} collective-permute-done((bf16[192,640]{1,0:T(8,128)(2,1)S(1)}, bf16[192,640]{1,0:T(8,128)(2,1)S(1)}, u32[]{:S(2)}, u32[]{:S(2)}) %collective-permute-start.1) | collective-permute-done | bytes 245792 | tf_op jit(solution)/shard_map/ppermute | solution.py:431
  16.4 0.0 copy-done.4
  16.4 4.0 %qkv_part.1 = (bf16[64,1280]{1,0:T(8,128)(2,1)}, bf16[528,384]{1,0:T(8,128)(2,1)S(1)}, bf16[528,384]{1,0:T(8,128)(2,1)S(1)}, bf16[528,384]{1,0:T(8,128)(2,1)S(1)}, bf16[528,384]{1,0:T(8,128)(2,1)S(1)}) custom-call(s32[1]{0:T(128)} %bitcast.seq, s32[1]{0:T(128)} %bitcast.1.core.half, s32[1]{0:T(128)} %bitcast.2.mine, f32[2]{0:T(128)S(1)} %convert_multiply_fusion.levels, ...), custom_call_target="tpu_custom_call" | custom-call | tf_op jit(solution)/shard_map/qkv_part/pallas_call | solution.py:300
  20.4 2.6 %collective-permute-start.2 = (bf16[528,384]{1,0:T(8,128)(2,1)S(1)}, bf16[528,384]{1,0:T(8,128)(2,1)S(1)}, u32[]{:S(2)}, u32[]{:S(2)}) collective-permute-start(bf16[528,384]{1,0:T(8,128)(2,1)S(1)} %get-tuple-element.49), channel_id=1, source_target_pairs={{0,2},{1,3},{2,0},{3,1},{4,6},{5,7},{6,4},{7,5},{8,10},{9,11},{10,... | collective-permute-start | bytes 1216520 | tf_op jit(solution)/shard_map/ppermute | solution.py:431
  22.9 1.3 %collective-permute-start.3 = (bf16[528,384]{1,0:T(8,128)(2,1)S(1)}, bf16[528,384]{1,0:T(8,128)(2,1)S(1)}, u32[]{:S(2)}, u32[]{:S(2)}) collective-permute-start(bf16[528,384]{1,0:T(8,128)(2,1)S(1)} %get-tuple-element.50), channel_id=1, source_target_pairs={{0,1},{1,0},{2,3},{3,2},{4,5},{5,4},{6,7},{7,6},{8,9},{9,8},{10,11... | collective-permute-start | bytes 1216520 | tf_op jit(solution)/shard_map/ppermute | solution.py:431
  24.3 0.0 copy-done.6
  24.3 0.0 copy-done.7
  24.3 0.1 fusion.10.refs_4_
  24.3 2.3 %constant_dynamic-slice_fusion = (bf16[512,1280]{1,0:T(8,128)(2,1)S(1)}, bf16[512,1280]{1,0:T(8,128)(2,1)S(1)}) fusion(bf16[2048,1280]{1,0:T(8,128)(2,1)} %param.25, s32[]{:T(128)} %mul.48, bf16[2048,1280]{1,0:T(8,128)(2,1)} %param.21), kind=kLoop, calls=%fused_computation.23 | loop fusion | bytes 5242884 | tf_op jit(solution)/shard_map/dynamic_slice | solution.py:435
  26.7 14.4 %collective-permute-done.2 = bf16[528,384]{1,0:T(8,128)(2,1)S(1)} collective-permute-done((bf16[528,384]{1,0:T(8,128)(2,1)S(1)}, bf16[528,384]{1,0:T(8,128)(2,1)S(1)}, u32[]{:S(2)}, u32[]{:S(2)}) %collective-permute-start.2) | collective-permute-done | bytes 405536 | tf_op jit(solution)/shard_map/ppermute | solution.py:431
  41.0 0.0 collective-permute-done.3
  41.0 0.0 copy-start.5
  41.0 0.1 convert_add_fusion.1.refs_0_
  41.2 1.2 %collective-permute-start.4 = (bf16[272,384]{1,0:T(8,128)(2,1)S(1)}, bf16[272,384]{1,0:T(8,128)(2,1)S(1)}, u32[]{:S(2)}, u32[]{:S(2)}) collective-permute-start(bf16[272,384]{1,0:T(8,128)(2,1)S(1)} %slice.26), channel_id=1, source_target_pairs={{0,2},{1,3},{2,0},{3,1},{4,6},{5,7},{6,4},{7,5},{8,10},{9,11},{10,... | collective-permute-start | bytes 626696 | tf_op jit(solution)/shard_map/ppermute | solution.py:431
  42.4 0.1 convert_add_fusion.refs_2_
  42.5 2.9 %collective-permute-start.5 = (bf16[272,384]{1,0:T(8,128)(2,1)S(1)}, bf16[272,384]{1,0:T(8,128)(2,1)S(1)}, u32[]{:S(2)}, u32[]{:S(2)}) collective-permute-start(bf16[272,384]{1,0:T(8,128)(2,1)S(1)} %slice.25), channel_id=1, source_target_pairs={{0,1},{1,0},{2,3},{3,2},{4,5},{5,4},{6,7},{7,6},{8,9},{9,8},{10,11... | collective-permute-start | bytes 626696 | tf_op jit(solution)/shard_map/ppermute | solution.py:431
  45.4 6.8 %collective-permute-done.4.refs_1_ = bf16[272,384]{1,0:T(8,128)(2,1)S(1)} collective-permute-done((bf16[272,384]{1,0:T(8,128)(2,1)S(1)}, bf16[272,384]{1,0:T(8,128)(2,1)S(1)}, u32[]{:S(2)}, u32[]{:S(2)}) %collective-permute-start.4) | collective-permute-done | bytes 208928 | tf_op jit(solution)/shard_map/ppermute | solution.py:431
  52.3 0.0 collective-permute-done.5.refs_3_
  52.3 1.3 %attend_part.1.refs_0_ = bf16[2,2,128,128]{3,2,1,0:T(8,128)(2,1)S(1)} custom-call(f32[528,384]{1,0:T(8,128)S(1)} %convert_add_fusion.1.refs_0_, bf16[272,384]{1,0:T(8,128)(2,1)S(1)} %collective-permute-done.4.refs_1_, f32[528,384]{1,0:T(8,128)S(1)} %convert_add_fusion.refs_2_, bf16[272,384]{1,0:T(8,128)(2,1)S(1)} %collective-permute-done.5.refs_3_, ...), custom_call_target="tpu_custom_call" | custom-call | tf_op jit(solution)/shard_map/attend_part/pallas_call | solution.py:350
  53.5 2.0 %collective-permute-start.7 = (bf16[2,2,128,128]{3,2,1,0:T(8,128)(2,1)S(1)}, bf16[2,2,128,128]{3,2,1,0:T(8,128)(2,1)S(1)}, u32[]{:S(2)}, u32[]{:S(2)}) collective-permute-start(bf16[2,2,128,128]{3,2,1,0:T(8,128)(2,1)S(1)} %attend_part.1.refs_0_), channel_id=1, source_target_pairs={{0,2},{1,3},{2,0},{3,1},{4,6},{5,7},{6,4},{7,5},{8,10},{9,11},{10,... | collective-permute-start | bytes 393224 | tf_op jit(solution)/shard_map/ppermute | solution.py:431
  55.6 1.8 %collective-permute-start.6 = (bf16[2,2,128,128]{3,2,1,0:T(8,128)(2,1)S(1)}, bf16[2,2,128,128]{3,2,1,0:T(8,128)(2,1)S(1)}, u32[]{:S(2)}, u32[]{:S(2)}) collective-permute-start(bf16[2,2,128,128]{3,2,1,0:T(8,128)(2,1)S(1)} %attend_part.1.refs_0_), channel_id=1, source_target_pairs={{0,1},{1,0},{2,3},{3,2},{4,5},{5,4},{6,7},{7,6},{8,9},{9,8},{10,11... | collective-permute-start | bytes 393224 | tf_op jit(solution)/shard_map/ppermute | solution.py:431
  57.4 2.4 %collective-permute-done.7.refs_2_ = bf16[2,2,128,128]{3,2,1,0:T(8,128)(2,1)S(1)} collective-permute-done((bf16[2,2,128,128]{3,2,1,0:T(8,128)(2,1)S(1)}, bf16[2,2,128,128]{3,2,1,0:T(8,128)(2,1)S(1)}, u32[]{:S(2)}, u32[]{:S(2)}) %collective-permute-start.7) | collective-permute-done | bytes 131104 | tf_op jit(solution)/shard_map/ppermute | solution.py:431
  59.8 1.3 %collective-permute-start.8 = (bf16[2,2,128,128]{3,2,1,0:T(8,128)(2,1)S(1)}, bf16[2,2,128,128]{3,2,1,0:T(8,128)(2,1)S(1)}, u32[]{:S(2)}, u32[]{:S(2)}) collective-permute-start(bf16[2,2,128,128]{3,2,1,0:T(8,128)(2,1)S(1)} %collective-permute-done.7.refs_2_), channel_id=1, source_target_pairs={{0,1},{1,0},{2,3},{3,2},{4,5},{5,4},{6,7},{7,6},{8,9},{9,8},{10,11... | collective-permute-start | bytes 393224 | tf_op jit(solution)/shard_map/ppermute | solution.py:431
  61.2 0.0 collective-permute-done.6.refs_1_
  61.2 3.1 %collective-permute-done.8.refs_3_ = bf16[2,2,128,128]{3,2,1,0:T(8,128)(2,1)S(1)} collective-permute-done((bf16[2,2,128,128]{3,2,1,0:T(8,128)(2,1)S(1)}, bf16[2,2,128,128]{3,2,1,0:T(8,128)(2,1)S(1)}, u32[]{:S(2)}, u32[]{:S(2)}) %collective-permute-start.8) | collective-permute-done | bytes 131104 | tf_op jit(solution)/shard_map/ppermute | solution.py:431
  64.3 1.0 %out_part.1 = (f32[128,640]{1,0:T(8,128)S(1)}, bf16[128,640]{1,0:T(8,128)(2,1)S(1)}) custom-call(s32[1]{0:T(128)} %bitcast.1.core.half, s32[1]{0:T(128)} %bitcast.2.mine, bf16[2,2,128,128]{3,2,1,0:T(8,128)(2,1)S(1)} %attend_part.1.refs_0_, bf16[2,2,128,128]{3,2,1,0:T(8,128)(2,1)S(1)} %collective-permute-done.6.refs_1_, ...), custom_call_target="tpu_custom_call" | custom-call | tf_op jit(solution)/shard_map/out_part/pallas_call | solution.py:384
  65.2 4.0 %collective-permute-start.9 = (bf16[128,640]{1,0:T(8,128)(2,1)S(1)}, bf16[128,640]{1,0:T(8,128)(2,1)S(1)}, u32[]{:S(2)}, u32[]{:S(2)}) collective-permute-start(bf16[128,640]{1,0:T(8,128)(2,1)S(1)} %get-tuple-element.59), channel_id=1, source_target_pairs={{0,8},{8,0},{16,24},{24,16},{1,9},{9,1},{17,25},{25,17},{2,10},{10... | collective-permute-start | bytes 491528 | tf_op jit(solution)/shard_map/ppermute | solution.py:431
  69.3 1.0 %collective-permute-done.9 = bf16[128,640]{1,0:T(8,128)(2,1)S(1)} collective-permute-done((bf16[128,640]{1,0:T(8,128)(2,1)S(1)}, bf16[128,640]{1,0:T(8,128)(2,1)S(1)}, u32[]{:S(2)}, u32[]{:S(2)}) %collective-permute-start.9) | collective-permute-done | bytes 163872 | tf_op jit(solution)/shard_map/ppermute | solution.py:431
  70.3 1.7 %collective-permute-start.12 = (bf16[128,640]{1,0:T(8,128)(2,1)S(1)}, bf16[128,640]{1,0:T(8,128)(2,1)S(1)}, u32[]{:S(2)}, u32[]{:S(2)}) collective-permute-start(bf16[128,640]{1,0:T(8,128)(2,1)S(1)} %add_convert_fusion), channel_id=1, source_target_pairs={{0,20},{4,16},{8,28},{12,24},{16,4},{20,0},{24,12},{28,8},{1,21},{... | collective-permute-start | bytes 491528 | tf_op jit(solution)/shard_map/ppermute | solution.py:509
  72.1 0.2 collective-permute-start.11
  72.3 0.8 collective-permute-start.10
  73.1 3.7 %collective-permute-done.12 = bf16[128,640]{1,0:T(8,128)(2,1)S(1)} collective-permute-done((bf16[128,640]{1,0:T(8,128)(2,1)S(1)}, bf16[128,640]{1,0:T(8,128)(2,1)S(1)}, u32[]{:S(2)}, u32[]{:S(2)}) %collective-permute-start.12) | collective-permute-done | bytes 163872 | tf_op jit(solution)/shard_map/ppermute | solution.py:509
  76.8 4.2 %collective-permute-done.11 = bf16[128,640]{1,0:T(8,128)(2,1)S(1)} collective-permute-done((bf16[128,640]{1,0:T(8,128)(2,1)S(1)}, bf16[128,640]{1,0:T(8,128)(2,1)S(1)}, u32[]{:S(2)}, u32[]{:S(2)}) %collective-permute-start.11) | collective-permute-done | bytes 163872 | tf_op jit(solution)/shard_map/ppermute | solution.py:431
  80.9 0.0 collective-permute-done.10
  80.9 0.1 multiply_convert_fusion.rows
  81.1 0.6 collective-permute-start.13
  81.6 0.0 copy-done.5
  81.6 0.3 copy.18
  81.9 2.1 %grad_part.2.refs_0_ = bf16[2048,1280]{1,0:T(8,128)(2,1)} custom-call(s32[1]{0:T(128)} %bitcast.1.core.half, bf16[2048,128]{1,0:T(8,128)(2,1)S(1)} %bitcast.16, bf16[128,640]{1,0:T(8,128)(2,1)S(1)} %multiply_convert_fusion.rows), custom_call_target="tpu_custom_call" | custom-call | tf_op jit(solution)/shard_map/grad_part/pallas_call | solution.py:420
  83.9 0.0 collective-permute-done.13.rows
  84.0 2.6 %grad_part.3 = bf16[2048,1280]{1,0:T(8,128)(2,1)} custom-call(s32[1]{0:T(128)} %bitcast.9.half, bf16[2048,128]{1,0:T(8,128)(2,1)S(1)} %bitcast.17, bf16[128,640]{1,0:T(8,128)(2,1)S(1)} %collective-permute-done.13.rows, bf16[2048,1280]{1,0:T(8,128)(2,1)} %grad_part.2.refs_0_), custom_call_target="tpu_custom_call", output_to_operand_aliasing={{}: (3, {})} | custom-call | tf_op jit(solution)/shard_map/grad_part/pallas_call | solution.py:420
  86.6 0.0 copy-done.1
  (8 shorter events, 0.2 us)
Async XLA Ops:
  0.6 4.1 %copy-start = (bf16[256,1280]{1,0:T(8,128)(2,1)S(1)}, bf16[256,1280]{1,0:T(8,128)(2,1)}, u32[]{:S(2)}) copy-start(bf16[256,1280]{1,0:T(8,128)(2,1)} %param.17) | copy-start | bytes 1966084
  0.6 7.6 %copy-start.2 = (bf16[256,3,1280]{2,0,1:T(8,128)(2,1)S(1)}, bf16[256,3,1280]{2,0,1:T(8,128)(2,1)}, u32[]{:S(2)}) copy-start(bf16[256,3,1280]{2,0,1:T(8,128)(2,1)} %param.22) | copy-start | bytes 5898244
  1.6 6.6 %copy-start.3 = (bf16[256,3,1280]{2,0,1:T(8,128)(2,1)S(1)}, bf16[256,3,1280]{2,0,1:T(8,128)(2,1)}, u32[]{:S(2)}) copy-start(bf16[256,3,1280]{2,0,1:T(8,128)(2,1)} %param.26) | copy-start | bytes 5898244
  6.1 7.6 %collective-permute-start = (bf16[192,640]{1,0:T(8,128)(2,1)S(1)}, bf16[192,640]{1,0:T(8,128)(2,1)S(1)}, u32[]{:S(2)}, u32[]{:S(2)}) collective-permute-start(bf16[192,640]{1,0:T(8,128)(2,1)S(1)} %get-tuple-element.37), channel_id=1, source_target_pairs={{0,4},{4,0},{1,5},{5,1},{2,6},{6,2},{3,7},{7,3},{8,12},{12,8},{9,1... | collective-permute-start | bytes 737288 | tf_op jit(solution)/shard_map/ppermute | solution.py:431
  8.2 7.0 %copy-start.8 = (s32[3]{0:T(128)S(1)}, s32[3]{0:T(128)}, u32[]{:S(2)}) copy-start(s32[3]{0:T(128)} %param.19) | copy-start | bytes 40
  8.2 8.2 %copy-start.4 = (bf16[64,1280]{1,0:T(8,128)(2,1)S(1)}, bf16[64,1280]{1,0:T(8,128)(2,1)}, u32[]{:S(2)}) copy-start(bf16[64,1280]{1,0:T(8,128)(2,1)} %noise.1) | copy-start | bytes 491524
  11.8 12.5 %copy-start.6 = (f32[2,2048]{1,0:T(2,128)S(1)}, f32[2,2048]{1,0:T(2,128)}, u32[]{:S(2)}) copy-start(f32[2,2048]{1,0:T(2,128)} %param.23) | copy-start | bytes 49156
  11.8 12.5 %copy-start.7 = (f32[2,2048]{1,0:T(2,128)S(1)}, f32[2,2048]{1,0:T(2,128)}, u32[]{:S(2)}) copy-start(f32[2,2048]{1,0:T(2,128)} %param.27) | copy-start | bytes 49156
  13.8 2.6 %collective-permute-start.1 = (bf16[192,640]{1,0:T(8,128)(2,1)S(1)}, bf16[192,640]{1,0:T(8,128)(2,1)S(1)}, u32[]{:S(2)}, u32[]{:S(2)}) collective-permute-start(bf16[192,640]{1,0:T(8,128)(2,1)S(1)} %join_part.1.joined), channel_id=1, source_target_pairs={{0,8},{8,0},{16,24},{24,16},{1,9},{9,1},{17,25},{25,17},{2,10},{10... | collective-permute-start | bytes 737288 | tf_op jit(solution)/shard_map/ppermute | solution.py:431
  20.4 20.6 %collective-permute-start.2 = (bf16[528,384]{1,0:T(8,128)(2,1)S(1)}, bf16[528,384]{1,0:T(8,128)(2,1)S(1)}, u32[]{:S(2)}, u32[]{:S(2)}) collective-permute-start(bf16[528,384]{1,0:T(8,128)(2,1)S(1)} %get-tuple-element.49), channel_id=1, source_target_pairs={{0,2},{1,3},{2,0},{3,1},{4,6},{5,7},{6,4},{7,5},{8,10},{9,11},{10,... | collective-permute-start | bytes 1216520 | tf_op jit(solution)/shard_map/ppermute | solution.py:431
  22.9 18.1 %collective-permute-start.3 = (bf16[528,384]{1,0:T(8,128)(2,1)S(1)}, bf16[528,384]{1,0:T(8,128)(2,1)S(1)}, u32[]{:S(2)}, u32[]{:S(2)}) collective-permute-start(bf16[528,384]{1,0:T(8,128)(2,1)S(1)} %get-tuple-element.50), channel_id=1, source_target_pairs={{0,1},{1,0},{2,3},{3,2},{4,5},{5,4},{6,7},{7,6},{8,9},{9,8},{10,11... | collective-permute-start | bytes 1216520 | tf_op jit(solution)/shard_map/ppermute | solution.py:431
  41.0 40.6 %copy-start.5 = (bf16[128,2048]{1,0:T(8,128)(2,1)S(1)}, bf16[128,2048]{1,0:T(8,128)(2,1)}, u32[]{:S(2)}) copy-start(bf16[128,2048]{1,0:T(8,128)(2,1)} %param.14) | copy-start | bytes 1572868
  41.2 11.1 %collective-permute-start.4 = (bf16[272,384]{1,0:T(8,128)(2,1)S(1)}, bf16[272,384]{1,0:T(8,128)(2,1)S(1)}, u32[]{:S(2)}, u32[]{:S(2)}) collective-permute-start(bf16[272,384]{1,0:T(8,128)(2,1)S(1)} %slice.26), channel_id=1, source_target_pairs={{0,2},{1,3},{2,0},{3,1},{4,6},{5,7},{6,4},{7,5},{8,10},{9,11},{10,... | collective-permute-start | bytes 626696 | tf_op jit(solution)/shard_map/ppermute | solution.py:431
  42.5 9.8 %collective-permute-start.5 = (bf16[272,384]{1,0:T(8,128)(2,1)S(1)}, bf16[272,384]{1,0:T(8,128)(2,1)S(1)}, u32[]{:S(2)}, u32[]{:S(2)}) collective-permute-start(bf16[272,384]{1,0:T(8,128)(2,1)S(1)} %slice.25), channel_id=1, source_target_pairs={{0,1},{1,0},{2,3},{3,2},{4,5},{5,4},{6,7},{7,6},{8,9},{9,8},{10,11... | collective-permute-start | bytes 626696 | tf_op jit(solution)/shard_map/ppermute | solution.py:431
  53.5 6.3 %collective-permute-start.7 = (bf16[2,2,128,128]{3,2,1,0:T(8,128)(2,1)S(1)}, bf16[2,2,128,128]{3,2,1,0:T(8,128)(2,1)S(1)}, u32[]{:S(2)}, u32[]{:S(2)}) collective-permute-start(bf16[2,2,128,128]{3,2,1,0:T(8,128)(2,1)S(1)} %attend_part.1.refs_0_), channel_id=1, source_target_pairs={{0,2},{1,3},{2,0},{3,1},{4,6},{5,7},{6,4},{7,5},{8,10},{9,11},{10,... | collective-permute-start | bytes 393224 | tf_op jit(solution)/shard_map/ppermute | solution.py:431
  55.6 5.6 %collective-permute-start.6 = (bf16[2,2,128,128]{3,2,1,0:T(8,128)(2,1)S(1)}, bf16[2,2,128,128]{3,2,1,0:T(8,128)(2,1)S(1)}, u32[]{:S(2)}, u32[]{:S(2)}) collective-permute-start(bf16[2,2,128,128]{3,2,1,0:T(8,128)(2,1)S(1)} %attend_part.1.refs_0_), channel_id=1, source_target_pairs={{0,1},{1,0},{2,3},{3,2},{4,5},{5,4},{6,7},{7,6},{8,9},{9,8},{10,11... | collective-permute-start | bytes 393224 | tf_op jit(solution)/shard_map/ppermute | solution.py:431
  59.8 4.4 %collective-permute-start.8 = (bf16[2,2,128,128]{3,2,1,0:T(8,128)(2,1)S(1)}, bf16[2,2,128,128]{3,2,1,0:T(8,128)(2,1)S(1)}, u32[]{:S(2)}, u32[]{:S(2)}) collective-permute-start(bf16[2,2,128,128]{3,2,1,0:T(8,128)(2,1)S(1)} %collective-permute-done.7.refs_2_), channel_id=1, source_target_pairs={{0,1},{1,0},{2,3},{3,2},{4,5},{5,4},{6,7},{7,6},{8,9},{9,8},{10,11... | collective-permute-start | bytes 393224 | tf_op jit(solution)/shard_map/ppermute | solution.py:431
  65.2 5.1 %collective-permute-start.9 = (bf16[128,640]{1,0:T(8,128)(2,1)S(1)}, bf16[128,640]{1,0:T(8,128)(2,1)S(1)}, u32[]{:S(2)}, u32[]{:S(2)}) collective-permute-start(bf16[128,640]{1,0:T(8,128)(2,1)S(1)} %get-tuple-element.59), channel_id=1, source_target_pairs={{0,8},{8,0},{16,24},{24,16},{1,9},{9,1},{17,25},{25,17},{2,10},{10... | collective-permute-start | bytes 491528 | tf_op jit(solution)/shard_map/ppermute | solution.py:431
  70.3 6.4 %collective-permute-start.12 = (bf16[128,640]{1,0:T(8,128)(2,1)S(1)}, bf16[128,640]{1,0:T(8,128)(2,1)S(1)}, u32[]{:S(2)}, u32[]{:S(2)}) collective-permute-start(bf16[128,640]{1,0:T(8,128)(2,1)S(1)} %add_convert_fusion), channel_id=1, source_target_pairs={{0,20},{4,16},{8,28},{12,24},{16,4},{20,0},{24,12},{28,8},{1,21},{... | collective-permute-start | bytes 491528 | tf_op jit(solution)/shard_map/ppermute | solution.py:509
  72.1 8.8 %collective-permute-start.11 = (bf16[128,640]{1,0:T(8,128)(2,1)S(1)}, bf16[128,640]{1,0:T(8,128)(2,1)S(1)}, u32[]{:S(2)}, u32[]{:S(2)}) collective-permute-start(bf16[128,640]{1,0:T(8,128)(2,1)S(1)} %add_convert_fusion), channel_id=1, source_target_pairs={{0,16},{8,24},{16,0},{24,8},{1,17},{9,25},{17,1},{25,9},{2,18},{10... | collective-permute-start | bytes 491528 | tf_op jit(solution)/shard_map/ppermute | solution.py:431
  72.3 8.7 %collective-permute-start.10 = (bf16[128,640]{1,0:T(8,128)(2,1)S(1)}, bf16[128,640]{1,0:T(8,128)(2,1)S(1)}, u32[]{:S(2)}, u32[]{:S(2)}) collective-permute-start(bf16[128,640]{1,0:T(8,128)(2,1)S(1)} %add_convert_fusion), channel_id=1, source_target_pairs={{0,4},{4,0},{1,5},{5,1},{2,6},{6,2},{3,7},{7,3},{8,12},{12,8},{9,1... | collective-permute-start | bytes 491528 | tf_op jit(solution)/shard_map/ppermute | solution.py:431
  81.1 2.9 %collective-permute-start.13 = (bf16[128,640]{1,0:T(8,128)(2,1)S(1)}, bf16[128,640]{1,0:T(8,128)(2,1)S(1)}, u32[]{:S(2)}, u32[]{:S(2)}) collective-permute-start(bf16[128,640]{1,0:T(8,128)(2,1)S(1)} %multiply_convert_fusion.rows), channel_id=1, source_target_pairs={{0,8},{8,0},{16,24},{24,16},{1,9},{9,1},{17,25},{25,17},{2,10},{10... | collective-permute-start | bytes 491528 | tf_op jit(solution)/shard_map/ppermute | solution.py:431
  83.9 2.6 %copy-start.1 = (bf16[256,1280]{1,0:T(8,128)(2,1)S(1)}, bf16[256,1280]{1,0:T(8,128)(2,1)}, u32[]{:S(2)}) copy-start(bf16[256,1280]{1,0:T(8,128)(2,1)} %param.17) | copy-start | bytes 1966084
